TPU v7x, 32 devices: a whole 2x2x4 slice. The times are simulated.
32 devices in a mesh: group: 2 (over x), row: 16 (over z, y, core).
Axes of the slice: x: 2, y: 2, z: 4, core: 2. Of those that a mesh axis runs over, the one named last changes fastest.
Arguments:
- specimen: bfloat16 [4, 2, 4096, 2048], P('group', None, 'row'), parts along dimension 0, may hold values from -3 to 3
- probe_field: float32 [4, 256, 256], P('group'), parts along dimension 0, may hold values from -6 to 6
- transfer_phase: float32 [256], replicated, may hold values from -3.140625 to 3.140625
- intensity: bfloat16 [512, 256, 256], P(('group', 'row')), parts along dimension 0, may hold values from 0 to 1
- row_offset: int32 [512], P(('group', 'row')), parts along dimension 0, may hold values from 0 to 255, as said below
- col_offset: int32 [512], P(('group', 'row')), parts along dimension 0, may hold values from 0 to 1792
- counts: int32 [32], P(('group', 'row')), parts along dimension 0, may hold values from 1 to 16, as said below
Outputs:
- specimen_grad: float32 [4, 2, 4096, 2048], P('group', None, 'row'), parts along dimension 0
- probe_grad: float32 [4, 256, 256], P('group'), parts along dimension 0
There are 2 independent parts, one for each index of `group`. A program takes and returns all parts, laid end to end along the dimension named above; an argument that names none is the same for every part. Nothing has to cross between parts.
Inputs may be any that keep to these rules, and one draw needn't show every extreme that they name: `row_offset`: on the last device every row offset is 0; slot 0 of the first device has row offset 256 - 1. The live slots of a device are its first counts entries; some device holds exactly 16.
All inputs are finite; a program needn't handle non-finite values.
Results may differ from a plain program's by a relative error of at most 0.012.
Values may be sent and summed in bfloat16 or wider, within the bound.
No kernel may reach another device: no remote copies, remote signals or barrier semaphores. Data moves between devices by JAX's collectives and lax.ppermute only.
A program may use at most 128 MiB of HBM per device.

v0:
```python
import functools
import math

import jax
import jax.numpy as jnp
import numpy as np
from jax import lax
from jax.experimental import pallas as pl
from jax.experimental.pallas import tpu as pltpu
from jax.sharding import PartitionSpec as P

LANES = 128
BF = jnp.bfloat16
F32 = jnp.float32


def passed_along(value, axis, steps):
    count = lax.axis_size(axis)
    first, last = (max(0, -steps), min(count, count - steps))
    return lax.ppermute(value, axis, [(source, source + steps) for source in range(first, last)])


def fourier(extent):
    indices = np.arange(extent, dtype=np.int64)
    angles = (indices[:, None] * indices[None, :] % extent) * (2.0 * math.pi / extent)
    norming = 1.0 / math.sqrt(extent)
    return (np.cos(angles) * norming).astype(np.float32), (-np.sin(angles) * norming).astype(np.float32)


def block_table(re, im):
    return jnp.concatenate(
        [jnp.concatenate([re, -im], axis=1), jnp.concatenate([im, re], axis=1)], axis=0
    ).astype(BF)


def make_tables(transfer_phase, extent):
    four_re, four_im = (jnp.asarray(item) for item in fourier(extent))
    cos_phase = jnp.cos(transfer_phase)[:, None]
    sin_phase = jnp.sin(transfer_phase)[:, None]
    mid_re = cos_phase * four_re - sin_phase * four_im
    mid_im = cos_phase * four_im + sin_phase * four_re
    highest = lax.Precision.HIGHEST
    prop_re = jnp.dot(four_re, mid_re, precision=highest) + jnp.dot(four_im, mid_im, precision=highest)
    prop_im = jnp.dot(four_re, mid_im, precision=highest) - jnp.dot(four_im, mid_re, precision=highest)
    return (
        block_table(four_re, four_im),
        block_table(four_re, -four_im),
        block_table(prop_re, prop_im),
        block_table(prop_re.T, -prop_im.T),
    )


def product(left, right):
    return jnp.dot(left, right, preferred_element_type=F32)


def beside(stacked):
    half = stacked.shape[0] // 2
    return jnp.concatenate([stacked[:half], stacked[half:]], axis=1).astype(BF)


def stage_kernel(
    plan, stage, *refs
):
    (first_tile, end_tile, final_tile, halo_start, has_past, is_last, group_tile, group_goes_on) = plan
    refs = list(refs)
    row_ref, col_ref, count_ref = refs[:3]
    del refs[:3]
    four_ref, conj_ref, prop_ref, back_ref = refs[:4]
    del refs[:4]
    probe_ref, intensity_ref, specimen_ref = refs[:3]
    del refs[:3]
    halo_now = refs.pop(0)
    if has_past:
        halo_past, carry_in, probe_in = refs[:3]
        del refs[:4]
    if group_goes_on:
        del refs[:1]
    interior_ref = refs.pop(0)
    overflow_ref = refs.pop(0)
    carry_out = None if is_last else refs.pop(0)
    probe_out = refs.pop(0)
    (slots_ref, ext_ref, acc_ref, measured_ref, round_ref, twice_ref, sum_ref, win_ref, wave0_ref, wave1_ref,
     stack_ref, tile_ref, load_sem, slot_sem, store_sem) = refs
    extent = probe_ref.shape[1]
    tiles = end_tile - first_tile
    past_tiles = halo_start - first_tile
    own_count = count_ref[0]
    slot_total = row_ref.shape[0]

    copies = []
    for j in range(tiles):
        lanes = pl.ds((first_tile + j) * LANES, LANES)
        copies.append(pltpu.make_async_copy(
            specimen_ref.at[:, :, :, lanes], ext_ref.at[:, :, j, pl.ds(0, extent), :], load_sem.at[2 * j]))
        if j < past_tiles:
            at = halo_past.shape[3] - (past_tiles - j) * LANES
            source = halo_past.at[:, :, :, pl.ds(at, LANES)]
        else:
            source = halo_now.at[:, :, :, pl.ds((j - past_tiles) * LANES, LANES)]
        copies.append(pltpu.make_async_copy(
            source, ext_ref.at[:, :, j, pl.ds(extent, extent), :], load_sem.at[2 * j + 1]))
    for copy in copies:
        copy.start()
    carried = None
    if has_past:
        carried = pltpu.make_async_copy(carry_in, acc_ref.at[:, :, pl.ds(0, past_tiles), :, :], store_sem.at[0])
        carried.start()

    def gather(k, n):
        last = (col_ref[k] + extent - 1) // LANES
        here = (last >= halo_start) & (last < end_tile) & (k < own_count)

        @pl.when(here)
        def _():
            slots_ref[n] = k

        return n + here.astype(jnp.int32)

    n_slots = lax.fori_loop(0, slot_total, gather, jnp.int32(0))

    def fetch(i):
        return pltpu.make_async_copy(
            intensity_ref.at[slots_ref[i]], measured_ref.at[lax.rem(i, 2)], slot_sem.at[lax.rem(i, 2)])

    @pl.when(n_slots > 0)
    def _():
        fetch(0).start()

    for part in range(2):
        for j in range(2):
            block = probe_ref[part, :, j * LANES:(j + 1) * LANES]
            twice_ref[part, j, pl.ds(0, extent), :] = block
            twice_ref[part, j, pl.ds(extent, extent), :] = block
    sum_ref[...] = jnp.zeros_like(sum_ref)
    for j in range(tiles):
        if not (has_past and j < past_tiles):
            acc_ref[:, :, j] = jnp.zeros_like(acc_ref[:, :, j])
    for copy in copies:
        copy.wait()
    if carried is not None:
        carried.wait()

    lane = lax.broadcasted_iota(jnp.int32, (extent, LANES), 1)

    def visit(i, unused):
        slot = slots_ref[i]

        @pl.when(i + 1 < n_slots)
        def _():
            fetch(i + 1).start()

        r = row_ref[slot]
        c = col_ref[slot]
        b = c // LANES
        shift = c - b * LANES
        at0 = b - first_tile
        at1 = at0 + 1
        at2 = jnp.minimum(at0 + 2, tiles - 1)

        def rows_of_window(t, unused):
            own = t * 16
            at = pl.multiple_of(jnp.where(own < r, own + extent, own), 16)
            own = pl.multiple_of(own, 16)
            low = lax.broadcasted_iota(jnp.int32, (16, LANES), 1) < shift
            mixed = (own < r) & (own + 16 > r)
            from_own = lax.broadcasted_iota(jnp.int32, (16, LANES), 0) + own >= r
            for part in range(2):
                for s in range(2):
                    pick = []
                    for j in (at0, at1, at2):
                        far = ext_ref[part, s, j, pl.ds(at, 16), :].astype(F32)
                        near = ext_ref[part, s, j, pl.ds(own, 16), :].astype(F32)
                        pick.append(jnp.where(from_own, near, far))
                    win_ref[part, s, pl.ds(own, 16), 0:LANES] = jnp.where(low, pick[2], pick[0]).astype(BF)
                    win_ref[part, s, pl.ds(own, 16), LANES:2 * LANES] = pick[1].astype(BF)
            return unused

        lax.fori_loop(0, extent // 16, rows_of_window, 0)

        low = lane < shift
        for part in range(2):
            left = pltpu.roll(twice_ref[part, 0, pl.ds(extent - r, extent), :], shift, 1)
            right = pltpu.roll(twice_ref[part, 1, pl.ds(extent - r, extent), :], shift, 1)
            wave0_ref[part, :, 0:LANES] = jnp.where(low, right, left)
            wave0_ref[part, :, LANES:2 * LANES] = jnp.where(low, left, right)

        def leave(wave_ref, s):
            spec_re = win_ref[0, s].astype(F32)
            spec_im = win_ref[1, s].astype(F32)
            wave_re, wave_im = wave_ref[0], wave_ref[1]
            stack_ref[0:extent] = (wave_re * spec_re - wave_im * spec_im).astype(BF)
            stack_ref[extent:2 * extent] = (wave_re * spec_im + wave_im * spec_re).astype(BF)

        def return_through(wave_ref, s, grad):
            grad_re, grad_im = grad[:, :extent], grad[:, extent:]
            wave_re, wave_im = wave_ref[0], wave_ref[1]
            tile_ref[0, s] = (wave_re * grad_re + wave_im * grad_im).astype(BF)
            tile_ref[1, s] = (wave_re * grad_im - wave_im * grad_re).astype(BF)
            spec_re = win_ref[0, s].astype(F32)
            spec_im = win_ref[1, s].astype(F32)
            return spec_re * grad_re + spec_im * grad_im, spec_re * grad_im - spec_im * grad_re

        leave(wave0_ref, 0)
        wave = product(beside(product(prop_ref[...], stack_ref[...])), back_ref[...])
        wave1_ref[0] = wave[:, :extent]
        wave1_ref[1] = wave[:, extent:]
        leave(wave1_ref, 1)
        far = product(beside(product(four_ref[...], stack_ref[...])), conj_ref[...])
        fetch(i).wait()
        far_re, far_im = far[:, :extent], far[:, extent:]
        residual = far_re * far_re + far_im * far_im - measured_ref[lax.rem(i, 2)].astype(F32)
        stack_ref[0:extent] = (residual * far_re).astype(BF)
        stack_ref[extent:2 * extent] = (residual * far_im).astype(BF)
        grad = product(beside(product(conj_ref[...], stack_ref[...])), four_ref[...])
        back_re, back_im = return_through(wave1_ref, 1, grad)
        stack_ref[0:extent] = back_re.astype(BF)
        stack_ref[extent:2 * extent] = back_im.astype(BF)
        grad = product(beside(product(back_ref[...], stack_ref[...])), prop_ref[...])
        back = return_through(wave0_ref, 0, grad)

        unroll = lax.rem(LANES - shift, LANES)
        low = lane < LANES - shift
        for part in range(2):
            left = pltpu.roll(back[part][:, :LANES], unroll, 1)
            right = pltpu.roll(back[part][:, LANES:], unroll, 1)
            rows = pl.ds(extent - r, extent)
            sum_ref[part, 0, rows, :] += jnp.where(low, left, right)
            sum_ref[part, 1, rows, :] += jnp.where(low, right, left)

        def rows_of_tile(t, unused):
            own = pl.multiple_of(t * 16, 16)
            low = lax.broadcasted_iota(jnp.int32, (16, LANES), 1) < shift
            from_own = lax.broadcasted_iota(jnp.int32, (16, LANES), 0) + own >= r

            def add_rows(at, keep):
                for part in range(2):
                    for s in range(2):
                        outer = tile_ref[part, s, pl.ds(own, 16), 0:LANES].astype(F32)
                        inner = tile_ref[part, s, pl.ds(own, 16), LANES:2 * LANES].astype(F32)
                        rows = pl.ds(at, 16)
                        acc_ref[part, s, at0, rows, :] += jnp.where(keep & ~low, outer, 0.0)
                        acc_ref[part, s, at1, rows, :] += jnp.where(keep, inner, 0.0)
                        acc_ref[part, s, at2, rows, :] += jnp.where(keep & low, outer, 0.0)

            @pl.when(own + 16 > r)
            def _():
                add_rows(own, from_own)

            @pl.when(own < r)
            def _():
                add_rows(pl.multiple_of(own + extent, 16), ~from_own)

            return unused

        lax.fori_loop(0, extent // 16, rows_of_tile, 0)
        return unused

    lax.fori_loop(0, n_slots, visit, 0)

    copies = []
    done_tiles = final_tile - first_tile
    for j in range(done_tiles):
        lanes = pl.ds((first_tile + j) * LANES, LANES)
        copies.append(pltpu.make_async_copy(
            acc_ref.at[:, :, j, pl.ds(0, extent), :], interior_ref.at[:, :, :, lanes], load_sem.at[2 * j]))
        copies[-1].start()
        round_ref[:, :, j] = acc_ref[:, :, j, extent:2 * extent, :].astype(BF)
        copies.append(pltpu.make_async_copy(
            round_ref.at[:, :, j], overflow_ref.at[:, :, :, pl.ds((first_tile - group_tile + j) * LANES, LANES)],
            load_sem.at[2 * j + 1]))
        copies[-1].start()
    if carry_out is not None:
        copies.append(pltpu.make_async_copy(
            acc_ref.at[:, :, pl.ds(done_tiles, tiles - done_tiles), :, :], carry_out, store_sem.at[0]))
        copies[-1].start()
    for part in range(2):
        for j in range(2):
            term = sum_ref[part, j, 0:extent, :] + sum_ref[part, j, extent:2 * extent, :]
            if has_past:
                term = term + probe_in[part, :, j * LANES:(j + 1) * LANES]
            probe_out[part, :, j * LANES:(j + 1) * LANES] = term
    for copy in copies:
        copy.wait()


def run_stage(stage, ends, group, meta, tables, probe_field, intensity, specimen, halos, past):
    slices, block_rows, columns = specimen.shape[1:]
    extent = probe_field.shape[1]
    is_last = stage == len(ends) - 1
    has_past = stage > 0
    halo_start = ends[stage - 1] if has_past else 0
    first_tile = max(halo_start - 2, 0) if has_past else 0
    end_tile = ends[stage]
    final_tile = end_tile if is_last else end_tile - 2
    tiles = end_tile - first_tile
    group_tile, group_end, overflow = group
    group_goes_on = overflow is not None
    plan = (first_tile, end_tile, final_tile, halo_start, has_past, is_last, group_tile, group_goes_on)
    smem = pl.BlockSpec(memory_space=pltpu.SMEM)
    vmem = pl.BlockSpec(memory_space=pltpu.VMEM)
    hbm = pl.BlockSpec(memory_space=pl.ANY)
    args = [*meta, *tables, probe_field, intensity, specimen, halos[stage]]
    in_specs = [smem] * 3 + [vmem] * 4 + [vmem, hbm, hbm, hbm]
    aliases = {}
    if has_past:
        interior, carry, probe_sum = past
        args += [halos[stage - 1], carry, probe_sum, interior]
        in_specs += [hbm, hbm, vmem, hbm]
        aliases = {len(args) - 1: 0}
    if group_goes_on:
        args += [overflow]
        in_specs += [hbm]
        aliases[len(args) - 1] = 1
    outs = [
        jax.ShapeDtypeStruct((2, slices, block_rows, columns), F32),
        jax.ShapeDtypeStruct((2, slices, extent, (group_end - group_tile) * LANES), BF),
    ]
    out_specs = [hbm, hbm]
    if not is_last:
        outs.append(jax.ShapeDtypeStruct((2, slices, end_tile - final_tile, 2 * extent, LANES), F32))
        out_specs.append(hbm)
    outs.append(jax.ShapeDtypeStruct((2, extent, extent), F32))
    out_specs.append(vmem)
    pairs = (2, slices)
    scratch = [
        pltpu.SMEM((meta[0].shape[0],), jnp.int32),
        pltpu.VMEM((*pairs, tiles, 2 * extent, LANES), BF),
        pltpu.VMEM((*pairs, tiles, 2 * extent, LANES), F32),
        pltpu.VMEM((2, extent, extent), BF),
        pltpu.VMEM((*pairs, max(final_tile - first_tile, 1), extent, LANES), BF),
        pltpu.VMEM((2, 2, 2 * extent, LANES), F32),
        pltpu.VMEM((2, 2, 2 * extent, LANES), F32),
        pltpu.VMEM((*pairs, extent, extent), BF),
        pltpu.VMEM((2, extent, extent), F32),
        pltpu.VMEM((2, extent, extent), F32),
        pltpu.VMEM((2 * extent, extent), BF),
        pltpu.VMEM((*pairs, extent, extent), BF),
        pltpu.SemaphoreType.DMA((2 * tiles,)),
        pltpu.SemaphoreType.DMA((2,)),
        pltpu.SemaphoreType.DMA((1,)),
    ]
    results = list(pl.pallas_call(
        functools.partial(stage_kernel, plan, stage),
        out_shape=outs,
        in_specs=in_specs,
        out_specs=out_specs,
        scratch_shapes=scratch,
        input_output_aliases=aliases,
        compiler_params=pltpu.CompilerParams(vmem_limit_bytes=50 * 1024 * 1024),
        cost_estimate=pl.CostEstimate(flops=3 * 10**9, bytes_accessed=8 * 10**6, transcendentals=0),
        name=f"stage{stage}",
    )(*args))
    interior = results.pop(0)
    overflow = results.pop(0)
    carry = None if is_last else results.pop(0)
    return (interior, carry, results.pop(0)), (group_tile, group_end, overflow)


def add_kernel(held_ref, came_ref, out_ref):
    out_ref[...] = held_ref[...] + came_ref[...].astype(F32)


def add_chunk(interior, came, first_tile):
    _, slices, rows, columns = interior.shape
    tiles = came.shape[3] // LANES
    wide = 2 if tiles % 2 == 0 and first_tile % 2 == 0 else 1
    block = (2, slices, rows, wide * LANES)
    place = pl.BlockSpec(block, lambda j: (0, 0, 0, first_tile // wide + j))
    return pl.pallas_call(
        add_kernel,
        grid=(tiles // wide,),
        out_shape=jax.ShapeDtypeStruct(interior.shape, interior.dtype),
        in_specs=[place, pl.BlockSpec(block, lambda j: (0, 0, 0, j))],
        out_specs=place,
        input_output_aliases={0: 0},
        compiler_params=pltpu.CompilerParams(vmem_limit_bytes=32 * 1024 * 1024),
        name=f"add{first_tile}",
    )(interior, came)


def sum_over(value, axis):
    count = lax.axis_size(axis)
    steps = [1 << k for k in range(count.bit_length() - 1)]
    for step in steps[:1] + steps[2:] + steps[1:2]:
        mine = value.astype(BF)
        other = lax.ppermute(mine, axis, [(k, k ^ step) for k in range(count)])
        value = mine.astype(F32) + other.astype(F32)
    return value


def body(ends, sends, specimen, probe_field, transfer_phase, intensity, row_offset, col_offset, counts):
    extent = probe_field.shape[1]
    tables = make_tables(transfer_phase, extent)
    halos, source, start = [], specimen, 0
    for k, end in enumerate(ends):
        piece = source[:, :, :, start * LANES:end * LANES]
        halos.append(passed_along(piece, "row", -1))
        start = end
    meta = (row_offset, col_offset, counts)
    past, came, at = None, [], 0
    for stage in range(len(ends)):
        if stage == 0 or stage - 1 in sends:
            last = min(send for send in sends if send >= stage)
            until = ends[last] if last == len(ends) - 1 else ends[last] - 2
            group = (at, until, None)
        past, group = run_stage(
            stage, ends, group, meta, tables, probe_field, intensity, specimen, halos, past)
        if stage in sends:
            if stage + 1 < len(ends):
                sent, halos[stage + 1] = lax.optimization_barrier((group[2], halos[stage + 1]))
                group = (*group[:2], sent)
            came.append((passed_along(group[2], "row", 1), group[0]))
            at = group[1]
    interior, _, probe_sum = past
    early = came[0][0]
    early, probe_sum = lax.optimization_barrier((early, probe_sum))
    came[0] = (early, came[0][1])
    probe_total = sum_over(probe_sum, "row")
    for chunk, first in came:
        interior = add_chunk(interior, chunk, first)
    return interior, probe_total


def solution(mesh):
    return jax.shard_map(
        functools.partial(body, (5, 10, 16), (1, 2)),
        mesh=mesh,
        in_specs=(
            P("group", None, "row", None),
            P("group", None, None),
            P(),
            P(("group", "row"), None, None),
            P(("group", "row")),
            P(("group", "row")),
            P(("group", "row")),
        ),
        out_specs=(P("group", None, "row", None), P("group", None, None)),
        check_vma=False,
    )
```

profile of v0, /device:TPU:1, one launch (start us, length us, event | category | flops | bytes accessed | tf_op | source)
XLA Modules:
  0.0 164.8 jit_solution(9636231538759553232)
XLA Ops:
  0.6 3.5 %fusion.11 = (bf16[2,2,256,640]{3,2,1,0:T(8,128)(2,1)}, bf16[2,2,256,640]{3,2,1,0:T(8,128)(2,1)}) fusion(bf16[2,2,256,2048]{3,2,1,0:T(8,128)(2,1)} %refs_9_.5), kind=kLoop, calls=%fused_computation.22 | loop fusion | bytes 5242880 | tf_op jit(solution)/shard_map/slice | solution.py:397
  4.1 2.1 %collective-permute-start.1 = (bf16[2,2,256,640]{3,2,1,0:T(8,128)(2,1)}, bf16[2,2,256,640]{3,2,1,0:T(8,128)(2,1)}, u32[]{:S(2)}, u32[]{:S(2)}) collective-permute-start(bf16[2,2,256,640]{3,2,1,0:T(8,128)(2,1)} %get-tuple-element.32), channel_id=1, source_target_pairs={{1,0},{2,1},{3,2},{4,3},{5,4},{6,5},{7,6},{8,7},{9,8},{10,9},{11,1... | collective-permute-start | bytes 3932168 | tf_op jit(solution)/shard_map/ppermute | solution.py:20
  6.2 1.9 %collective-permute-start = (bf16[2,2,256,640]{3,2,1,0:T(8,128)(2,1)}, bf16[2,2,256,640]{3,2,1,0:T(8,128)(2,1)S(1)}, u32[]{:S(2)}, u32[]{:S(2)}) collective-permute-start(bf16[2,2,256,640]{3,2,1,0:T(8,128)(2,1)} %get-tuple-element.33), channel_id=1, source_target_pairs={{1,0},{2,1},{3,2},{4,3},{5,4},{6,5},{7,6},{8,7},{9,8},{10,9},{11,1... | collective-permute-start | bytes 3932168 | tf_op jit(solution)/shard_map/ppermute | solution.py:20
  8.2 2.8 %slice.11 = bf16[2,2,256,768]{3,2,1,0:T(8,128)(2,1)} slice(bf16[2,2,256,2048]{3,2,1,0:T(8,128)(2,1)} %refs_9_.5), slice={[0:2], [0:2], [0:256], [1280:2048]} | slice | bytes 3145728 | tf_op jit(solution)/shard_map/slice | solution.py:397
  10.9 1.9 %collective-permute-start.2 = (bf16[2,2,256,768]{3,2,1,0:T(8,128)(2,1)}, bf16[2,2,256,768]{3,2,1,0:T(8,128)(2,1)}, u32[]{:S(2)}, u32[]{:S(2)}) collective-permute-start(bf16[2,2,256,768]{3,2,1,0:T(8,128)(2,1)} %slice.11), channel_id=1, source_target_pairs={{1,0},{2,1},{3,2},{4,3},{5,4},{6,5},{7,6},{8,7},{9,8},{10,9},{11,1... | collective-permute-start | bytes 4718600 | tf_op jit(solution)/shard_map/ppermute | solution.py:20
  12.9 0.7 fusion.1
  13.6 0.7 fusion.2
  14.3 0.7 fusion
  15.1 0.7 negate_convert_fusion
  15.8 0.6 copy-done.8
  16.5 0.8 maximum_maximum_fusion
  17.3 1.3 copy.18.refs_5_
  19.2 1.0 maximum_maximum_fusion.1.refs_6_
  20.2 4.2 %collective-permute-done.1.refs_10_.refs_11_ = bf16[2,2,256,640]{3,2,1,0:T(8,128)(2,1)} collective-permute-done((bf16[2,2,256,640]{3,2,1,0:T(8,128)(2,1)}, bf16[2,2,256,640]{3,2,1,0:T(8,128)(2,1)}, u32[]{:S(2)}, u32[]{:S(2)}) %collective-permute-start.1) | collective-permute-done | bytes 1310752 | tf_op jit(solution)/shard_map/ppermute | solution.py:20
  24.4 24.7 %stage0.1 = (f32[2,2,256,2048]{3,2,1,0:T(8,128)}, bf16[2,2,256,1024]{3,2,1,0:T(8,128)(2,1)}, f32[2,2,2,512,128]{4,3,2,1,0:T(8,128)}, f32[2,256,256]{2,1,0:T(8,128)S(1)}) custom-call(s32[16]{0:T(128)S(1)} %copy-done.3, s32[16]{0:T(128)S(1)} %copy-done.4, s32[1]{0:T(128)S(6)} %copy.24.refs_2_, bf16[512,512]{1,0:T(8,128)(2,1)S(1)} %copy-done.1, ...), custom_call_target="tpu_custom_call" | custom-call | flops 3000000000 | bytes 8000000 | tf_op jit(solution)/shard_map/stage0/pallas_call | solution.py:343
  49.1 1.0 copy-done.7
  50.2 26.5 %stage1.1 = (f32[2,2,256,2048]{3,2,1,0:T(8,128)}, bf16[2,2,256,1024]{3,2,1,0:T(8,128)(2,1)}, f32[2,2,2,512,128]{4,3,2,1,0:T(8,128)}, f32[2,256,256]{2,1,0:T(8,128)S(1)}) custom-call(s32[16]{0:T(128)S(1)} %copy-done.3, s32[16]{0:T(128)S(1)} %copy-done.4, s32[1]{0:T(128)S(6)} %copy.24.refs_2_, ...), custom_call_target="tpu_custom_call", output_to_operand_aliasing={{0}: (14, {}), {1}: (15, {})} | custom-call | flops 3000000000 | bytes 8000000 | tf_op jit(solution)/shard_map/stage1/pallas_call | solution.py:343
  76.7 1.9 %collective-permute-start.3 = (bf16[2,2,256,1024]{3,2,1,0:T(8,128)(2,1)}, bf16[2,2,256,1024]{3,2,1,0:T(8,128)(2,1)S(1)}, u32[]{:S(2)}, u32[]{:S(2)}) collective-permute-start(bf16[2,2,256,1024]{3,2,1,0:T(8,128)(2,1)} %get-tuple-element.27), channel_id=1, source_target_pairs={{0,1},{1,2},{2,3},{3,4},{4,5},{5,6},{6,7},{7,8},{8,9},{9,10},{10,1... | collective-permute-start | bytes 6291464 | tf_op jit(solution)/shard_map/ppermute | solution.py:20
  78.7 22.7 %stage2.1 = (f32[2,2,256,2048]{3,2,1,0:T(8,128)}, bf16[2,2,256,1024]{3,2,1,0:T(8,128)(2,1)}, f32[2,256,256]{2,1,0:T(8,128)S(1)}) custom-call(s32[16]{0:T(128)S(1)} %copy-done.3, s32[16]{0:T(128)S(1)} %copy-done.4, s32[1]{0:T(128)S(6)} %copy.24.refs_2_, bf16[512,512]{1,0:T(8,128)(2,1)S(1)} %copy-done.1, ...), custom_call_target="tpu_custom_call", output_to_operand_aliasing={{0}: (14, {})} | custom-call | flops 3000000000 | bytes 8000000 | tf_op jit(solution)/shard_map/stage2/pallas_call | solution.py:343
  101.3 1.9 %collective-permute-start.4 = (bf16[2,2,256,1024]{3,2,1,0:T(8,128)(2,1)}, bf16[2,2,256,1024]{3,2,1,0:T(8,128)(2,1)S(1)}, u32[]{:S(2)}, u32[]{:S(2)}) collective-permute-start(bf16[2,2,256,1024]{3,2,1,0:T(8,128)(2,1)} %get-tuple-element.30), channel_id=1, source_target_pairs={{0,1},{1,2},{2,3},{3,4},{4,5},{5,6},{6,7},{7,8},{8,9},{9,10},{10,1... | collective-permute-start | bytes 6291464 | tf_op jit(solution)/shard_map/ppermute | solution.py:20
  103.3 0.7 collective-permute-start.5
  104.0 3.8 %collective-permute-done.5 = bf16[2,256,256]{2,1,0:T(8,128)(2,1)S(1)} collective-permute-done((bf16[2,256,256]{2,1,0:T(8,128)(2,1)S(1)}, bf16[2,256,256]{2,1,0:T(8,128)(2,1)S(1)}, u32[]{:S(2)}, u32[]{:S(2)}) %collective-permute-start.5) | collective-permute-done | bytes 262176 | tf_op jit(solution)/shard_map/ppermute | solution.py:387
  107.8 8.7 %collective-permute-start.6 = (bf16[2,256,256]{2,1,0:T(8,128)(2,1)S(1)}, bf16[2,256,256]{2,1,0:T(8,128)(2,1)S(1)}, u32[]{:S(2)}, u32[]{:S(2)}) collective-permute-start(bf16[2,256,256]{2,1,0:T(8,128)(2,1)S(1)} %add_convert_fusion.2), channel_id=1, source_target_pairs={{0,4},{1,5},{2,6},{3,7},{4,0},{5,1},{6,2},{7,3},{8,12},{9,13},{10,... | collective-permute-start | bytes 786440 | tf_op jit(solution)/shard_map/ppermute | solution.py:387
  116.5 6.5 %collective-permute-done.6 = bf16[2,256,256]{2,1,0:T(8,128)(2,1)S(1)} collective-permute-done((bf16[2,256,256]{2,1,0:T(8,128)(2,1)S(1)}, bf16[2,256,256]{2,1,0:T(8,128)(2,1)S(1)}, u32[]{:S(2)}, u32[]{:S(2)}) %collective-permute-start.6) | collective-permute-done | bytes 262176 | tf_op jit(solution)/shard_map/ppermute | solution.py:387
  123.1 0.1 add_convert_fusion.1
  123.1 0.1 collective-permute-start.7
  123.2 13.8 %collective-permute-done.7 = bf16[2,256,256]{2,1,0:T(8,128)(2,1)S(1)} collective-permute-done((bf16[2,256,256]{2,1,0:T(8,128)(2,1)S(1)}, bf16[2,256,256]{2,1,0:T(8,128)(2,1)S(1)}, u32[]{:S(2)}, u32[]{:S(2)}) %collective-permute-start.7) | collective-permute-done | bytes 262176 | tf_op jit(solution)/shard_map/ppermute | solution.py:387
  137.0 0.1 add_convert_fusion
  137.1 17.4 %collective-permute-start.8 = (bf16[2,256,256]{2,1,0:T(8,128)(2,1)S(1)}, bf16[2,256,256]{2,1,0:T(8,128)(2,1)S(1)}, u32[]{:S(2)}, u32[]{:S(2)}) collective-permute-start(bf16[2,256,256]{2,1,0:T(8,128)(2,1)S(1)} %add_convert_fusion), channel_id=1, source_target_pairs={{0,2},{1,3},{2,0},{3,1},{4,6},{5,7},{6,4},{7,5},{8,10},{9,11},{10,... | collective-permute-start | bytes 786440 | tf_op jit(solution)/shard_map/ppermute | solution.py:387
  154.4 4.8 %add0.1.held_ref = f32[2,2,256,2048]{3,2,1,0:T(8,128)} custom-call(f32[2,2,256,2048]{3,2,1,0:T(8,128)} %get-tuple-element.26.held_ref, bf16[2,2,256,1024]{3,2,1,0:T(8,128)(2,1)S(1)} %collective-permute-done.3.came_ref), custom_call_target="tpu_custom_call", output_to_operand_aliasing={{}: (0, {})} | custom-call | tf_op jit(solution)/shard_map/add0/pallas_call | solution.py:370
  159.2 4.8 %add8.1 = f32[2,2,256,2048]{3,2,1,0:T(8,128)} custom-call(f32[2,2,256,2048]{3,2,1,0:T(8,128)} %add0.1.held_ref, bf16[2,2,256,1024]{3,2,1,0:T(8,128)(2,1)S(1)} %collective-permute-done.4.came_ref), custom_call_target="tpu_custom_call", output_to_operand_aliasing={{}: (0, {})} | custom-call | tf_op jit(solution)/shard_map/add8/pallas_call | solution.py:370
  164.0 0.8 convert_add_fusion
  (28 shorter events, 0.2 us)
Async XLA Ops:
  4.1 8.7 %copy-start.10 = (f32[256]{0:T(256)S(1)}, f32[256]{0:T(256)}, u32[]{:S(2)}) copy-start(f32[256]{0:T(256)} %param.11) | copy-start | bytes 3076
  4.1 8.8 %copy-start.5 = (f32[256,256]{1,0:T(8,128)S(1)}, f32[256,256]{1,0:T(8,128)}, u32[]{:S(2)}) copy-start(f32[256,256]{1,0:T(8,128)} %constant.4.clone) | copy-start | bytes 786436
  4.1 8.8 %copy-start.6 = (f32[256,256]{1,0:T(8,128)S(1)}, f32[256,256]{1,0:T(8,128)}, u32[]{:S(2)}) copy-start(f32[256,256]{1,0:T(8,128)} %constant.5.clone) | copy-start | bytes 786436
  4.1 20.3 %collective-permute-start.1 = (bf16[2,2,256,640]{3,2,1,0:T(8,128)(2,1)}, bf16[2,2,256,640]{3,2,1,0:T(8,128)(2,1)}, u32[]{:S(2)}, u32[]{:S(2)}) collective-permute-start(bf16[2,2,256,640]{3,2,1,0:T(8,128)(2,1)} %get-tuple-element.32), channel_id=1, source_target_pairs={{1,0},{2,1},{3,2},{4,3},{5,4},{6,5},{7,6},{8,7},{9,8},{10,9},{11,1... | collective-permute-start | bytes 3932168 | tf_op jit(solution)/shard_map/ppermute | solution.py:20
  6.2 42.9 %collective-permute-start = (bf16[2,2,256,640]{3,2,1,0:T(8,128)(2,1)}, bf16[2,2,256,640]{3,2,1,0:T(8,128)(2,1)S(1)}, u32[]{:S(2)}, u32[]{:S(2)}) collective-permute-start(bf16[2,2,256,640]{3,2,1,0:T(8,128)(2,1)} %get-tuple-element.33), channel_id=1, source_target_pairs={{1,0},{2,1},{3,2},{4,3},{5,4},{6,5},{7,6},{8,7},{9,8},{10,9},{11,1... | collective-permute-start | bytes 3932168 | tf_op jit(solution)/shard_map/ppermute | solution.py:20
  10.9 65.8 %collective-permute-start.2 = (bf16[2,2,256,768]{3,2,1,0:T(8,128)(2,1)}, bf16[2,2,256,768]{3,2,1,0:T(8,128)(2,1)}, u32[]{:S(2)}, u32[]{:S(2)}) collective-permute-start(bf16[2,2,256,768]{3,2,1,0:T(8,128)(2,1)} %slice.11), channel_id=1, source_target_pairs={{1,0},{2,1},{3,2},{4,3},{5,4},{6,5},{7,6},{8,7},{9,8},{10,9},{11,1... | collective-permute-start | bytes 4718600 | tf_op jit(solution)/shard_map/ppermute | solution.py:20
  15.0 9.4 %copy-start = (f32[2,256,256]{2,1,0:T(8,128)S(1)}, f32[2,256,256]{2,1,0:T(8,128)}, u32[]{:S(2)}) copy-start(f32[2,256,256]{2,1,0:T(8,128)} %refs_7_.5) | copy-start | bytes 1572868
  15.0 9.4 %copy-start.1 = (bf16[512,512]{1,0:T(8,128)(2,1)S(1)}, bf16[512,512]{1,0:T(8,128)(2,1)}, u32[]{:S(2)}) copy-start(bf16[512,512]{1,0:T(8,128)(2,1)} %constant.16.refs_3_) | copy-start | bytes 1572868
  15.0 9.4 %copy-start.2 = (bf16[512,512]{1,0:T(8,128)(2,1)S(1)}, bf16[512,512]{1,0:T(8,128)(2,1)}, u32[]{:S(2)}) copy-start(bf16[512,512]{1,0:T(8,128)(2,1)} %constant.19.refs_4_) | copy-start | bytes 1572868
  15.0 9.4 %copy-start.3 = (s32[16]{0:T(128)S(1)}, s32[16]{0:T(128)}, u32[]{:S(2)}) copy-start(s32[16]{0:T(128)} %refs_0_.5) | copy-start | bytes 196
  15.1 9.4 %copy-start.4 = (s32[16]{0:T(128)S(1)}, s32[16]{0:T(128)}, u32[]{:S(2)}) copy-start(s32[16]{0:T(128)} %refs_1_.5) | copy-start | bytes 196
  15.8 0.7 copy-start.8
  15.8 0.7 copy-start.9
  49.1 1.0 copy-start.7
  76.7 26.5 %collective-permute-start.3 = (bf16[2,2,256,1024]{3,2,1,0:T(8,128)(2,1)}, bf16[2,2,256,1024]{3,2,1,0:T(8,128)(2,1)S(1)}, u32[]{:S(2)}, u32[]{:S(2)}) collective-permute-start(bf16[2,2,256,1024]{3,2,1,0:T(8,128)(2,1)} %get-tuple-element.27), channel_id=1, source_target_pairs={{0,1},{1,2},{2,3},{3,4},{4,5},{5,6},{6,7},{7,8},{8,9},{9,10},{10,1... | collective-permute-start | bytes 6291464 | tf_op jit(solution)/shard_map/ppermute | solution.py:20
  101.3 57.8 %collective-permute-start.4 = (bf16[2,2,256,1024]{3,2,1,0:T(8,128)(2,1)}, bf16[2,2,256,1024]{3,2,1,0:T(8,128)(2,1)S(1)}, u32[]{:S(2)}, u32[]{:S(2)}) collective-permute-start(bf16[2,2,256,1024]{3,2,1,0:T(8,128)(2,1)} %get-tuple-element.30), channel_id=1, source_target_pairs={{0,1},{1,2},{2,3},{3,4},{4,5},{5,6},{6,7},{7,8},{8,9},{9,10},{10,1... | collective-permute-start | bytes 6291464 | tf_op jit(solution)/shard_map/ppermute | solution.py:20
  103.3 4.5 %collective-permute-start.5 = (bf16[2,256,256]{2,1,0:T(8,128)(2,1)S(1)}, bf16[2,256,256]{2,1,0:T(8,128)(2,1)S(1)}, u32[]{:S(2)}, u32[]{:S(2)}) collective-permute-start(bf16[2,256,256]{2,1,0:T(8,128)(2,1)S(1)} %convert_element_type.40), channel_id=1, source_target_pairs={{0,1},{1,0},{2,3},{3,2},{4,5},{5,4},{6,7},{7,6},{8,9},{9,8},{10,11... | collective-permute-start | bytes 786440 | tf_op jit(solution)/shard_map/ppermute | solution.py:387
  107.8 15.2 %collective-permute-start.6 = (bf16[2,256,256]{2,1,0:T(8,128)(2,1)S(1)}, bf16[2,256,256]{2,1,0:T(8,128)(2,1)S(1)}, u32[]{:S(2)}, u32[]{:S(2)}) collective-permute-start(bf16[2,256,256]{2,1,0:T(8,128)(2,1)S(1)} %add_convert_fusion.2), channel_id=1, source_target_pairs={{0,4},{1,5},{2,6},{3,7},{4,0},{5,1},{6,2},{7,3},{8,12},{9,13},{10,... | collective-permute-start | bytes 786440 | tf_op jit(solution)/shard_map/ppermute | solution.py:387
  123.1 13.8 %collective-permute-start.7 = (bf16[2,256,256]{2,1,0:T(8,128)(2,1)S(1)}, bf16[2,256,256]{2,1,0:T(8,128)(2,1)S(1)}, u32[]{:S(2)}, u32[]{:S(2)}) collective-permute-start(bf16[2,256,256]{2,1,0:T(8,128)(2,1)S(1)} %add_convert_fusion.1), channel_id=1, source_target_pairs={{0,8},{1,9},{2,10},{3,11},{4,12},{5,13},{6,14},{7,15},{8,0},{9,1},... | collective-permute-start | bytes 786440 | tf_op jit(solution)/shard_map/ppermute | solution.py:387
  137.1 26.9 %collective-permute-start.8 = (bf16[2,256,256]{2,1,0:T(8,128)(2,1)S(1)}, bf16[2,256,256]{2,1,0:T(8,128)(2,1)S(1)}, u32[]{:S(2)}, u32[]{:S(2)}) collective-permute-start(bf16[2,256,256]{2,1,0:T(8,128)(2,1)S(1)} %add_convert_fusion), channel_id=1, source_target_pairs={{0,2},{1,3},{2,0},{3,1},{4,6},{5,7},{6,4},{7,5},{8,10},{9,11},{10,... | collective-permute-start | bytes 786440 | tf_op jit(solution)/shard_map/ppermute | solution.py:387
where the time goes:
time: 167 us; the launch traced here: 165 us
  Pallas kernels  83.4 us (50%)
  starting transfers between devices  36.6 us (22%)
  waiting for transfers between devices  28.3 us (17%)
  local copies, waits for them, and re-layouts  9.33 us (6%)
  other arithmetic  2.89 us (2%)
  matrix products  2.74 us (2%)
    pallas_call x3, Pallas kernels, run_stage(): pl.pallas_call(functools.partial(stage_kernel, plan, stage), out_shape=ou...  73.9 us
    ppermute x4, starting transfers between devices, sum_over(): other = lax.ppermute(mine, axis, [(k, k ^ step) for k in range(count)])  26.8 us
    ppermute x4, waiting for transfers between devices, sum_over(): other = lax.ppermute(mine, axis, [(k, k ^ step) for k in range(count)])  24.1 us
    ppermute x5, starting transfers between devices, passed_along(): lax.ppermute(value, axis, [(source, source + steps) for source in range(f...  9.76 us
    pallas_call x2, Pallas kernels, add_chunk(): pl.pallas_call(add_kernel, grid=(tiles // wide,), out_shape=jax.ShapeDtyp...  9.54 us
    slice x2, local copies, waits for them, and re-layouts, body(): piece = source[:, :, :, start * LANES:end * LANES]  6.27 us
    ppermute x5, waiting for transfers between devices, passed_along(): lax.ppermute(value, axis, [(source, source + steps) for source in range(f...  4.21 us
  transfers between devices with their start and end apart: 9, of which 4 were waited for; matrix products, arithmetic and copies ran while one was open for 5% of the time, Pallas kernels for 51%

commit v1 on v0

--- a/solution.py
+++ b/solution.py
@@ -81,7 +81,7 @@
     carry_out = None if is_last else refs.pop(0)
     probe_out = refs.pop(0)
     (slots_ref, ext_ref, acc_ref, measured_ref, round_ref, twice_ref, sum_ref, win_ref, wave0_ref, wave1_ref,
-     stack_ref, tile_ref, load_sem, slot_sem, store_sem) = refs
+     stack_ref, half_ref, tile_ref, load_sem, slot_sem, store_sem) = refs
     extent = probe_ref.shape[1]
     tiles = end_tile - first_tile
     past_tiles = halo_start - first_tile
@@ -121,11 +121,15 @@
 
     def fetch(i):
         return pltpu.make_async_copy(
-            intensity_ref.at[slots_ref[i]], measured_ref.at[lax.rem(i, 2)], slot_sem.at[lax.rem(i, 2)])
-
-    @pl.when(n_slots > 0)
-    def _():
-        fetch(0).start()
+            intensity_ref.at[slots_ref[i]], measured_ref.at[lax.rem(i, 4)], slot_sem.at[lax.rem(i, 4)])
+
+    def fetch_pair(i):
+        for g in range(2):
+            @pl.when(i + g < n_slots)
+            def _():
+                fetch(i + g).start()
+
+    fetch_pair(0)
 
     for part in range(2):
         for j in range(2):
@@ -143,120 +147,148 @@
 
     lane = lax.broadcasted_iota(jnp.int32, (extent, LANES), 1)
 
-    def visit(i, unused):
-        slot = slots_ref[i]
-
-        @pl.when(i + 1 < n_slots)
-        def _():
-            fetch(i + 1).start()
-
-        r = row_ref[slot]
-        c = col_ref[slot]
-        b = c // LANES
-        shift = c - b * LANES
-        at0 = b - first_tile
-        at1 = at0 + 1
-        at2 = jnp.minimum(at0 + 2, tiles - 1)
-
-        def rows_of_window(t, unused):
-            own = t * 16
-            at = pl.multiple_of(jnp.where(own < r, own + extent, own), 16)
-            own = pl.multiple_of(own, 16)
+    def visit(i, many):
+        places = []
+        for g in range(many):
+            slot = slots_ref[i + g]
+            r = row_ref[slot]
+            c = col_ref[slot]
+            b = c // LANES
+            at0 = b - first_tile
+            places.append((r, c - b * LANES, (at0, at0 + 1, jnp.minimum(at0 + 2, tiles - 1))))
+        every = range(many)
+
+        def row_starts(r):
+            return [pl.multiple_of(jnp.where(t + 16 <= r, t + extent, t), 16) for t in range(0, extent, 16)]
+
+        def masks(r, shift):
+            mixed = pl.multiple_of(r // 16 * 16, 16)
             low = lax.broadcasted_iota(jnp.int32, (16, LANES), 1) < shift
-            mixed = (own < r) & (own + 16 > r)
-            from_own = lax.broadcasted_iota(jnp.int32, (16, LANES), 0) + own >= r
+            own = lax.broadcasted_iota(jnp.int32, (16, LANES), 0) + mixed >= r
+            return mixed, low, own
+
+        def take_window(g):
+            r, shift, ats = places[g]
+            at0, at1, at2 = ats
+            mixed, low, own = masks(r, shift)
+            row_at = row_starts(r)
             for part in range(2):
                 for s in range(2):
-                    pick = []
-                    for j in (at0, at1, at2):
-                        far = ext_ref[part, s, j, pl.ds(at, 16), :].astype(F32)
-                        near = ext_ref[part, s, j, pl.ds(own, 16), :].astype(F32)
-                        pick.append(jnp.where(from_own, near, far))
-                    win_ref[part, s, pl.ds(own, 16), 0:LANES] = jnp.where(low, pick[2], pick[0]).astype(BF)
-                    win_ref[part, s, pl.ds(own, 16), LANES:2 * LANES] = pick[1].astype(BF)
-            return unused
-
-        lax.fori_loop(0, extent // 16, rows_of_window, 0)
-
-        low = lane < shift
-        for part in range(2):
-            left = pltpu.roll(twice_ref[part, 0, pl.ds(extent - r, extent), :], shift, 1)
-            right = pltpu.roll(twice_ref[part, 1, pl.ds(extent - r, extent), :], shift, 1)
-            wave0_ref[part, :, 0:LANES] = jnp.where(low, right, left)
-            wave0_ref[part, :, LANES:2 * LANES] = jnp.where(low, left, right)
-
-        def leave(wave_ref, s):
-            spec_re = win_ref[0, s].astype(F32)
-            spec_im = win_ref[1, s].astype(F32)
-            wave_re, wave_im = wave_ref[0], wave_ref[1]
-            stack_ref[0:extent] = (wave_re * spec_re - wave_im * spec_im).astype(BF)
-            stack_ref[extent:2 * extent] = (wave_re * spec_im + wave_im * spec_re).astype(BF)
-
-        def return_through(wave_ref, s, grad):
-            grad_re, grad_im = grad[:, :extent], grad[:, extent:]
-            wave_re, wave_im = wave_ref[0], wave_ref[1]
-            tile_ref[0, s] = (wave_re * grad_re + wave_im * grad_im).astype(BF)
-            tile_ref[1, s] = (wave_re * grad_im - wave_im * grad_re).astype(BF)
-            spec_re = win_ref[0, s].astype(F32)
-            spec_im = win_ref[1, s].astype(F32)
+                    for t, at in zip(range(0, extent, 16), row_at):
+                        rows = pl.ds(at, 16)
+                        win_ref[g, part, s, t:t + 16, 0:LANES] = jnp.where(
+                            low, ext_ref[part, s, at2, rows, :], ext_ref[part, s, at0, rows, :])
+                        win_ref[g, part, s, t:t + 16, LANES:2 * LANES] = ext_ref[part, s, at1, rows, :]
+                    rows, rows_under = pl.ds(mixed, 16), pl.ds(pl.multiple_of(mixed + extent, 16), 16)
+                    picked = [jnp.where(own, ext_ref[part, s, at, rows, :], ext_ref[part, s, at, rows_under, :])
+                              for at in ats]
+                    win_ref[g, part, s, rows, 0:LANES] = jnp.where(low, picked[2], picked[0])
+                    win_ref[g, part, s, rows, LANES:2 * LANES] = picked[1]
+
+        def take_probe(g):
+            r, shift, _ = places[g]
+            low = lane < shift
+            for part in range(2):
+                left = pltpu.roll(twice_ref[part, 0, pl.ds(extent - r, extent), :], shift, 1)
+                right = pltpu.roll(twice_ref[part, 1, pl.ds(extent - r, extent), :], shift, 1)
+                wave0_ref[g, part, :, 0:LANES] = jnp.where(low, right, left)
+                wave0_ref[g, part, :, LANES:2 * LANES] = jnp.where(low, left, right)
+
+        def put(g, re, im):
+            lanes = slice(g * extent, (g + 1) * extent)
+            stack_ref[0:extent, lanes] = re.astype(BF)
+            stack_ref[extent:2 * extent, lanes] = im.astype(BF)
+
+        def leave(wave_ref, s, g):
+            spec_re = win_ref[g, 0, s].astype(F32)
+            spec_im = win_ref[g, 1, s].astype(F32)
+            wave_re, wave_im = wave_ref[g, 0], wave_ref[g, 1]
+            put(g, wave_re * spec_re - wave_im * spec_im, wave_re * spec_im + wave_im * spec_re)
+
+        def return_through(wave_ref, s, g, grad_re, grad_im):
+            wave_re, wave_im = wave_ref[g, 0], wave_ref[g, 1]
+            tile_ref[g, 0, s] = (wave_re * grad_re + wave_im * grad_im).astype(BF)
+            tile_ref[g, 1, s] = (wave_re * grad_im - wave_im * grad_re).astype(BF)
+            spec_re = win_ref[g, 0, s].astype(F32)
+            spec_im = win_ref[g, 1, s].astype(F32)
             return spec_re * grad_re + spec_im * grad_im, spec_re * grad_im - spec_im * grad_re
 
-        leave(wave0_ref, 0)
-        wave = product(beside(product(prop_ref[...], stack_ref[...])), back_ref[...])
-        wave1_ref[0] = wave[:, :extent]
-        wave1_ref[1] = wave[:, extent:]
-        leave(wave1_ref, 1)
-        far = product(beside(product(four_ref[...], stack_ref[...])), conj_ref[...])
-        fetch(i).wait()
-        far_re, far_im = far[:, :extent], far[:, extent:]
-        residual = far_re * far_re + far_im * far_im - measured_ref[lax.rem(i, 2)].astype(F32)
-        stack_ref[0:extent] = (residual * far_re).astype(BF)
-        stack_ref[extent:2 * extent] = (residual * far_im).astype(BF)
-        grad = product(beside(product(conj_ref[...], stack_ref[...])), four_ref[...])
-        back_re, back_im = return_through(wave1_ref, 1, grad)
-        stack_ref[0:extent] = back_re.astype(BF)
-        stack_ref[extent:2 * extent] = back_im.astype(BF)
-        grad = product(beside(product(back_ref[...], stack_ref[...])), prop_ref[...])
-        back = return_through(wave0_ref, 0, grad)
-
-        unroll = lax.rem(LANES - shift, LANES)
-        low = lane < LANES - shift
-        for part in range(2):
-            left = pltpu.roll(back[part][:, :LANES], unroll, 1)
-            right = pltpu.roll(back[part][:, LANES:], unroll, 1)
+        def transform(left_ref, right_ref):
+            for g in every:
+                half = product(left_ref[...], stack_ref[:, g * extent:(g + 1) * extent])
+                half_ref[g * extent:(g + 1) * extent, 0:extent] = half[:extent].astype(BF)
+                half_ref[g * extent:(g + 1) * extent, extent:2 * extent] = half[extent:].astype(BF)
+            whole = product(half_ref[0:many * extent], right_ref[...])
+            return [(whole[g * extent:(g + 1) * extent, :extent], whole[g * extent:(g + 1) * extent, extent:])
+                    for g in every]
+
+        def give_probe(g, back):
+            r, shift, _ = places[g]
+            unroll = lax.rem(LANES - shift, LANES)
+            low = lane < LANES - shift
             rows = pl.ds(extent - r, extent)
-            sum_ref[part, 0, rows, :] += jnp.where(low, left, right)
-            sum_ref[part, 1, rows, :] += jnp.where(low, right, left)
-
-        def rows_of_tile(t, unused):
-            own = pl.multiple_of(t * 16, 16)
-            low = lax.broadcasted_iota(jnp.int32, (16, LANES), 1) < shift
-            from_own = lax.broadcasted_iota(jnp.int32, (16, LANES), 0) + own >= r
-
-            def add_rows(at, keep):
-                for part in range(2):
-                    for s in range(2):
-                        outer = tile_ref[part, s, pl.ds(own, 16), 0:LANES].astype(F32)
-                        inner = tile_ref[part, s, pl.ds(own, 16), LANES:2 * LANES].astype(F32)
-                        rows = pl.ds(at, 16)
-                        acc_ref[part, s, at0, rows, :] += jnp.where(keep & ~low, outer, 0.0)
-                        acc_ref[part, s, at1, rows, :] += jnp.where(keep, inner, 0.0)
-                        acc_ref[part, s, at2, rows, :] += jnp.where(keep & low, outer, 0.0)
-
-            @pl.when(own + 16 > r)
-            def _():
-                add_rows(own, from_own)
-
-            @pl.when(own < r)
-            def _():
-                add_rows(pl.multiple_of(own + extent, 16), ~from_own)
-
-            return unused
-
-        lax.fori_loop(0, extent // 16, rows_of_tile, 0)
+            for part in range(2):
+                left = pltpu.roll(back[part][:, :LANES], unroll, 1)
+                right = pltpu.roll(back[part][:, LANES:], unroll, 1)
+                sum_ref[part, 0, rows, :] += jnp.where(low, left, right)
+                sum_ref[part, 1, rows, :] += jnp.where(low, right, left)
+
+        def give_tile(g, s):
+            r, shift, ats = places[g]
+            at0, at1, at2 = ats
+            mixed, low, own = masks(r, shift)
+
+            def add_rows(part, at, outer, inner):
+                rows = pl.ds(at, 16)
+                acc_ref[part, s, at0, rows, :] += jnp.where(low, 0.0, outer)
+                acc_ref[part, s, at1, rows, :] += inner
+                acc_ref[part, s, at2, rows, :] += jnp.where(low, outer, 0.0)
+
+            for part in range(2):
+                rows = pl.ds(mixed, 16)
+                outer = tile_ref[g, part, s, rows, 0:LANES].astype(F32)
+                inner = tile_ref[g, part, s, rows, LANES:2 * LANES].astype(F32)
+                add_rows(part, pl.multiple_of(mixed + extent, 16),
+                         jnp.where(own, 0.0, outer), jnp.where(own, 0.0, inner))
+                tile_ref[g, part, s, rows, 0:LANES] = jnp.where(own, outer, 0.0).astype(BF)
+                tile_ref[g, part, s, rows, LANES:2 * LANES] = jnp.where(own, inner, 0.0).astype(BF)
+                for t, at in zip(range(0, extent, 16), row_starts(r)):
+                    add_rows(part, at, tile_ref[g, part, s, t:t + 16, 0:LANES].astype(F32),
+                             tile_ref[g, part, s, t:t + 16, LANES:2 * LANES].astype(F32))
+
+        for g in every:
+            take_window(g)
+            take_probe(g)
+            leave(wave0_ref, 0, g)
+        for g, (re, im) in enumerate(transform(prop_ref, back_ref)):
+            wave1_ref[g, 0] = re
+            wave1_ref[g, 1] = im
+            leave(wave1_ref, 1, g)
+        far = transform(four_ref, conj_ref)
+        for g in every:
+            fetch(i + g).wait()
+        for g, (re, im) in enumerate(far):
+            residual = re * re + im * im - measured_ref[lax.rem(i + g, 4)].astype(F32)
+            put(g, residual * re, residual * im)
+        for g, (re, im) in enumerate(transform(conj_ref, four_ref)):
+            put(g, *return_through(wave1_ref, 1, g, re, im))
+        grads = transform(back_ref, prop_ref)
+        for g, (re, im) in enumerate(grads):
+            give_probe(g, return_through(wave0_ref, 0, g, re, im))
+        for g in every:
+            for s in range(2):
+                give_tile(g, s)
+
+    def visit_pair(p, unused):
+        fetch_pair(2 * p + 2)
+        visit(2 * p, 2)
         return unused
 
-    lax.fori_loop(0, n_slots, visit, 0)
+    lax.fori_loop(0, n_slots // 2, visit_pair, 0)
+
+    @pl.when(lax.rem(n_slots, 2) == 1)
+    def _():
+        visit(n_slots - 1, 1)
 
     copies = []
     done_tiles = final_tile - first_tile
@@ -327,17 +359,18 @@
         pltpu.SMEM((meta[0].shape[0],), jnp.int32),
         pltpu.VMEM((*pairs, tiles, 2 * extent, LANES), BF),
         pltpu.VMEM((*pairs, tiles, 2 * extent, LANES), F32),
-        pltpu.VMEM((2, extent, extent), BF),
+        pltpu.VMEM((4, extent, extent), BF),
         pltpu.VMEM((*pairs, max(final_tile - first_tile, 1), extent, LANES), BF),
         pltpu.VMEM((2, 2, 2 * extent, LANES), F32),
         pltpu.VMEM((2, 2, 2 * extent, LANES), F32),
-        pltpu.VMEM((*pairs, extent, extent), BF),
-        pltpu.VMEM((2, extent, extent), F32),
-        pltpu.VMEM((2, extent, extent), F32),
-        pltpu.VMEM((2 * extent, extent), BF),
-        pltpu.VMEM((*pairs, extent, extent), BF),
+        pltpu.VMEM((2, *pairs, extent, extent), BF),
+        pltpu.VMEM((2, 2, extent, extent), F32),
+        pltpu.VMEM((2, 2, extent, extent), F32),
+        pltpu.VMEM((2 * extent, 2 * extent), BF),
+        pltpu.VMEM((2 * extent, 2 * extent), BF),
+        pltpu.VMEM((2, *pairs, extent, extent), BF),
         pltpu.SemaphoreType.DMA((2 * tiles,)),
-        pltpu.SemaphoreType.DMA((2,)),
+        pltpu.SemaphoreType.DMA((4,)),
         pltpu.SemaphoreType.DMA((1,)),
     ]
     results = list(pl.pallas_call(

time: 167 us -> 144 us (0.86)
  the two profiles are of different devices: /device:TPU:1 before, /device:TPU:3 now
where the time goes in v1:
time: 144 us; the launch traced here: 143 us
  Pallas kernels  49.3 us (34%)
  starting transfers between devices  42.7 us (30%)
  waiting for transfers between devices  34.4 us (24%)
  local copies, waits for them, and re-layouts  9.33 us (6%)
  other arithmetic  2.89 us (2%)
  matrix products  2.74 us (2%)
  between operations  1.52 us (1%)
    pallas_call x3, Pallas kernels, run_stage(): pl.pallas_call(functools.partial(stage_kernel, plan, stage), out_shape=ou...  39.8 us
    ppermute x4, starting transfers between devices, sum_over(): other = lax.ppermute(mine, axis, [(k, k ^ step) for k in range(count)])  24.2 us
    ppermute x4, waiting for transfers between devices, sum_over(): other = lax.ppermute(mine, axis, [(k, k ^ step) for k in range(count)])  21.3 us
    ppermute x5, starting transfers between devices, passed_along(): lax.ppermute(value, axis, [(source, source + steps) for source in range(f...  18.5 us
    ppermute x5, waiting for transfers between devices, passed_along(): lax.ppermute(value, axis, [(source, source + steps) for source in range(f...  13.1 us
    pallas_call x2, Pallas kernels, add_chunk(): pl.pallas_call(add_kernel, grid=(tiles // wide,), out_shape=jax.ShapeDtyp...  9.54 us
    slice x2, local copies, waits for them, and re-layouts, body(): piece = source[:, :, :, start * LANES:end * LANES]  6.27 us
  transfers between devices with their start and end apart: 9, of which 6 were waited for; matrix products, arithmetic and copies ran while one was open for 6% of the time, Pallas kernels for 35%

profile of v1, /device:TPU:3, one launch (start us, length us, event | category | flops | bytes accessed | tf_op | source)
XLA Modules:
  0.0 142.9 jit_solution(853707944046082060)
XLA Ops:
  0.6 3.5 %fusion.11 = (bf16[2,2,256,640]{3,2,1,0:T(8,128)(2,1)}, bf16[2,2,256,640]{3,2,1,0:T(8,128)(2,1)}) fusion(bf16[2,2,256,2048]{3,2,1,0:T(8,128)(2,1)} %refs_9_.5), kind=kLoop, calls=%fused_computation.22 | loop fusion | bytes 5242880 | tf_op jit(solution)/shard_map/slice | solution.py:430
  4.1 2.7 %collective-permute-start.1 = (bf16[2,2,256,640]{3,2,1,0:T(8,128)(2,1)}, bf16[2,2,256,640]{3,2,1,0:T(8,128)(2,1)}, u32[]{:S(2)}, u32[]{:S(2)}) collective-permute-start(bf16[2,2,256,640]{3,2,1,0:T(8,128)(2,1)} %get-tuple-element.32), channel_id=1, source_target_pairs={{1,0},{2,1},{3,2},{4,3},{5,4},{6,5},{7,6},{8,7},{9,8},{10,9},{11,1... | collective-permute-start | bytes 3932168 | tf_op jit(solution)/shard_map/ppermute | solution.py:20
  6.9 1.9 %collective-permute-start = (bf16[2,2,256,640]{3,2,1,0:T(8,128)(2,1)}, bf16[2,2,256,640]{3,2,1,0:T(8,128)(2,1)S(1)}, u32[]{:S(2)}, u32[]{:S(2)}) collective-permute-start(bf16[2,2,256,640]{3,2,1,0:T(8,128)(2,1)} %get-tuple-element.33), channel_id=1, source_target_pairs={{1,0},{2,1},{3,2},{4,3},{5,4},{6,5},{7,6},{8,7},{9,8},{10,9},{11,1... | collective-permute-start | bytes 3932168 | tf_op jit(solution)/shard_map/ppermute | solution.py:20
  8.8 2.8 %slice.11 = bf16[2,2,256,768]{3,2,1,0:T(8,128)(2,1)} slice(bf16[2,2,256,2048]{3,2,1,0:T(8,128)(2,1)} %refs_9_.5), slice={[0:2], [0:2], [0:256], [1280:2048]} | slice | bytes 3145728 | tf_op jit(solution)/shard_map/slice | solution.py:430
  11.6 1.9 %collective-permute-start.2 = (bf16[2,2,256,768]{3,2,1,0:T(8,128)(2,1)}, bf16[2,2,256,768]{3,2,1,0:T(8,128)(2,1)}, u32[]{:S(2)}, u32[]{:S(2)}) collective-permute-start(bf16[2,2,256,768]{3,2,1,0:T(8,128)(2,1)} %slice.11), channel_id=1, source_target_pairs={{1,0},{2,1},{3,2},{4,3},{5,4},{6,5},{7,6},{8,7},{9,8},{10,9},{11,1... | collective-permute-start | bytes 4718600 | tf_op jit(solution)/shard_map/ppermute | solution.py:20
  13.5 0.7 fusion.1
  14.2 0.7 fusion.2
  14.9 0.7 fusion
  15.7 0.7 negate_convert_fusion
  16.4 0.6 copy-done.8
  17.1 0.8 maximum_maximum_fusion
  17.9 1.3 copy.18.refs_5_
  19.8 1.0 maximum_maximum_fusion.1.refs_6_
  20.8 2.8 %collective-permute-done.1.refs_10_.refs_11_ = bf16[2,2,256,640]{3,2,1,0:T(8,128)(2,1)} collective-permute-done((bf16[2,2,256,640]{3,2,1,0:T(8,128)(2,1)}, bf16[2,2,256,640]{3,2,1,0:T(8,128)(2,1)}, u32[]{:S(2)}, u32[]{:S(2)}) %collective-permute-start.1) | collective-permute-done | bytes 1310752 | tf_op jit(solution)/shard_map/ppermute | solution.py:20
  23.6 9.6 %stage0.1 = (f32[2,2,256,2048]{3,2,1,0:T(8,128)}, bf16[2,2,256,1024]{3,2,1,0:T(8,128)(2,1)}, f32[2,2,2,512,128]{4,3,2,1,0:T(8,128)}, f32[2,256,256]{2,1,0:T(8,128)S(1)}) custom-call(s32[16]{0:T(128)S(1)} %copy-done.3, s32[16]{0:T(128)S(1)} %copy-done.4, s32[1]{0:T(128)S(6)} %copy.24.refs_2_, bf16[512,512]{1,0:T(8,128)(2,1)S(1)} %copy-done.1, ...), custom_call_target="tpu_custom_call" | custom-call | flops 3000000000 | bytes 8000000 | tf_op jit(solution)/shard_map/stage0/pallas_call | solution.py:376
  33.2 4.3 %collective-permute-done.refs_10_.refs_11_ = bf16[2,2,256,640]{3,2,1,0:T(8,128)(2,1)S(1)} collective-permute-done((bf16[2,2,256,640]{3,2,1,0:T(8,128)(2,1)}, bf16[2,2,256,640]{3,2,1,0:T(8,128)(2,1)S(1)}, u32[]{:S(2)}, u32[]{:S(2)}) %collective-permute-start) | collective-permute-done | bytes 1310752 | tf_op jit(solution)/shard_map/ppermute | solution.py:20
  37.5 1.0 copy-done.7
  38.6 9.9 %stage1.1 = (f32[2,2,256,2048]{3,2,1,0:T(8,128)}, bf16[2,2,256,1024]{3,2,1,0:T(8,128)(2,1)}, f32[2,2,2,512,128]{4,3,2,1,0:T(8,128)}, f32[2,256,256]{2,1,0:T(8,128)S(1)}) custom-call(s32[16]{0:T(128)S(1)} %copy-done.3, s32[16]{0:T(128)S(1)} %copy-done.4, s32[1]{0:T(128)S(6)} %copy.24.refs_2_, ...), custom_call_target="tpu_custom_call", output_to_operand_aliasing={{0}: (14, {}), {1}: (15, {})} | custom-call | flops 3000000000 | bytes 8000000 | tf_op jit(solution)/shard_map/stage1/pallas_call | solution.py:376
  48.4 6.0 %collective-permute-done.2.refs_10_ = bf16[2,2,256,768]{3,2,1,0:T(8,128)(2,1)} collective-permute-done((bf16[2,2,256,768]{3,2,1,0:T(8,128)(2,1)}, bf16[2,2,256,768]{3,2,1,0:T(8,128)(2,1)}, u32[]{:S(2)}, u32[]{:S(2)}) %collective-permute-start.2) | collective-permute-done | bytes 1572896 | tf_op jit(solution)/shard_map/ppermute | solution.py:20
  54.5 1.9 %collective-permute-start.3 = (bf16[2,2,256,1024]{3,2,1,0:T(8,128)(2,1)}, bf16[2,2,256,1024]{3,2,1,0:T(8,128)(2,1)S(1)}, u32[]{:S(2)}, u32[]{:S(2)}) collective-permute-start(bf16[2,2,256,1024]{3,2,1,0:T(8,128)(2,1)} %get-tuple-element.27), channel_id=1, source_target_pairs={{0,1},{1,2},{2,3},{3,4},{4,5},{5,6},{6,7},{7,8},{8,9},{9,10},{10,1... | collective-permute-start | bytes 6291464 | tf_op jit(solution)/shard_map/ppermute | solution.py:20
  56.4 20.3 %stage2.1 = (f32[2,2,256,2048]{3,2,1,0:T(8,128)}, bf16[2,2,256,1024]{3,2,1,0:T(8,128)(2,1)}, f32[2,256,256]{2,1,0:T(8,128)S(1)}) custom-call(s32[16]{0:T(128)S(1)} %copy-done.3, s32[16]{0:T(128)S(1)} %copy-done.4, s32[1]{0:T(128)S(6)} %copy.24.refs_2_, bf16[512,512]{1,0:T(8,128)(2,1)S(1)} %copy-done.1, ...), custom_call_target="tpu_custom_call", output_to_operand_aliasing={{0}: (14, {})} | custom-call | flops 3000000000 | bytes 8000000 | tf_op jit(solution)/shard_map/stage2/pallas_call | solution.py:376
  76.7 10.0 %collective-permute-start.4 = (bf16[2,2,256,1024]{3,2,1,0:T(8,128)(2,1)}, bf16[2,2,256,1024]{3,2,1,0:T(8,128)(2,1)S(1)}, u32[]{:S(2)}, u32[]{:S(2)}) collective-permute-start(bf16[2,2,256,1024]{3,2,1,0:T(8,128)(2,1)} %get-tuple-element.30), channel_id=1, source_target_pairs={{0,1},{1,2},{2,3},{3,4},{4,5},{5,6},{6,7},{7,8},{8,9},{9,10},{10,1... | collective-permute-start | bytes 6291464 | tf_op jit(solution)/shard_map/ppermute | solution.py:20
  86.8 0.1 collective-permute-start.5
  86.9 1.5 %collective-permute-done.5 = bf16[2,256,256]{2,1,0:T(8,128)(2,1)S(1)} collective-permute-done((bf16[2,256,256]{2,1,0:T(8,128)(2,1)S(1)}, bf16[2,256,256]{2,1,0:T(8,128)(2,1)S(1)}, u32[]{:S(2)}, u32[]{:S(2)}) %collective-permute-start.5) | collective-permute-done | bytes 262176 | tf_op jit(solution)/shard_map/ppermute | solution.py:420
  88.5 7.6 %collective-permute-start.6 = (bf16[2,256,256]{2,1,0:T(8,128)(2,1)S(1)}, bf16[2,256,256]{2,1,0:T(8,128)(2,1)S(1)}, u32[]{:S(2)}, u32[]{:S(2)}) collective-permute-start(bf16[2,256,256]{2,1,0:T(8,128)(2,1)S(1)} %add_convert_fusion.2), channel_id=1, source_target_pairs={{0,4},{1,5},{2,6},{3,7},{4,0},{5,1},{6,2},{7,3},{8,12},{9,13},{10,... | collective-permute-start | bytes 786440 | tf_op jit(solution)/shard_map/ppermute | solution.py:420
  96.1 6.4 %collective-permute-done.6 = bf16[2,256,256]{2,1,0:T(8,128)(2,1)S(1)} collective-permute-done((bf16[2,256,256]{2,1,0:T(8,128)(2,1)S(1)}, bf16[2,256,256]{2,1,0:T(8,128)(2,1)S(1)}, u32[]{:S(2)}, u32[]{:S(2)}) %collective-permute-start.6) | collective-permute-done | bytes 262176 | tf_op jit(solution)/shard_map/ppermute | solution.py:420
  102.5 0.5 collective-permute-start.7
  103.1 13.4 %collective-permute-done.7 = bf16[2,256,256]{2,1,0:T(8,128)(2,1)S(1)} collective-permute-done((bf16[2,256,256]{2,1,0:T(8,128)(2,1)S(1)}, bf16[2,256,256]{2,1,0:T(8,128)(2,1)S(1)}, u32[]{:S(2)}, u32[]{:S(2)}) %collective-permute-start.7) | collective-permute-done | bytes 262176 | tf_op jit(solution)/shard_map/ppermute | solution.py:420
  116.5 16.0 %collective-permute-start.8 = (bf16[2,256,256]{2,1,0:T(8,128)(2,1)S(1)}, bf16[2,256,256]{2,1,0:T(8,128)(2,1)S(1)}, u32[]{:S(2)}, u32[]{:S(2)}) collective-permute-start(bf16[2,256,256]{2,1,0:T(8,128)(2,1)S(1)} %add_convert_fusion), channel_id=1, source_target_pairs={{0,2},{1,3},{2,0},{3,1},{4,6},{5,7},{6,4},{7,5},{8,10},{9,11},{10,... | collective-permute-start | bytes 786440 | tf_op jit(solution)/shard_map/ppermute | solution.py:420
  132.5 4.8 %add0.1.held_ref = f32[2,2,256,2048]{3,2,1,0:T(8,128)} custom-call(f32[2,2,256,2048]{3,2,1,0:T(8,128)} %get-tuple-element.26.held_ref, bf16[2,2,256,1024]{3,2,1,0:T(8,128)(2,1)S(1)} %collective-permute-done.3.came_ref), custom_call_target="tpu_custom_call", output_to_operand_aliasing={{}: (0, {})} | custom-call | tf_op jit(solution)/shard_map/add0/pallas_call | solution.py:403
  137.3 4.8 %add8.1 = f32[2,2,256,2048]{3,2,1,0:T(8,128)} custom-call(f32[2,2,256,2048]{3,2,1,0:T(8,128)} %add0.1.held_ref, bf16[2,2,256,1024]{3,2,1,0:T(8,128)(2,1)S(1)} %collective-permute-done.4.came_ref), custom_call_target="tpu_custom_call", output_to_operand_aliasing={{}: (0, {})} | custom-call | tf_op jit(solution)/shard_map/add8/pallas_call | solution.py:403
  142.1 0.8 convert_add_fusion
  (28 shorter events, 0.3 us)
Async XLA Ops:
  4.1 9.4 %copy-start.10 = (f32[256]{0:T(256)S(1)}, f32[256]{0:T(256)}, u32[]{:S(2)}) copy-start(f32[256]{0:T(256)} %param.11) | copy-start | bytes 3076
  4.1 9.4 %copy-start.5 = (f32[256,256]{1,0:T(8,128)S(1)}, f32[256,256]{1,0:T(8,128)}, u32[]{:S(2)}) copy-start(f32[256,256]{1,0:T(8,128)} %constant.4.clone) | copy-start | bytes 786436
  4.1 9.4 %copy-start.6 = (f32[256,256]{1,0:T(8,128)S(1)}, f32[256,256]{1,0:T(8,128)}, u32[]{:S(2)}) copy-start(f32[256,256]{1,0:T(8,128)} %constant.5.clone) | copy-start | bytes 786436
  4.1 19.4 %collective-permute-start.1 = (bf16[2,2,256,640]{3,2,1,0:T(8,128)(2,1)}, bf16[2,2,256,640]{3,2,1,0:T(8,128)(2,1)}, u32[]{:S(2)}, u32[]{:S(2)}) collective-permute-start(bf16[2,2,256,640]{3,2,1,0:T(8,128)(2,1)} %get-tuple-element.32), channel_id=1, source_target_pairs={{1,0},{2,1},{3,2},{4,3},{5,4},{6,5},{7,6},{8,7},{9,8},{10,9},{11,1... | collective-permute-start | bytes 3932168 | tf_op jit(solution)/shard_map/ppermute | solution.py:20
  6.9 30.7 %collective-permute-start = (bf16[2,2,256,640]{3,2,1,0:T(8,128)(2,1)}, bf16[2,2,256,640]{3,2,1,0:T(8,128)(2,1)S(1)}, u32[]{:S(2)}, u32[]{:S(2)}) collective-permute-start(bf16[2,2,256,640]{3,2,1,0:T(8,128)(2,1)} %get-tuple-element.33), channel_id=1, source_target_pairs={{1,0},{2,1},{3,2},{4,3},{5,4},{6,5},{7,6},{8,7},{9,8},{10,9},{11,1... | collective-permute-start | bytes 3932168 | tf_op jit(solution)/shard_map/ppermute | solution.py:20
  11.6 42.9 %collective-permute-start.2 = (bf16[2,2,256,768]{3,2,1,0:T(8,128)(2,1)}, bf16[2,2,256,768]{3,2,1,0:T(8,128)(2,1)}, u32[]{:S(2)}, u32[]{:S(2)}) collective-permute-start(bf16[2,2,256,768]{3,2,1,0:T(8,128)(2,1)} %slice.11), channel_id=1, source_target_pairs={{1,0},{2,1},{3,2},{4,3},{5,4},{6,5},{7,6},{8,7},{9,8},{10,9},{11,1... | collective-permute-start | bytes 4718600 | tf_op jit(solution)/shard_map/ppermute | solution.py:20
  15.6 8.0 %copy-start = (f32[2,256,256]{2,1,0:T(8,128)S(1)}, f32[2,256,256]{2,1,0:T(8,128)}, u32[]{:S(2)}) copy-start(f32[2,256,256]{2,1,0:T(8,128)} %refs_7_.5) | copy-start | bytes 1572868
  15.6 7.9 %copy-start.1 = (bf16[512,512]{1,0:T(8,128)(2,1)S(1)}, bf16[512,512]{1,0:T(8,128)(2,1)}, u32[]{:S(2)}) copy-start(bf16[512,512]{1,0:T(8,128)(2,1)} %constant.16.refs_3_) | copy-start | bytes 1572868
  15.6 7.9 %copy-start.2 = (bf16[512,512]{1,0:T(8,128)(2,1)S(1)}, bf16[512,512]{1,0:T(8,128)(2,1)}, u32[]{:S(2)}) copy-start(bf16[512,512]{1,0:T(8,128)(2,1)} %constant.19.refs_4_) | copy-start | bytes 1572868
  15.7 7.9 %copy-start.3 = (s32[16]{0:T(128)S(1)}, s32[16]{0:T(128)}, u32[]{:S(2)}) copy-start(s32[16]{0:T(128)} %refs_0_.5) | copy-start | bytes 196
  15.7 7.9 %copy-start.4 = (s32[16]{0:T(128)S(1)}, s32[16]{0:T(128)}, u32[]{:S(2)}) copy-start(s32[16]{0:T(128)} %refs_1_.5) | copy-start | bytes 196
  16.4 0.7 copy-start.8
  16.4 0.7 copy-start.9
  37.5 1.0 copy-start.7
  54.5 32.3 %collective-permute-start.3 = (bf16[2,2,256,1024]{3,2,1,0:T(8,128)(2,1)}, bf16[2,2,256,1024]{3,2,1,0:T(8,128)(2,1)S(1)}, u32[]{:S(2)}, u32[]{:S(2)}) collective-permute-start(bf16[2,2,256,1024]{3,2,1,0:T(8,128)(2,1)} %get-tuple-element.27), channel_id=1, source_target_pairs={{0,1},{1,2},{2,3},{3,4},{4,5},{5,6},{6,7},{7,8},{8,9},{9,10},{10,1... | collective-permute-start | bytes 6291464 | tf_op jit(solution)/shard_map/ppermute | solution.py:20
  76.7 60.6 %collective-permute-start.4 = (bf16[2,2,256,1024]{3,2,1,0:T(8,128)(2,1)}, bf16[2,2,256,1024]{3,2,1,0:T(8,128)(2,1)S(1)}, u32[]{:S(2)}, u32[]{:S(2)}) collective-permute-start(bf16[2,2,256,1024]{3,2,1,0:T(8,128)(2,1)} %get-tuple-element.30), channel_id=1, source_target_pairs={{0,1},{1,2},{2,3},{3,4},{4,5},{5,6},{6,7},{7,8},{8,9},{9,10},{10,1... | collective-permute-start | bytes 6291464 | tf_op jit(solution)/shard_map/ppermute | solution.py:20
  86.8 1.6 %collective-permute-start.5 = (bf16[2,256,256]{2,1,0:T(8,128)(2,1)S(1)}, bf16[2,256,256]{2,1,0:T(8,128)(2,1)S(1)}, u32[]{:S(2)}, u32[]{:S(2)}) collective-permute-start(bf16[2,256,256]{2,1,0:T(8,128)(2,1)S(1)} %convert_element_type.40), channel_id=1, source_target_pairs={{0,1},{1,0},{2,3},{3,2},{4,5},{5,4},{6,7},{7,6},{8,9},{9,8},{10,11... | collective-permute-start | bytes 786440 | tf_op jit(solution)/shard_map/ppermute | solution.py:420
  88.5 14.0 %collective-permute-start.6 = (bf16[2,256,256]{2,1,0:T(8,128)(2,1)S(1)}, bf16[2,256,256]{2,1,0:T(8,128)(2,1)S(1)}, u32[]{:S(2)}, u32[]{:S(2)}) collective-permute-start(bf16[2,256,256]{2,1,0:T(8,128)(2,1)S(1)} %add_convert_fusion.2), channel_id=1, source_target_pairs={{0,4},{1,5},{2,6},{3,7},{4,0},{5,1},{6,2},{7,3},{8,12},{9,13},{10,... | collective-permute-start | bytes 786440 | tf_op jit(solution)/shard_map/ppermute | solution.py:420
  102.5 13.9 %collective-permute-start.7 = (bf16[2,256,256]{2,1,0:T(8,128)(2,1)S(1)}, bf16[2,256,256]{2,1,0:T(8,128)(2,1)S(1)}, u32[]{:S(2)}, u32[]{:S(2)}) collective-permute-start(bf16[2,256,256]{2,1,0:T(8,128)(2,1)S(1)} %add_convert_fusion.1), channel_id=1, source_target_pairs={{0,8},{1,9},{2,10},{3,11},{4,12},{5,13},{6,14},{7,15},{8,0},{9,1},... | collective-permute-start | bytes 786440 | tf_op jit(solution)/shard_map/ppermute | solution.py:420
  116.5 25.6 %collective-permute-start.8 = (bf16[2,256,256]{2,1,0:T(8,128)(2,1)S(1)}, bf16[2,256,256]{2,1,0:T(8,128)(2,1)S(1)}, u32[]{:S(2)}, u32[]{:S(2)}) collective-permute-start(bf16[2,256,256]{2,1,0:T(8,128)(2,1)S(1)} %add_convert_fusion), channel_id=1, source_target_pairs={{0,2},{1,3},{2,0},{3,1},{4,6},{5,7},{6,4},{7,5},{8,10},{9,11},{10,... | collective-permute-start | bytes 786440 | tf_op jit(solution)/shard_map/ppermute | solution.py:420

commit v2 on v1

--- a/solution.py
+++ b/solution.py
@@ -54,11 +54,6 @@
     return jnp.dot(left, right, preferred_element_type=F32)
 
 
-def beside(stacked):
-    half = stacked.shape[0] // 2
-    return jnp.concatenate([stacked[:half], stacked[half:]], axis=1).astype(BF)
-
-
 def stage_kernel(
     plan, stage, *refs
 ):
@@ -66,7 +61,7 @@
     refs = list(refs)
     row_ref, col_ref, count_ref = refs[:3]
     del refs[:3]
-    four_ref, conj_ref, prop_ref, back_ref = refs[:4]
+    tables_hbm = refs[:4]
     del refs[:4]
     probe_ref, intensity_ref, specimen_ref = refs[:3]
     del refs[:3]
@@ -81,7 +76,9 @@
     carry_out = None if is_last else refs.pop(0)
     probe_out = refs.pop(0)
     (slots_ref, ext_ref, acc_ref, measured_ref, round_ref, twice_ref, sum_ref, win_ref, wave0_ref, wave1_ref,
-     stack_ref, half_ref, tile_ref, load_sem, slot_sem, store_sem) = refs
+     stack_ref, half_ref, tile_ref, tables_ref,
+     load_sem, slot_sem, store_sem, table_sem) = refs
+    four_ref, conj_ref, prop_ref, back_ref = (tables_ref.at[k] for k in range(4))
     extent = probe_ref.shape[1]
     tiles = end_tile - first_tile
     past_tiles = halo_start - first_tile
@@ -100,6 +97,8 @@
             source = halo_now.at[:, :, :, pl.ds((j - past_tiles) * LANES, LANES)]
         copies.append(pltpu.make_async_copy(
             source, ext_ref.at[:, :, j, pl.ds(extent, extent), :], load_sem.at[2 * j + 1]))
+    for k in range(4):
+        copies.append(pltpu.make_async_copy(tables_hbm[k], tables_ref.at[k], table_sem.at[k]))
     for copy in copies:
         copy.start()
     carried = None
@@ -167,23 +166,22 @@
             own = lax.broadcasted_iota(jnp.int32, (16, LANES), 0) + mixed >= r
             return mixed, low, own
 
-        def take_window(g):
+        def take_window(g, s):
             r, shift, ats = places[g]
             at0, at1, at2 = ats
             mixed, low, own = masks(r, shift)
             row_at = row_starts(r)
             for part in range(2):
-                for s in range(2):
-                    for t, at in zip(range(0, extent, 16), row_at):
-                        rows = pl.ds(at, 16)
-                        win_ref[g, part, s, t:t + 16, 0:LANES] = jnp.where(
-                            low, ext_ref[part, s, at2, rows, :], ext_ref[part, s, at0, rows, :])
-                        win_ref[g, part, s, t:t + 16, LANES:2 * LANES] = ext_ref[part, s, at1, rows, :]
-                    rows, rows_under = pl.ds(mixed, 16), pl.ds(pl.multiple_of(mixed + extent, 16), 16)
-                    picked = [jnp.where(own, ext_ref[part, s, at, rows, :], ext_ref[part, s, at, rows_under, :])
-                              for at in ats]
-                    win_ref[g, part, s, rows, 0:LANES] = jnp.where(low, picked[2], picked[0])
-                    win_ref[g, part, s, rows, LANES:2 * LANES] = picked[1]
+                for t, at in zip(range(0, extent, 16), row_at):
+                    rows = pl.ds(at, 16)
+                    win_ref[g, part, s, t:t + 16, 0:LANES] = jnp.where(
+                        low, ext_ref[part, s, at2, rows, :], ext_ref[part, s, at0, rows, :])
+                    win_ref[g, part, s, t:t + 16, LANES:2 * LANES] = ext_ref[part, s, at1, rows, :]
+                rows, rows_under = pl.ds(mixed, 16), pl.ds(pl.multiple_of(mixed + extent, 16), 16)
+                picked = [jnp.where(own, ext_ref[part, s, at, rows, :], ext_ref[part, s, at, rows_under, :])
+                          for at in ats]
+                win_ref[g, part, s, rows, 0:LANES] = jnp.where(low, picked[2], picked[0])
+                win_ref[g, part, s, rows, LANES:2 * LANES] = picked[1]
 
         def take_probe(g):
             r, shift, _ = places[g]
@@ -213,11 +211,14 @@
             spec_im = win_ref[g, 1, s].astype(F32)
             return spec_re * grad_re + spec_im * grad_im, spec_re * grad_im - spec_im * grad_re
 
-        def transform(left_ref, right_ref):
+        def transform(left_ref, right_ref, beside=None):
+            wide = product(left_ref[...], stack_ref[:, 0:many * extent])
             for g in every:
-                half = product(left_ref[...], stack_ref[:, g * extent:(g + 1) * extent])
+                half = wide[:, g * extent:(g + 1) * extent]
                 half_ref[g * extent:(g + 1) * extent, 0:extent] = half[:extent].astype(BF)
                 half_ref[g * extent:(g + 1) * extent, extent:2 * extent] = half[extent:].astype(BF)
+                if beside is not None:
+                    beside(g)
             whole = product(half_ref[0:many * extent], right_ref[...])
             return [(whole[g * extent:(g + 1) * extent, :extent], whole[g * extent:(g + 1) * extent, extent:])
                     for g in every]
@@ -257,10 +258,10 @@
                              tile_ref[g, part, s, t:t + 16, LANES:2 * LANES].astype(F32))
 
         for g in every:
-            take_window(g)
+            take_window(g, 0)
             take_probe(g)
             leave(wave0_ref, 0, g)
-        for g, (re, im) in enumerate(transform(prop_ref, back_ref)):
+        for g, (re, im) in enumerate(transform(prop_ref, back_ref, lambda g: take_window(g, 1))):
             wave1_ref[g, 0] = re
             wave1_ref[g, 1] = im
             leave(wave1_ref, 1, g)
@@ -272,12 +273,11 @@
             put(g, residual * re, residual * im)
         for g, (re, im) in enumerate(transform(conj_ref, four_ref)):
             put(g, *return_through(wave1_ref, 1, g, re, im))
-        grads = transform(back_ref, prop_ref)
+        grads = transform(back_ref, prop_ref, lambda g: give_tile(g, 1))
         for g, (re, im) in enumerate(grads):
             give_probe(g, return_through(wave0_ref, 0, g, re, im))
         for g in every:
-            for s in range(2):
-                give_tile(g, s)
+            give_tile(g, 0)
 
     def visit_pair(p, unused):
         fetch_pair(2 * p + 2)
@@ -333,7 +333,7 @@
     vmem = pl.BlockSpec(memory_space=pltpu.VMEM)
     hbm = pl.BlockSpec(memory_space=pl.ANY)
     args = [*meta, *tables, probe_field, intensity, specimen, halos[stage]]
-    in_specs = [smem] * 3 + [vmem] * 4 + [vmem, hbm, hbm, hbm]
+    in_specs = [smem] * 3 + [hbm] * 4 + [vmem, hbm, hbm, hbm]
     aliases = {}
     if has_past:
         interior, carry, probe_sum = past
@@ -369,9 +369,11 @@
         pltpu.VMEM((2 * extent, 2 * extent), BF),
         pltpu.VMEM((2 * extent, 2 * extent), BF),
         pltpu.VMEM((2, *pairs, extent, extent), BF),
+        pltpu.VMEM((4, 2 * extent, 2 * extent), BF),
         pltpu.SemaphoreType.DMA((2 * tiles,)),
         pltpu.SemaphoreType.DMA((4,)),
         pltpu.SemaphoreType.DMA((1,)),
+        pltpu.SemaphoreType.DMA((4,)),
     ]
     results = list(pl.pallas_call(
         functools.partial(stage_kernel, plan, stage),
@@ -380,7 +382,7 @@
         out_specs=out_specs,
         scratch_shapes=scratch,
         input_output_aliases=aliases,
-        compiler_params=pltpu.CompilerParams(vmem_limit_bytes=50 * 1024 * 1024),
+        compiler_params=pltpu.CompilerParams(vmem_limit_bytes=56 * 1024 * 1024),
         cost_estimate=pl.CostEstimate(flops=3 * 10**9, bytes_accessed=8 * 10**6, transcendentals=0),
         name=f"stage{stage}",
     )(*args))
@@ -390,36 +392,66 @@
     return (interior, carry, results.pop(0)), (group_tile, group_end, overflow)
 
 
-def add_kernel(held_ref, came_ref, out_ref):
-    out_ref[...] = held_ref[...] + came_ref[...].astype(F32)
+def add_kernel(first_tile, tiles, held_ref, came_ref, out_ref, held, came, in_sem, out_sem):
+    def copies(j):
+        lanes = pl.ds((first_tile + j) * LANES, LANES)
+        return (
+            pltpu.make_async_copy(held_ref.at[:, :, :, lanes], held.at[j], in_sem.at[2 * j]),
+            pltpu.make_async_copy(came_ref.at[:, :, :, pl.ds(j * LANES, LANES)], came.at[j], in_sem.at[2 * j + 1]),
+            pltpu.make_async_copy(held.at[j], out_ref.at[:, :, :, lanes], out_sem.at[j]),
+        )
+
+    for j in range(tiles):
+        for copy in copies(j)[:2]:
+            copy.start()
+    for j in range(tiles):
+        for copy in copies(j)[:2]:
+            copy.wait()
+        held[j] = held[j] + came[j].astype(F32)
+        copies(j)[2].start()
+    for j in range(tiles):
+        copies(j)[2].wait()
 
 
 def add_chunk(interior, came, first_tile):
-    _, slices, rows, columns = interior.shape
+    _, slices, rows, _ = interior.shape
     tiles = came.shape[3] // LANES
-    wide = 2 if tiles % 2 == 0 and first_tile % 2 == 0 else 1
-    block = (2, slices, rows, wide * LANES)
-    place = pl.BlockSpec(block, lambda j: (0, 0, 0, first_tile // wide + j))
+    hbm = pl.BlockSpec(memory_space=pl.ANY)
+    block = (tiles, 2, slices, rows, LANES)
     return pl.pallas_call(
-        add_kernel,
-        grid=(tiles // wide,),
+        functools.partial(add_kernel, first_tile, tiles),
         out_shape=jax.ShapeDtypeStruct(interior.shape, interior.dtype),
-        in_specs=[place, pl.BlockSpec(block, lambda j: (0, 0, 0, j))],
-        out_specs=place,
+        in_specs=[hbm, hbm],
+        out_specs=hbm,
+        scratch_shapes=[
+            pltpu.VMEM(block, F32),
+            pltpu.VMEM(block, BF),
+            pltpu.SemaphoreType.DMA((2 * tiles,)),
+            pltpu.SemaphoreType.DMA((tiles,)),
+        ],
         input_output_aliases={0: 0},
-        compiler_params=pltpu.CompilerParams(vmem_limit_bytes=32 * 1024 * 1024),
+        compiler_params=pltpu.CompilerParams(vmem_limit_bytes=56 * 1024 * 1024),
         name=f"add{first_tile}",
     )(interior, came)
 
 
-def sum_over(value, axis):
+def exchanged(value, axis, step):
+    return lax.ppermute(value, axis, [(k, k ^ step) for k in range(lax.axis_size(axis))])
+
+
+def sum_over(value, axis, meanwhile):
     count = lax.axis_size(axis)
-    steps = [1 << k for k in range(count.bit_length() - 1)]
-    for step in steps[:1] + steps[2:] + steps[1:2]:
-        mine = value.astype(BF)
-        other = lax.ppermute(mine, axis, [(k, k ^ step) for k in range(count)])
-        value = mine.astype(F32) + other.astype(F32)
-    return value
+    steps = [1 << k for k in range(1, count.bit_length() - 1)]
+    odd = lax.rem(lax.axis_index(axis), 2) == 1
+    kept, given = jnp.where(odd, value[1], value[0]), jnp.where(odd, value[0], value[1])
+    kept = kept.astype(BF).astype(F32) + exchanged(given.astype(BF), axis, 1).astype(F32)
+    for n, step in enumerate(steps[1:] + steps[:1]):
+        mine = kept.astype(BF)
+        kept = mine.astype(F32) + exchanged(mine, axis, step).astype(F32)
+        if n == len(steps) - 1:
+            kept = meanwhile(kept)
+    other = exchanged(kept, axis, 1)
+    return jnp.stack([jnp.where(odd, other, kept), jnp.where(odd, kept, other)])
 
 
 def body(ends, sends, specimen, probe_field, transfer_phase, intensity, row_offset, col_offset, counts):
@@ -446,18 +478,20 @@
             came.append((passed_along(group[2], "row", 1), group[0]))
             at = group[1]
     interior, _, probe_sum = past
-    early = came[0][0]
-    early, probe_sum = lax.optimization_barrier((early, probe_sum))
-    came[0] = (early, came[0][1])
-    probe_total = sum_over(probe_sum, "row")
-    for chunk, first in came:
-        interior = add_chunk(interior, chunk, first)
+    held = [interior]
+
+    def meanwhile(kept):
+        kept, held[0] = lax.optimization_barrier((kept, add_chunk(held[0], *came[0])))
+        return kept
+
+    probe_total = sum_over(probe_sum, "row", meanwhile)
+    interior = add_chunk(held[0], *came[1])
     return interior, probe_total
 
 
 def solution(mesh):
     return jax.shard_map(
-        functools.partial(body, (5, 10, 16), (1, 2)),
+        functools.partial(body, (5, 10, 13, 16), (2, 3)),
         mesh=mesh,
         in_specs=(
             P("group", None, "row", None),

time: 144 us -> 154 us (1.069)
  the two profiles are of different devices: /device:TPU:3 before, /device:TPU:21 now
where the time goes in v2:
time: 154 us; the launch traced here: 155 us
  Pallas kernels  73.1 us (47%)
  waiting for transfers between devices  33.5 us (22%)
  starting transfers between devices  28.4 us (18%)
  local copies, waits for them, and re-layouts  12.1 us (8%)
  other arithmetic  3.97 us (3%)
  matrix products  2.75 us (2%)
  between operations  1.58 us (1%)
    pallas_call x4, Pallas kernels, run_stage(): pl.pallas_call(functools.partial(stage_kernel, plan, stage), out_shape=ou...  63.4 us
    ppermute x5, waiting for transfers between devices, exchanged(): lax.ppermute(value, axis, [(k, k ^ step) for k in range(lax.axis_size(axi...  31.2 us
    ppermute x6, starting transfers between devices, passed_along(): lax.ppermute(value, axis, [(source, source + steps) for source in range(f...  16.4 us
    ppermute x5, starting transfers between devices, exchanged(): lax.ppermute(value, axis, [(k, k ^ step) for k in range(lax.axis_size(axi...  12 us
    pallas_call x2, Pallas kernels, add_chunk(): pl.pallas_call(functools.partial(add_kernel, first_tile, tiles), out_shap...  9.73 us
    slice x2, local copies, waits for them, and re-layouts, body(): piece = source[:, :, :, start * LANES:end * LANES]  6.25 us
    unnamed x14, local copies, waits for them, and re-layouts  4.75 us
  transfers between devices with their start and end apart: 11, of which 5 were waited for; matrix products, arithmetic and copies ran while one was open for 6% of the time, Pallas kernels for 47%

profile of v2, /device:TPU:21, one launch (start us, length us, event | category | flops | bytes accessed | tf_op | source)
XLA Modules:
  0.0 155.4 jit_solution(17880978009902089393)
XLA Ops:
  0.6 3.6 %fusion.15 = (bf16[2,2,256,640]{3,2,1,0:T(8,128)(2,1)}, bf16[2,2,256,640]{3,2,1,0:T(8,128)(2,1)}) fusion(bf16[2,2,256,2048]{3,2,1,0:T(8,128)(2,1)} %refs_9_.7), kind=kLoop, calls=%fused_computation.31 | loop fusion | bytes 5242880 | tf_op jit(solution)/shard_map/slice | solution.py:462
  4.2 2.7 %collective-permute-start.2 = (bf16[2,2,256,640]{3,2,1,0:T(8,128)(2,1)}, bf16[2,2,256,640]{3,2,1,0:T(8,128)(2,1)}, u32[]{:S(2)}, u32[]{:S(2)}) collective-permute-start(bf16[2,2,256,640]{3,2,1,0:T(8,128)(2,1)} %get-tuple-element.42), channel_id=1, source_target_pairs={{1,0},{2,1},{3,2},{4,3},{5,4},{6,5},{7,6},{8,7},{9,8},{10,9},{11,1... | collective-permute-start | bytes 3932168 | tf_op jit(solution)/shard_map/ppermute | solution.py:20
  6.9 1.9 %collective-permute-start.1 = (bf16[2,2,256,640]{3,2,1,0:T(8,128)(2,1)}, bf16[2,2,256,640]{3,2,1,0:T(8,128)(2,1)S(1)}, u32[]{:S(2)}, u32[]{:S(2)}) collective-permute-start(bf16[2,2,256,640]{3,2,1,0:T(8,128)(2,1)} %get-tuple-element.43), channel_id=1, source_target_pairs={{1,0},{2,1},{3,2},{4,3},{5,4},{6,5},{7,6},{8,7},{9,8},{10,9},{11,1... | collective-permute-start | bytes 3932168 | tf_op jit(solution)/shard_map/ppermute | solution.py:20
  8.9 2.7 %fusion.14 = (bf16[2,2,256,384]{3,2,1,0:T(8,128)(2,1)}, bf16[2,2,256,384]{3,2,1,0:T(8,128)(2,1)}) fusion(bf16[2,2,256,2048]{3,2,1,0:T(8,128)(2,1)} %refs_9_.7), kind=kLoop, calls=%fused_computation.30 | loop fusion | bytes 3145728 | tf_op jit(solution)/shard_map/slice | solution.py:462
  11.5 2.5 %collective-permute-start = (bf16[2,2,256,384]{3,2,1,0:T(8,128)(2,1)}, bf16[2,2,256,384]{3,2,1,0:T(8,128)(2,1)S(1)}, u32[]{:S(2)}, u32[]{:S(2)}) collective-permute-start(bf16[2,2,256,384]{3,2,1,0:T(8,128)(2,1)} %get-tuple-element.41), channel_id=1, source_target_pairs={{1,0},{2,1},{3,2},{4,3},{5,4},{6,5},{7,6},{8,7},{9,8},{10,9},{11,1... | collective-permute-start | bytes 2359304 | tf_op jit(solution)/shard_map/ppermute | solution.py:20
  14.0 2.8 %collective-permute-start.3 = (bf16[2,2,256,384]{3,2,1,0:T(8,128)(2,1)}, bf16[2,2,256,384]{3,2,1,0:T(8,128)(2,1)}, u32[]{:S(2)}, u32[]{:S(2)}) collective-permute-start(bf16[2,2,256,384]{3,2,1,0:T(8,128)(2,1)} %get-tuple-element.40), channel_id=1, source_target_pairs={{1,0},{2,1},{3,2},{4,3},{5,4},{6,5},{7,6},{8,7},{9,8},{10,9},{11,1... | collective-permute-start | bytes 2359304 | tf_op jit(solution)/shard_map/ppermute | solution.py:20
  16.9 0.7 fusion.2
  18.3 0.7 fusion
  19.0 0.7 negate_convert_fusion
  19.7 1.0 copy.21.refs_5_
  21.4 0.8 maximum_maximum_fusion.1.refs_6_
  22.2 2.3 %collective-permute-done.2.refs_10_.refs_11_ = bf16[2,2,256,640]{3,2,1,0:T(8,128)(2,1)} collective-permute-done((bf16[2,2,256,640]{3,2,1,0:T(8,128)(2,1)}, bf16[2,2,256,640]{3,2,1,0:T(8,128)(2,1)}, u32[]{:S(2)}, u32[]{:S(2)}) %collective-permute-start.2) | collective-permute-done | bytes 1310752 | tf_op jit(solution)/shard_map/ppermute | solution.py:20
  24.5 15.7 %stage0.1 = (f32[2,2,256,2048]{3,2,1,0:T(8,128)}, bf16[2,2,256,1408]{3,2,1,0:T(8,128)(2,1)}, f32[2,2,2,512,128]{4,3,2,1,0:T(8,128)}, f32[2,256,256]{2,1,0:T(8,128)}) custom-call(s32[16]{0:T(128)} %refs_0_.7, s32[16]{0:T(128)} %refs_1_.7, s32[1]{0:T(128)S(6)} %copy.29.refs_2_, bf16[512,512]{1,0:T(8,128)(2,1)} %constant.26.refs_3_, ...), custom_call_target="tpu_custom_call" | custom-call | flops 3000000000 | bytes 8000000 | tf_op jit(solution)/shard_map/stage0/pallas_call | solution.py:378
  40.2 1.2 copy-done.2
  41.4 16.5 %stage1.1 = (f32[2,2,256,2048]{3,2,1,0:T(8,128)}, bf16[2,2,256,1408]{3,2,1,0:T(8,128)(2,1)}, f32[2,2,2,512,128]{4,3,2,1,0:T(8,128)}, f32[2,256,256]{2,1,0:T(8,128)}) custom-call(s32[16]{0:T(128)} %refs_0_.7, s32[16]{0:T(128)} %refs_1_.7, s32[1]{0:T(128)S(6)} %copy.29.refs_2_, ...), custom_call_target="tpu_custom_call", output_to_operand_aliasing={{0}: (14, {}), {1}: (15, {})} | custom-call | flops 3000000000 | bytes 8000000 | tf_op jit(solution)/shard_map/stage1/pallas_call | solution.py:378
  57.9 1.0 copy-done.3
  58.9 15.8 %stage2.1 = (f32[2,2,256,2048]{3,2,1,0:T(8,128)}, bf16[2,2,256,1408]{3,2,1,0:T(8,128)(2,1)}, f32[2,2,2,512,128]{4,3,2,1,0:T(8,128)}, f32[2,256,256]{2,1,0:T(8,128)}) custom-call(s32[16]{0:T(128)} %refs_0_.7, s32[16]{0:T(128)} %refs_1_.7, s32[1]{0:T(128)S(6)} %copy.29.refs_2_, ...), custom_call_target="tpu_custom_call", output_to_operand_aliasing={{0}: (14, {}), {1}: (15, {})} | custom-call | flops 3000000000 | bytes 8000000 | tf_op jit(solution)/shard_map/stage2/pallas_call | solution.py:378
  74.7 1.9 %collective-permute-start.8 = (bf16[2,2,256,1408]{3,2,1,0:T(8,128)(2,1)}, bf16[2,2,256,1408]{3,2,1,0:T(8,128)(2,1)S(1)}, u32[]{:S(2)}, u32[]{:S(2)}) collective-permute-start(bf16[2,2,256,1408]{3,2,1,0:T(8,128)(2,1)} %get-tuple-element.36), channel_id=1, source_target_pairs={{0,1},{1,2},{2,3},{3,4},{4,5},{5,6},{6,7},{7,8},{8,9},{9,10},{10,1... | collective-permute-start | bytes 8650760 | tf_op jit(solution)/shard_map/ppermute | solution.py:20
  76.6 15.4 %stage3.1 = (f32[2,2,256,2048]{3,2,1,0:T(8,128)}, bf16[2,2,256,640]{3,2,1,0:T(8,128)(2,1)}, f32[2,256,256]{2,1,0:T(8,128)}) custom-call(s32[16]{0:T(128)} %refs_0_.7, s32[16]{0:T(128)} %refs_1_.7, s32[1]{0:T(128)S(6)} %copy.29.refs_2_, bf16[512,512]{1,0:T(8,128)(2,1)} %constant.26.refs_3_, ...), custom_call_target="tpu_custom_call", output_to_operand_aliasing={{0}: (14, {})} | custom-call | flops 3000000000 | bytes 8000000 | tf_op jit(solution)/shard_map/stage3/pallas_call | solution.py:378
  92.0 1.1 fusion.5
  93.7 1.0 collective-permute-done.4
  94.7 1.1 fusion.1
  95.8 4.6 %collective-permute-start.9 = (bf16[2,2,256,640]{3,2,1,0:T(8,128)(2,1)}, bf16[2,2,256,640]{3,2,1,0:T(8,128)(2,1)S(1)}, u32[]{:S(2)}, u32[]{:S(2)}) collective-permute-start(bf16[2,2,256,640]{3,2,1,0:T(8,128)(2,1)} %get-tuple-element.38), channel_id=1, source_target_pairs={{0,1},{1,2},{2,3},{3,4},{4,5},{5,6},{6,7},{7,8},{8,9},{9,10},{10,1... | collective-permute-start | bytes 3932168 | tf_op jit(solution)/shard_map/ppermute | solution.py:20
  100.4 10.6 %collective-permute-done.5 = bf16[256,256]{1,0:T(8,128)(2,1)S(1)} collective-permute-done((bf16[256,256]{1,0:T(8,128)(2,1)S(1)}, bf16[256,256]{1,0:T(8,128)(2,1)S(1)}, u32[]{:S(2)}, u32[]{:S(2)}) %collective-permute-start.5) | collective-permute-done | bytes 131104 | tf_op jit(solution)/shard_map/ppermute | solution.py:439
  111.0 11.2 %collective-permute-start.6 = (bf16[256,256]{1,0:T(8,128)(2,1)S(1)}, bf16[256,256]{1,0:T(8,128)(2,1)S(1)}, u32[]{:S(2)}, u32[]{:S(2)}) collective-permute-start(bf16[256,256]{1,0:T(8,128)(2,1)S(1)} %add_convert_fusion.1), channel_id=1, source_target_pairs={{0,8},{1,9},{2,10},{3,11},{4,12},{5,13},{6,14},{7,15},{8,0},{9,1},... | collective-permute-start | bytes 393224 | tf_op jit(solution)/shard_map/ppermute | solution.py:439
  122.3 15.8 %collective-permute-done.6 = bf16[256,256]{1,0:T(8,128)(2,1)S(1)} collective-permute-done((bf16[256,256]{1,0:T(8,128)(2,1)S(1)}, bf16[256,256]{1,0:T(8,128)(2,1)S(1)}, u32[]{:S(2)}, u32[]{:S(2)}) %collective-permute-start.6) | collective-permute-done | bytes 131104 | tf_op jit(solution)/shard_map/ppermute | solution.py:439
  138.2 3.8 %collective-permute-done.7 = bf16[256,256]{1,0:T(8,128)(2,1)S(1)} collective-permute-done((bf16[256,256]{1,0:T(8,128)(2,1)S(1)}, bf16[256,256]{1,0:T(8,128)(2,1)S(1)}, u32[]{:S(2)}, u32[]{:S(2)}) %collective-permute-start.7) | collective-permute-done | bytes 131104 | tf_op jit(solution)/shard_map/ppermute | solution.py:439
  142.1 1.5 copy-done.4
  143.6 6.4 %add0.1.held_ref = f32[2,2,256,2048]{3,2,1,0:T(8,128)} custom-call(f32[2,2,256,2048]{3,2,1,0:T(8,128)} %get-tuple-element.35.held_ref, bf16[2,2,256,1408]{3,2,1,0:T(8,128)(2,1)} %copy-done.4), custom_call_target="tpu_custom_call", output_to_operand_aliasing={{}: (0, {})} | custom-call | tf_op jit(solution)/shard_map/add0/pallas_call | solution.py:421
  150.2 1.1 copy-done.5
  151.2 3.3 %add11.1 = f32[2,2,256,2048]{3,2,1,0:T(8,128)} custom-call(f32[2,2,256,2048]{3,2,1,0:T(8,128)} %add0.1.held_ref, bf16[2,2,256,640]{3,2,1,0:T(8,128)(2,1)} %copy-done.5), custom_call_target="tpu_custom_call", output_to_operand_aliasing={{}: (0, {})} | custom-call | tf_op jit(solution)/shard_map/add11/pallas_call | solution.py:421
  154.6 0.8 pad_maximum_fusion
  (27 shorter events, 1.7 us)
Async XLA Ops:
  4.2 12.6 %copy-start.6 = (f32[256]{0:T(256)S(1)}, f32[256]{0:T(256)}, u32[]{:S(2)}) copy-start(f32[256]{0:T(256)} %param.11) | copy-start | bytes 3076
  4.2 12.6 %copy-start = (f32[256,256]{1,0:T(8,128)S(1)}, f32[256,256]{1,0:T(8,128)}, u32[]{:S(2)}) copy-start(f32[256,256]{1,0:T(8,128)} %constant.14.clone) | copy-start | bytes 786436
  4.2 12.6 %copy-start.1 = (f32[256,256]{1,0:T(8,128)S(1)}, f32[256,256]{1,0:T(8,128)}, u32[]{:S(2)}) copy-start(f32[256,256]{1,0:T(8,128)} %constant.15.clone) | copy-start | bytes 786436
  4.2 20.3 %collective-permute-start.2 = (bf16[2,2,256,640]{3,2,1,0:T(8,128)(2,1)}, bf16[2,2,256,640]{3,2,1,0:T(8,128)(2,1)}, u32[]{:S(2)}, u32[]{:S(2)}) collective-permute-start(bf16[2,2,256,640]{3,2,1,0:T(8,128)(2,1)} %get-tuple-element.42), channel_id=1, source_target_pairs={{1,0},{2,1},{3,2},{4,3},{5,4},{6,5},{7,6},{8,7},{9,8},{10,9},{11,1... | collective-permute-start | bytes 3932168 | tf_op jit(solution)/shard_map/ppermute | solution.py:20
  6.9 33.2 %collective-permute-start.1 = (bf16[2,2,256,640]{3,2,1,0:T(8,128)(2,1)}, bf16[2,2,256,640]{3,2,1,0:T(8,128)(2,1)S(1)}, u32[]{:S(2)}, u32[]{:S(2)}) collective-permute-start(bf16[2,2,256,640]{3,2,1,0:T(8,128)(2,1)} %get-tuple-element.43), channel_id=1, source_target_pairs={{1,0},{2,1},{3,2},{4,3},{5,4},{6,5},{7,6},{8,7},{9,8},{10,9},{11,1... | collective-permute-start | bytes 3932168 | tf_op jit(solution)/shard_map/ppermute | solution.py:20
  11.5 46.4 %collective-permute-start = (bf16[2,2,256,384]{3,2,1,0:T(8,128)(2,1)}, bf16[2,2,256,384]{3,2,1,0:T(8,128)(2,1)S(1)}, u32[]{:S(2)}, u32[]{:S(2)}) collective-permute-start(bf16[2,2,256,384]{3,2,1,0:T(8,128)(2,1)} %get-tuple-element.41), channel_id=1, source_target_pairs={{1,0},{2,1},{3,2},{4,3},{5,4},{6,5},{7,6},{8,7},{9,8},{10,9},{11,1... | collective-permute-start | bytes 2359304 | tf_op jit(solution)/shard_map/ppermute | solution.py:20
  14.0 60.6 %collective-permute-start.3 = (bf16[2,2,256,384]{3,2,1,0:T(8,128)(2,1)}, bf16[2,2,256,384]{3,2,1,0:T(8,128)(2,1)}, u32[]{:S(2)}, u32[]{:S(2)}) collective-permute-start(bf16[2,2,256,384]{3,2,1,0:T(8,128)(2,1)} %get-tuple-element.40), channel_id=1, source_target_pairs={{1,0},{2,1},{3,2},{4,3},{5,4},{6,5},{7,6},{8,7},{9,8},{10,9},{11,1... | collective-permute-start | bytes 2359304 | tf_op jit(solution)/shard_map/ppermute | solution.py:20
  40.2 1.2 copy-start.2
  57.9 1.0 copy-start.3
  74.7 67.4 %collective-permute-start.8 = (bf16[2,2,256,1408]{3,2,1,0:T(8,128)(2,1)}, bf16[2,2,256,1408]{3,2,1,0:T(8,128)(2,1)S(1)}, u32[]{:S(2)}, u32[]{:S(2)}) collective-permute-start(bf16[2,2,256,1408]{3,2,1,0:T(8,128)(2,1)} %get-tuple-element.36), channel_id=1, source_target_pairs={{0,1},{1,2},{2,3},{3,4},{4,5},{5,6},{6,7},{7,8},{8,9},{9,10},{10,1... | collective-permute-start | bytes 8650760 | tf_op jit(solution)/shard_map/ppermute | solution.py:20
  93.1 1.6 %collective-permute-start.4 = (bf16[256,256]{1,0:T(8,128)(2,1)S(1)}, bf16[256,256]{1,0:T(8,128)(2,1)S(1)}, u32[]{:S(2)}, u32[]{:S(2)}) collective-permute-start(bf16[256,256]{1,0:T(8,128)(2,1)S(1)} %fusion.5), channel_id=1, source_target_pairs={{0,1},{1,0},{2,3},{3,2},{4,5},{5,4},{6,7},{7,6},{8,9},{9,8},{10,11... | collective-permute-start | bytes 393224 | tf_op jit(solution)/shard_map/ppermute | solution.py:439
  95.8 15.3 %collective-permute-start.5 = (bf16[256,256]{1,0:T(8,128)(2,1)S(1)}, bf16[256,256]{1,0:T(8,128)(2,1)S(1)}, u32[]{:S(2)}, u32[]{:S(2)}) collective-permute-start(bf16[256,256]{1,0:T(8,128)(2,1)S(1)} %fusion.1), channel_id=1, source_target_pairs={{0,4},{1,5},{2,6},{3,7},{4,0},{5,1},{6,2},{7,3},{8,12},{9,13},{10,... | collective-permute-start | bytes 393224 | tf_op jit(solution)/shard_map/ppermute | solution.py:439
  95.8 54.3 %collective-permute-start.9 = (bf16[2,2,256,640]{3,2,1,0:T(8,128)(2,1)}, bf16[2,2,256,640]{3,2,1,0:T(8,128)(2,1)S(1)}, u32[]{:S(2)}, u32[]{:S(2)}) collective-permute-start(bf16[2,2,256,640]{3,2,1,0:T(8,128)(2,1)} %get-tuple-element.38), channel_id=1, source_target_pairs={{0,1},{1,2},{2,3},{3,4},{4,5},{5,6},{6,7},{7,8},{8,9},{9,10},{10,1... | collective-permute-start | bytes 3932168 | tf_op jit(solution)/shard_map/ppermute | solution.py:20
  111.0 27.1 %collective-permute-start.6 = (bf16[256,256]{1,0:T(8,128)(2,1)S(1)}, bf16[256,256]{1,0:T(8,128)(2,1)S(1)}, u32[]{:S(2)}, u32[]{:S(2)}) collective-permute-start(bf16[256,256]{1,0:T(8,128)(2,1)S(1)} %add_convert_fusion.1), channel_id=1, source_target_pairs={{0,8},{1,9},{2,10},{3,11},{4,12},{5,13},{6,14},{7,15},{8,0},{9,1},... | collective-permute-start | bytes 393224 | tf_op jit(solution)/shard_map/ppermute | solution.py:439
  138.2 3.9 %collective-permute-start.7 = (bf16[256,256]{1,0:T(8,128)(2,1)S(1)}, bf16[256,256]{1,0:T(8,128)(2,1)S(1)}, u32[]{:S(2)}, u32[]{:S(2)}) collective-permute-start(bf16[256,256]{1,0:T(8,128)(2,1)S(1)} %add_convert_fusion), channel_id=1, source_target_pairs={{0,2},{1,3},{2,0},{3,1},{4,6},{5,7},{6,4},{7,5},{8,10},{9,11},{10,... | collective-permute-start | bytes 393224 | tf_op jit(solution)/shard_map/ppermute | solution.py:439
  142.1 1.6 copy-start.4
  150.1 4.5 %collective-permute-start.10 = (f32[256,256]{1,0:T(8,128)S(1)}, f32[256,256]{1,0:T(8,128)S(1)}, u32[]{:S(2)}, u32[]{:S(2)}) collective-permute-start(f32[256,256]{1,0:T(8,128)S(1)} %convert_add_fusion.1), channel_id=1, source_target_pairs={{0,1},{1,0},{2,3},{3,2},{4,5},{5,4},{6,7},{7,6},{8,9},{9,8},{10,11... | collective-permute-start | bytes 786440 | tf_op jit(solution)/shard_map/ppermute | solution.py:439
  150.2 1.1 copy-start.5

commit v3 on v2

--- a/solution.py
+++ b/solution.py
@@ -331,14 +331,15 @@
     plan = (first_tile, end_tile, final_tile, halo_start, has_past, is_last, group_tile, group_goes_on)
     smem = pl.BlockSpec(memory_space=pltpu.SMEM)
     vmem = pl.BlockSpec(memory_space=pltpu.VMEM)
-    hbm = pl.BlockSpec(memory_space=pl.ANY)
+    hbm = pl.BlockSpec(memory_space=pltpu.HBM)
+    free = pl.BlockSpec(memory_space=pl.ANY)
     args = [*meta, *tables, probe_field, intensity, specimen, halos[stage]]
-    in_specs = [smem] * 3 + [hbm] * 4 + [vmem, hbm, hbm, hbm]
+    in_specs = [smem] * 3 + [hbm] * 4 + [vmem, hbm, hbm, free]
     aliases = {}
     if has_past:
         interior, carry, probe_sum = past
         args += [halos[stage - 1], carry, probe_sum, interior]
-        in_specs += [hbm, hbm, vmem, hbm]
+        in_specs += [free, hbm, vmem, hbm]
         aliases = {len(args) - 1: 0}
     if group_goes_on:
         args += [overflow]
@@ -416,12 +417,12 @@
 def add_chunk(interior, came, first_tile):
     _, slices, rows, _ = interior.shape
     tiles = came.shape[3] // LANES
-    hbm = pl.BlockSpec(memory_space=pl.ANY)
+    hbm = pl.BlockSpec(memory_space=pltpu.HBM)
     block = (tiles, 2, slices, rows, LANES)
     return pl.pallas_call(
         functools.partial(add_kernel, first_tile, tiles),
         out_shape=jax.ShapeDtypeStruct(interior.shape, interior.dtype),
-        in_specs=[hbm, hbm],
+        in_specs=[hbm, pl.BlockSpec(memory_space=pl.ANY)],
         out_specs=hbm,
         scratch_shapes=[
             pltpu.VMEM(block, F32),
@@ -439,16 +440,18 @@
     return lax.ppermute(value, axis, [(k, k ^ step) for k in range(lax.axis_size(axis))])
 
 
-def sum_over(value, axis, meanwhile):
+def sum_over(value, axis, after_pair, meanwhile):
     count = lax.axis_size(axis)
     steps = [1 << k for k in range(1, count.bit_length() - 1)]
     odd = lax.rem(lax.axis_index(axis), 2) == 1
     kept, given = jnp.where(odd, value[1], value[0]), jnp.where(odd, value[0], value[1])
     kept = kept.astype(BF).astype(F32) + exchanged(given.astype(BF), axis, 1).astype(F32)
-    for n, step in enumerate(steps[1:] + steps[:1]):
+    for n, step in enumerate(steps):
         mine = kept.astype(BF)
+        if n == 1:
+            mine = after_pair(mine)
         kept = mine.astype(F32) + exchanged(mine, axis, step).astype(F32)
-        if n == len(steps) - 1:
+        if n == 2:
             kept = meanwhile(kept)
     other = exchanged(kept, axis, 1)
     return jnp.stack([jnp.where(odd, other, kept), jnp.where(odd, kept, other)])
@@ -463,7 +466,7 @@
         halos.append(passed_along(piece, "row", -1))
         start = end
     meta = (row_offset, col_offset, counts)
-    past, came, at = None, [], 0
+    past, sent, at = None, [], 0
     for stage in range(len(ends)):
         if stage == 0 or stage - 1 in sends:
             last = min(send for send in sends if send >= stage)
@@ -473,25 +476,31 @@
             stage, ends, group, meta, tables, probe_field, intensity, specimen, halos, past)
         if stage in sends:
             if stage + 1 < len(ends):
-                sent, halos[stage + 1] = lax.optimization_barrier((group[2], halos[stage + 1]))
-                group = (*group[:2], sent)
-            came.append((passed_along(group[2], "row", 1), group[0]))
+                ready, halos[stage + 1] = lax.optimization_barrier((group[2], halos[stage + 1]))
+                group = (*group[:2], ready)
+            sent.append((group[2], group[0]))
             at = group[1]
     interior, _, probe_sum = past
-    held = [interior]
+    held = {}
+
+    def after_pair(mine):
+        ready, mine = lax.optimization_barrier((sent[1][0], mine))
+        held["came"] = passed_along(ready, "row", 1)
+        return mine
 
     def meanwhile(kept):
-        kept, held[0] = lax.optimization_barrier((kept, add_chunk(held[0], *came[0])))
+        first = add_chunk(interior, passed_along(sent[0][0], "row", 1), sent[0][1])
+        kept, held["interior"] = lax.optimization_barrier((kept, first))
         return kept
 
-    probe_total = sum_over(probe_sum, "row", meanwhile)
-    interior = add_chunk(held[0], *came[1])
+    probe_total = sum_over(probe_sum, "row", after_pair, meanwhile)
+    interior = add_chunk(held["interior"], held["came"], sent[1][1])
     return interior, probe_total
 
 
 def solution(mesh):
     return jax.shard_map(
-        functools.partial(body, (5, 10, 13, 16), (2, 3)),
+        functools.partial(body, (6, 12, 16), (1, 2)),
         mesh=mesh,
         in_specs=(
             P("group", None, "row", None),

time: 154 us -> 156 us (1.013)
  the two profiles are of different devices: /device:TPU:21 before, /device:TPU:13 now
where the time goes in v3:
time: 156 us; the launch traced here: 154 us
  waiting for transfers between devices  61.9 us (40%)
  Pallas kernels  44.8 us (29%)
  starting transfers between devices  27.3 us (18%)
  local copies, waits for them, and re-layouts  12 us (8%)
  other arithmetic  3.96 us (3%)
  matrix products  2.72 us (2%)
    ppermute x5, waiting for transfers between devices, exchanged(): lax.ppermute(value, axis, [(k, k ^ step) for k in range(lax.axis_size(axi...  47.4 us
    pallas_call x3, Pallas kernels, run_stage(): pl.pallas_call(functools.partial(stage_kernel, plan, stage), out_shape=ou...  35.1 us
    ppermute x5, starting transfers between devices, passed_along(): lax.ppermute(value, axis, [(source, source + steps) for source in range(f...  21.9 us
    ppermute x5, waiting for transfers between devices, passed_along(): lax.ppermute(value, axis, [(source, source + steps) for source in range(f...  14.6 us
    pallas_call x2, Pallas kernels, add_chunk(): pl.pallas_call(functools.partial(add_kernel, first_tile, tiles), out_shap...  9.72 us
    slice x2, local copies, waits for them, and re-layouts, body(): piece = source[:, :, :, start * LANES:end * LANES]  6.08 us
    ppermute x5, starting transfers between devices, exchanged(): lax.ppermute(value, axis, [(k, k ^ step) for k in range(lax.axis_size(axi...  5.47 us
    unnamed x14, local copies, waits for them, and re-layouts  4.92 us
  transfers between devices with their start and end apart: 10, of which 6 were waited for; matrix products, arithmetic and copies ran while one was open for 6% of the time, Pallas kernels for 29%

profile of v3, /device:TPU:13, one launch (start us, length us, event | category | flops | bytes accessed | tf_op | source)
XLA Modules:
  0.0 154.4 jit_solution(2999331651528197624)
XLA Ops:
  0.6 3.8 %fusion.14 = (bf16[2,2,256,768]{3,2,1,0:T(8,128)(2,1)}, bf16[2,2,256,768]{3,2,1,0:T(8,128)(2,1)}) fusion(bf16[2,2,256,2048]{3,2,1,0:T(8,128)(2,1)} %refs_9_.5), kind=kLoop, calls=%fused_computation.30 | loop fusion | bytes 6291456 | tf_op jit(solution)/shard_map/slice | solution.py:465
  4.5 2.7 %collective-permute-start.1 = (bf16[2,2,256,768]{3,2,1,0:T(8,128)(2,1)}, bf16[2,2,256,768]{3,2,1,0:T(8,128)(2,1)}, u32[]{:S(2)}, u32[]{:S(2)}) collective-permute-start(bf16[2,2,256,768]{3,2,1,0:T(8,128)(2,1)} %get-tuple-element.36), channel_id=1, source_target_pairs={{1,0},{2,1},{3,2},{4,3},{5,4},{6,5},{7,6},{8,7},{9,8},{10,9},{11,1... | collective-permute-start | bytes 4718600 | tf_op jit(solution)/shard_map/ppermute | solution.py:20
  7.2 1.9 %collective-permute-start = (bf16[2,2,256,768]{3,2,1,0:T(8,128)(2,1)}, bf16[2,2,256,768]{3,2,1,0:T(8,128)(2,1)S(1)}, u32[]{:S(2)}, u32[]{:S(2)}) collective-permute-start(bf16[2,2,256,768]{3,2,1,0:T(8,128)(2,1)} %get-tuple-element.37), channel_id=1, source_target_pairs={{1,0},{2,1},{3,2},{4,3},{5,4},{6,5},{7,6},{8,7},{9,8},{10,9},{11,1... | collective-permute-start | bytes 4718600 | tf_op jit(solution)/shard_map/ppermute | solution.py:20
  9.1 2.3 %slice.19 = bf16[2,2,256,512]{3,2,1,0:T(8,128)(2,1)} slice(bf16[2,2,256,2048]{3,2,1,0:T(8,128)(2,1)} %refs_9_.5), slice={[0:2], [0:2], [0:256], [1536:2048]} | slice | bytes 2097152 | tf_op jit(solution)/shard_map/slice | solution.py:465
  11.4 2.5 %collective-permute-start.2 = (bf16[2,2,256,512]{3,2,1,0:T(8,128)(2,1)}, bf16[2,2,256,512]{3,2,1,0:T(8,128)(2,1)S(1)}, u32[]{:S(2)}, u32[]{:S(2)}) collective-permute-start(bf16[2,2,256,512]{3,2,1,0:T(8,128)(2,1)} %slice.19), channel_id=1, source_target_pairs={{1,0},{2,1},{3,2},{4,3},{5,4},{6,5},{7,6},{8,7},{9,8},{10,9},{11,1... | collective-permute-start | bytes 3145736 | tf_op jit(solution)/shard_map/ppermute | solution.py:20
  14.6 0.7 fusion.3
  15.3 0.7 negate_convert_fusion
  16.0 0.7 fusion
  16.7 1.0 copy.18.refs_5_
  18.4 0.8 maximum_maximum_fusion.1.refs_6_
  19.2 8.3 %collective-permute-done.1.refs_10_.refs_11_ = bf16[2,2,256,768]{3,2,1,0:T(8,128)(2,1)} collective-permute-done((bf16[2,2,256,768]{3,2,1,0:T(8,128)(2,1)}, bf16[2,2,256,768]{3,2,1,0:T(8,128)(2,1)}, u32[]{:S(2)}, u32[]{:S(2)}) %collective-permute-start.1) | collective-permute-done | bytes 1572896 | tf_op jit(solution)/shard_map/ppermute | solution.py:20
  27.5 10.5 %stage0.1 = (f32[2,2,256,2048]{3,2,1,0:T(8,128)}, bf16[2,2,256,1280]{3,2,1,0:T(8,128)(2,1)}, f32[2,2,2,512,128]{4,3,2,1,0:T(8,128)}, f32[2,256,256]{2,1,0:T(8,128)}) custom-call(s32[16]{0:T(128)} %refs_0_.5, s32[16]{0:T(128)} %refs_1_.5, s32[1]{0:T(128)S(6)} %copy.24.refs_2_, bf16[512,512]{1,0:T(8,128)(2,1)} %constant.26.refs_3_, ...), custom_call_target="tpu_custom_call" | custom-call | flops 3000000000 | bytes 8000000 | tf_op jit(solution)/shard_map/stage0/pallas_call | solution.py:379
  38.1 6.2 %collective-permute-done.refs_10_.refs_11_ = bf16[2,2,256,768]{3,2,1,0:T(8,128)(2,1)S(1)} collective-permute-done((bf16[2,2,256,768]{3,2,1,0:T(8,128)(2,1)}, bf16[2,2,256,768]{3,2,1,0:T(8,128)(2,1)S(1)}, u32[]{:S(2)}, u32[]{:S(2)}) %collective-permute-start) | collective-permute-done | bytes 1572896 | tf_op jit(solution)/shard_map/ppermute | solution.py:20
  44.3 1.2 copy-done.2
  45.5 12.1 %stage1.1 = (f32[2,2,256,2048]{3,2,1,0:T(8,128)}, bf16[2,2,256,1280]{3,2,1,0:T(8,128)(2,1)}, f32[2,2,2,512,128]{4,3,2,1,0:T(8,128)}, f32[2,256,256]{2,1,0:T(8,128)}) custom-call(s32[16]{0:T(128)} %refs_0_.5, s32[16]{0:T(128)} %refs_1_.5, s32[1]{0:T(128)S(6)} %copy.24.refs_2_, ...), custom_call_target="tpu_custom_call", output_to_operand_aliasing={{0}: (14, {}), {1}: (15, {})} | custom-call | flops 3000000000 | bytes 8000000 | tf_op jit(solution)/shard_map/stage1/pallas_call | solution.py:379
  57.7 1.0 copy-done.5
  58.7 12.8 %collective-permute-start.7 = (bf16[2,2,256,1280]{3,2,1,0:T(8,128)(2,1)}, bf16[2,2,256,1280]{3,2,1,0:T(8,128)(2,1)S(1)}, u32[]{:S(2)}, u32[]{:S(2)}) collective-permute-start(bf16[2,2,256,1280]{3,2,1,0:T(8,128)(2,1)} %get-tuple-element.32), channel_id=1, source_target_pairs={{0,1},{1,2},{2,3},{3,4},{4,5},{5,6},{6,7},{7,8},{8,9},{9,10},{10,1... | collective-permute-start | bytes 7864328 | tf_op jit(solution)/shard_map/ppermute | solution.py:20
  71.5 12.5 %stage2.1 = (f32[2,2,256,2048]{3,2,1,0:T(8,128)}, bf16[2,2,256,768]{3,2,1,0:T(8,128)(2,1)}, f32[2,256,256]{2,1,0:T(8,128)}) custom-call(s32[16]{0:T(128)} %refs_0_.5, s32[16]{0:T(128)} %refs_1_.5, s32[1]{0:T(128)S(6)} %copy.24.refs_2_, bf16[512,512]{1,0:T(8,128)(2,1)} %constant.26.refs_3_, ...), custom_call_target="tpu_custom_call", output_to_operand_aliasing={{0}: (14, {})} | custom-call | flops 3000000000 | bytes 8000000 | tf_op jit(solution)/shard_map/stage2/pallas_call | solution.py:379
  84.0 1.1 fusion.5
  85.2 1.3 collective-permute-done.3
  86.5 1.1 fusion.1
  87.6 1.5 collective-permute-start.4
  89.0 20.3 %collective-permute-done.4 = bf16[256,256]{1,0:T(8,128)(2,1)S(1)} collective-permute-done((bf16[256,256]{1,0:T(8,128)(2,1)S(1)}, bf16[256,256]{1,0:T(8,128)(2,1)S(1)}, u32[]{:S(2)}, u32[]{:S(2)}) %collective-permute-start.4) | collective-permute-done | bytes 131104 | tf_op jit(solution)/shard_map/ppermute | solution.py:440
  109.4 1.9 %collective-permute-start.8 = (bf16[2,2,256,768]{3,2,1,0:T(8,128)(2,1)}, bf16[2,2,256,768]{3,2,1,0:T(8,128)(2,1)S(1)}, u32[]{:S(2)}, u32[]{:S(2)}) collective-permute-start(bf16[2,2,256,768]{3,2,1,0:T(8,128)(2,1)} %get-tuple-element.34), channel_id=1, source_target_pairs={{0,1},{1,2},{2,3},{3,4},{4,5},{5,6},{6,7},{7,8},{8,9},{9,10},{10,1... | collective-permute-start | bytes 4718600 | tf_op jit(solution)/shard_map/ppermute | solution.py:20
  111.3 3.8 %collective-permute-start.5 = (bf16[256,256]{1,0:T(8,128)(2,1)S(1)}, bf16[256,256]{1,0:T(8,128)(2,1)S(1)}, u32[]{:S(2)}, u32[]{:S(2)}) collective-permute-start(bf16[256,256]{1,0:T(8,128)(2,1)S(1)} %add_convert_fusion.1), channel_id=1, source_target_pairs={{0,4},{1,5},{2,6},{3,7},{4,0},{5,1},{6,2},{7,3},{8,12},{9,13},{10,... | collective-permute-start | bytes 393224 | tf_op jit(solution)/shard_map/ppermute | solution.py:440
  115.1 21.0 %collective-permute-done.5 = bf16[256,256]{1,0:T(8,128)(2,1)S(1)} collective-permute-done((bf16[256,256]{1,0:T(8,128)(2,1)S(1)}, bf16[256,256]{1,0:T(8,128)(2,1)S(1)}, u32[]{:S(2)}, u32[]{:S(2)}) %collective-permute-start.5) | collective-permute-done | bytes 131104 | tf_op jit(solution)/shard_map/ppermute | solution.py:440
  136.2 4.7 %collective-permute-done.6 = bf16[256,256]{1,0:T(8,128)(2,1)S(1)} collective-permute-done((bf16[256,256]{1,0:T(8,128)(2,1)S(1)}, bf16[256,256]{1,0:T(8,128)(2,1)S(1)}, u32[]{:S(2)}, u32[]{:S(2)}) %collective-permute-start.6) | collective-permute-done | bytes 131104 | tf_op jit(solution)/shard_map/ppermute | solution.py:440
  141.0 1.5 copy-done.3
  142.5 5.6 %add0.1.held_ref = f32[2,2,256,2048]{3,2,1,0:T(8,128)} custom-call(f32[2,2,256,2048]{3,2,1,0:T(8,128)} %get-tuple-element.31.held_ref, bf16[2,2,256,1280]{3,2,1,0:T(8,128)(2,1)} %copy-done.3), custom_call_target="tpu_custom_call", output_to_operand_aliasing={{}: (0, {})} | custom-call | tf_op jit(solution)/shard_map/add0/pallas_call | solution.py:422
  148.2 1.2 copy-done.4
  149.3 4.1 %add10.1 = f32[2,2,256,2048]{3,2,1,0:T(8,128)} custom-call(f32[2,2,256,2048]{3,2,1,0:T(8,128)} %add0.1.held_ref, bf16[2,2,256,768]{3,2,1,0:T(8,128)(2,1)} %copy-done.4), custom_call_target="tpu_custom_call", output_to_operand_aliasing={{}: (0, {})} | custom-call | tf_op jit(solution)/shard_map/add10/pallas_call | solution.py:422
  153.5 0.8 pad_maximum_fusion
  (24 shorter events, 1.1 us)
Async XLA Ops:
  4.5 9.4 %copy-start.6 = (f32[256]{0:T(256)S(1)}, f32[256]{0:T(256)}, u32[]{:S(2)}) copy-start(f32[256]{0:T(256)} %param.11) | copy-start | bytes 3076
  4.5 9.5 %copy-start = (f32[256,256]{1,0:T(8,128)S(1)}, f32[256,256]{1,0:T(8,128)}, u32[]{:S(2)}) copy-start(f32[256,256]{1,0:T(8,128)} %constant.14.clone) | copy-start | bytes 786436
  4.5 9.5 %copy-start.1 = (f32[256,256]{1,0:T(8,128)S(1)}, f32[256,256]{1,0:T(8,128)}, u32[]{:S(2)}) copy-start(f32[256,256]{1,0:T(8,128)} %constant.15.clone) | copy-start | bytes 786436
  4.5 23.1 %collective-permute-start.1 = (bf16[2,2,256,768]{3,2,1,0:T(8,128)(2,1)}, bf16[2,2,256,768]{3,2,1,0:T(8,128)(2,1)}, u32[]{:S(2)}, u32[]{:S(2)}) collective-permute-start(bf16[2,2,256,768]{3,2,1,0:T(8,128)(2,1)} %get-tuple-element.36), channel_id=1, source_target_pairs={{1,0},{2,1},{3,2},{4,3},{5,4},{6,5},{7,6},{8,7},{9,8},{10,9},{11,1... | collective-permute-start | bytes 4718600 | tf_op jit(solution)/shard_map/ppermute | solution.py:20
  7.2 37.1 %collective-permute-start = (bf16[2,2,256,768]{3,2,1,0:T(8,128)(2,1)}, bf16[2,2,256,768]{3,2,1,0:T(8,128)(2,1)S(1)}, u32[]{:S(2)}, u32[]{:S(2)}) collective-permute-start(bf16[2,2,256,768]{3,2,1,0:T(8,128)(2,1)} %get-tuple-element.37), channel_id=1, source_target_pairs={{1,0},{2,1},{3,2},{4,3},{5,4},{6,5},{7,6},{8,7},{9,8},{10,9},{11,1... | collective-permute-start | bytes 4718600 | tf_op jit(solution)/shard_map/ppermute | solution.py:20
  11.4 46.3 %collective-permute-start.2 = (bf16[2,2,256,512]{3,2,1,0:T(8,128)(2,1)}, bf16[2,2,256,512]{3,2,1,0:T(8,128)(2,1)S(1)}, u32[]{:S(2)}, u32[]{:S(2)}) collective-permute-start(bf16[2,2,256,512]{3,2,1,0:T(8,128)(2,1)} %slice.19), channel_id=1, source_target_pairs={{1,0},{2,1},{3,2},{4,3},{5,4},{6,5},{7,6},{8,7},{9,8},{10,9},{11,1... | collective-permute-start | bytes 3145736 | tf_op jit(solution)/shard_map/ppermute | solution.py:20
  44.3 1.2 copy-start.2
  57.6 1.1 copy-start.5
  58.7 82.3 %collective-permute-start.7 = (bf16[2,2,256,1280]{3,2,1,0:T(8,128)(2,1)}, bf16[2,2,256,1280]{3,2,1,0:T(8,128)(2,1)S(1)}, u32[]{:S(2)}, u32[]{:S(2)}) collective-permute-start(bf16[2,2,256,1280]{3,2,1,0:T(8,128)(2,1)} %get-tuple-element.32), channel_id=1, source_target_pairs={{0,1},{1,2},{2,3},{3,4},{4,5},{5,6},{6,7},{7,8},{8,9},{9,10},{10,1... | collective-permute-start | bytes 7864328 | tf_op jit(solution)/shard_map/ppermute | solution.py:20
  85.1 1.4 collective-permute-start.3
  87.6 21.8 %collective-permute-start.4 = (bf16[256,256]{1,0:T(8,128)(2,1)S(1)}, bf16[256,256]{1,0:T(8,128)(2,1)S(1)}, u32[]{:S(2)}, u32[]{:S(2)}) collective-permute-start(bf16[256,256]{1,0:T(8,128)(2,1)S(1)} %fusion.1), channel_id=1, source_target_pairs={{0,2},{1,3},{2,0},{3,1},{4,6},{5,7},{6,4},{7,5},{8,10},{9,11},{10,... | collective-permute-start | bytes 393224 | tf_op jit(solution)/shard_map/ppermute | solution.py:440
  109.4 38.8 %collective-permute-start.8 = (bf16[2,2,256,768]{3,2,1,0:T(8,128)(2,1)}, bf16[2,2,256,768]{3,2,1,0:T(8,128)(2,1)S(1)}, u32[]{:S(2)}, u32[]{:S(2)}) collective-permute-start(bf16[2,2,256,768]{3,2,1,0:T(8,128)(2,1)} %get-tuple-element.34), channel_id=1, source_target_pairs={{0,1},{1,2},{2,3},{3,4},{4,5},{5,6},{6,7},{7,8},{8,9},{9,10},{10,1... | collective-permute-start | bytes 4718600 | tf_op jit(solution)/shard_map/ppermute | solution.py:20
  111.3 24.8 %collective-permute-start.5 = (bf16[256,256]{1,0:T(8,128)(2,1)S(1)}, bf16[256,256]{1,0:T(8,128)(2,1)S(1)}, u32[]{:S(2)}, u32[]{:S(2)}) collective-permute-start(bf16[256,256]{1,0:T(8,128)(2,1)S(1)} %add_convert_fusion.1), channel_id=1, source_target_pairs={{0,4},{1,5},{2,6},{3,7},{4,0},{5,1},{6,2},{7,3},{8,12},{9,13},{10,... | collective-permute-start | bytes 393224 | tf_op jit(solution)/shard_map/ppermute | solution.py:440
  136.2 4.8 %collective-permute-start.6 = (bf16[256,256]{1,0:T(8,128)(2,1)S(1)}, bf16[256,256]{1,0:T(8,128)(2,1)S(1)}, u32[]{:S(2)}, u32[]{:S(2)}) collective-permute-start(bf16[256,256]{1,0:T(8,128)(2,1)S(1)} %add_convert_fusion), channel_id=1, source_target_pairs={{0,8},{1,9},{2,10},{3,11},{4,12},{5,13},{6,14},{7,15},{8,0},{9,1},... | collective-permute-start | bytes 393224 | tf_op jit(solution)/shard_map/ppermute | solution.py:440
  141.0 1.5 copy-start.3
  148.1 5.4 %collective-permute-start.9 = (f32[256,256]{1,0:T(8,128)S(1)}, f32[256,256]{1,0:T(8,128)S(1)}, u32[]{:S(2)}, u32[]{:S(2)}) collective-permute-start(f32[256,256]{1,0:T(8,128)S(1)} %convert_add_fusion.1), channel_id=1, source_target_pairs={{0,1},{1,0},{2,3},{3,2},{4,5},{5,4},{6,7},{7,6},{8,9},{9,8},{10,11... | collective-permute-start | bytes 786440 | tf_op jit(solution)/shard_map/ppermute | solution.py:440
  148.2 1.2 copy-start.4

commit v4 on v3

--- a/solution.py
+++ b/solution.py
@@ -61,7 +61,7 @@
     refs = list(refs)
     row_ref, col_ref, count_ref = refs[:3]
     del refs[:3]
-    tables_hbm = refs[:4]
+    four_ref, conj_ref, prop_ref, back_ref = refs[:4]
     del refs[:4]
     probe_ref, intensity_ref, specimen_ref = refs[:3]
     del refs[:3]
@@ -76,9 +76,7 @@
     carry_out = None if is_last else refs.pop(0)
     probe_out = refs.pop(0)
     (slots_ref, ext_ref, acc_ref, measured_ref, round_ref, twice_ref, sum_ref, win_ref, wave0_ref, wave1_ref,
-     stack_ref, half_ref, tile_ref, tables_ref,
-     load_sem, slot_sem, store_sem, table_sem) = refs
-    four_ref, conj_ref, prop_ref, back_ref = (tables_ref.at[k] for k in range(4))
+     stack_ref, half_ref, tile_ref, load_sem, slot_sem, store_sem) = refs
     extent = probe_ref.shape[1]
     tiles = end_tile - first_tile
     past_tiles = halo_start - first_tile
@@ -97,8 +95,6 @@
             source = halo_now.at[:, :, :, pl.ds((j - past_tiles) * LANES, LANES)]
         copies.append(pltpu.make_async_copy(
             source, ext_ref.at[:, :, j, pl.ds(extent, extent), :], load_sem.at[2 * j + 1]))
-    for k in range(4):
-        copies.append(pltpu.make_async_copy(tables_hbm[k], tables_ref.at[k], table_sem.at[k]))
     for copy in copies:
         copy.start()
     carried = None
@@ -334,7 +330,7 @@
     hbm = pl.BlockSpec(memory_space=pltpu.HBM)
     free = pl.BlockSpec(memory_space=pl.ANY)
     args = [*meta, *tables, probe_field, intensity, specimen, halos[stage]]
-    in_specs = [smem] * 3 + [hbm] * 4 + [vmem, hbm, hbm, free]
+    in_specs = [smem] * 3 + [vmem] * 4 + [vmem, hbm, hbm, free]
     aliases = {}
     if has_past:
         interior, carry, probe_sum = past
@@ -370,11 +366,9 @@
         pltpu.VMEM((2 * extent, 2 * extent), BF),
         pltpu.VMEM((2 * extent, 2 * extent), BF),
         pltpu.VMEM((2, *pairs, extent, extent), BF),
-        pltpu.VMEM((4, 2 * extent, 2 * extent), BF),
         pltpu.SemaphoreType.DMA((2 * tiles,)),
         pltpu.SemaphoreType.DMA((4,)),
         pltpu.SemaphoreType.DMA((1,)),
-        pltpu.SemaphoreType.DMA((4,)),
     ]
     results = list(pl.pallas_call(
         functools.partial(stage_kernel, plan, stage),
@@ -383,7 +377,7 @@
         out_specs=out_specs,
         scratch_shapes=scratch,
         input_output_aliases=aliases,
-        compiler_params=pltpu.CompilerParams(vmem_limit_bytes=56 * 1024 * 1024),
+        compiler_params=pltpu.CompilerParams(vmem_limit_bytes=50 * 1024 * 1024),
         cost_estimate=pl.CostEstimate(flops=3 * 10**9, bytes_accessed=8 * 10**6, transcendentals=0),
         name=f"stage{stage}",
     )(*args))
@@ -431,7 +425,7 @@
             pltpu.SemaphoreType.DMA((tiles,)),
         ],
         input_output_aliases={0: 0},
-        compiler_params=pltpu.CompilerParams(vmem_limit_bytes=56 * 1024 * 1024),
+        compiler_params=pltpu.CompilerParams(vmem_limit_bytes=50 * 1024 * 1024),
         name=f"add{first_tile}",
     )(interior, came)
 
@@ -440,19 +434,15 @@
     return lax.ppermute(value, axis, [(k, k ^ step) for k in range(lax.axis_size(axis))])
 
 
-def sum_over(value, axis, after_pair, meanwhile):
+def sum_over(value, axis):
     count = lax.axis_size(axis)
     steps = [1 << k for k in range(1, count.bit_length() - 1)]
     odd = lax.rem(lax.axis_index(axis), 2) == 1
     kept, given = jnp.where(odd, value[1], value[0]), jnp.where(odd, value[0], value[1])
     kept = kept.astype(BF).astype(F32) + exchanged(given.astype(BF), axis, 1).astype(F32)
-    for n, step in enumerate(steps):
+    for step in steps[1:] + steps[:1]:
         mine = kept.astype(BF)
-        if n == 1:
-            mine = after_pair(mine)
         kept = mine.astype(F32) + exchanged(mine, axis, step).astype(F32)
-        if n == 2:
-            kept = meanwhile(kept)
     other = exchanged(kept, axis, 1)
     return jnp.stack([jnp.where(odd, other, kept), jnp.where(odd, kept, other)])
 
@@ -481,26 +471,17 @@
             sent.append((group[2], group[0]))
             at = group[1]
     interior, _, probe_sum = past
-    held = {}
-
-    def after_pair(mine):
-        ready, mine = lax.optimization_barrier((sent[1][0], mine))
-        held["came"] = passed_along(ready, "row", 1)
-        return mine
-
-    def meanwhile(kept):
-        first = add_chunk(interior, passed_along(sent[0][0], "row", 1), sent[0][1])
-        kept, held["interior"] = lax.optimization_barrier((kept, first))
-        return kept
-
-    probe_total = sum_over(probe_sum, "row", after_pair, meanwhile)
-    interior = add_chunk(held["interior"], held["came"], sent[1][1])
+    came = [(passed_along(chunk, "row", 1), first) for chunk, first in sent]
+    interior = add_chunk(interior, *came[0])
+    interior, probe_sum = lax.optimization_barrier((interior, probe_sum))
+    probe_total = sum_over(probe_sum, "row")
+    interior = add_chunk(interior, *came[1])
     return interior, probe_total
 
 
 def solution(mesh):
     return jax.shard_map(
-        functools.partial(body, (6, 12, 16), (1, 2)),
+        functools.partial(body, (5, 10, 16), (1, 2)),
         mesh=mesh,
         in_specs=(
             P("group", None, "row", None),

time: 156 us -> 130 us (0.83)
  the two profiles are of different devices: /device:TPU:13 before, /device:TPU:31 now
where the time goes in v4:
time: 130 us; the launch traced here: 132 us
  Pallas kernels  43.4 us (33%)
  starting transfers between devices  43.2 us (33%)
  waiting for transfers between devices  33.4 us (26%)
  local copies, waits for them, and re-layouts  6.58 us (5%)
  matrix products  2.72 us (2%)
  between operations  1.58 us (1%)
    pallas_call x3, Pallas kernels, run_stage(): pl.pallas_call(functools.partial(stage_kernel, plan, stage), out_shape=ou...  34.6 us
    ppermute x5, starting transfers between devices, exchanged(): lax.ppermute(value, axis, [(k, k ^ step) for k in range(lax.axis_size(axi...  32 us
    ppermute x5, waiting for transfers between devices, exchanged(): lax.ppermute(value, axis, [(k, k ^ step) for k in range(lax.axis_size(axi...  30.9 us
    ppermute x5, starting transfers between devices, passed_along(): lax.ppermute(value, axis, [(source, source + steps) for source in range(f...  11.2 us
    pallas_call x2, Pallas kernels, add_chunk(): pl.pallas_call(functools.partial(add_kernel, first_tile, tiles), out_shap...  8.8 us
    slice x2, local copies, waits for them, and re-layouts, body(): piece = source[:, :, :, start * LANES:end * LANES]  6.28 us
  transfers between devices with their start and end apart: 10, of which 5 were waited for; matrix products, arithmetic and copies ran while one was open for 5% of the time, Pallas kernels for 33%

profile of v4, /device:TPU:31, one launch (start us, length us, event | category | flops | bytes accessed | tf_op | source)
XLA Modules:
  0.0 132.0 jit_solution(13350034669136574153)
XLA Ops:
  0.6 3.5 %fusion.14 = (bf16[2,2,256,640]{3,2,1,0:T(8,128)(2,1)}, bf16[2,2,256,640]{3,2,1,0:T(8,128)(2,1)}) fusion(bf16[2,2,256,2048]{3,2,1,0:T(8,128)(2,1)} %refs_9_.5), kind=kLoop, calls=%fused_computation.30 | loop fusion | bytes 5242880 | tf_op jit(solution)/shard_map/slice | solution.py:455
  4.2 3.8 %collective-permute-start.1 = (bf16[2,2,256,640]{3,2,1,0:T(8,128)(2,1)}, bf16[2,2,256,640]{3,2,1,0:T(8,128)(2,1)}, u32[]{:S(2)}, u32[]{:S(2)}) collective-permute-start(bf16[2,2,256,640]{3,2,1,0:T(8,128)(2,1)} %get-tuple-element.32), channel_id=1, source_target_pairs={{1,0},{2,1},{3,2},{4,3},{5,4},{6,5},{7,6},{8,7},{9,8},{10,9},{11,1... | collective-permute-start | bytes 3932168 | tf_op jit(solution)/shard_map/ppermute | solution.py:20
  8.0 2.4 %collective-permute-start = (bf16[2,2,256,640]{3,2,1,0:T(8,128)(2,1)}, bf16[2,2,256,640]{3,2,1,0:T(8,128)(2,1)}, u32[]{:S(2)}, u32[]{:S(2)}) collective-permute-start(bf16[2,2,256,640]{3,2,1,0:T(8,128)(2,1)} %get-tuple-element.33), channel_id=1, source_target_pairs={{1,0},{2,1},{3,2},{4,3},{5,4},{6,5},{7,6},{8,7},{9,8},{10,9},{11,1... | collective-permute-start | bytes 3932168 | tf_op jit(solution)/shard_map/ppermute | solution.py:20
  10.3 2.8 %slice.19 = bf16[2,2,256,768]{3,2,1,0:T(8,128)(2,1)} slice(bf16[2,2,256,2048]{3,2,1,0:T(8,128)(2,1)} %refs_9_.5), slice={[0:2], [0:2], [0:256], [1280:2048]} | slice | bytes 3145728 | tf_op jit(solution)/shard_map/slice | solution.py:455
  13.1 2.4 %collective-permute-start.2 = (bf16[2,2,256,768]{3,2,1,0:T(8,128)(2,1)}, bf16[2,2,256,768]{3,2,1,0:T(8,128)(2,1)}, u32[]{:S(2)}, u32[]{:S(2)}) collective-permute-start(bf16[2,2,256,768]{3,2,1,0:T(8,128)(2,1)} %slice.19), channel_id=1, source_target_pairs={{1,0},{2,1},{3,2},{4,3},{5,4},{6,5},{7,6},{8,7},{9,8},{10,9},{11,1... | collective-permute-start | bytes 4718600 | tf_op jit(solution)/shard_map/ppermute | solution.py:20
  15.6 0.7 fusion.2
  16.2 0.7 fusion.3
  16.9 0.7 fusion
  17.6 0.0 copy-start.1
  17.6 0.0 copy-start.2
  17.7 0.0 copy-start.3
  17.7 0.0 copy-start.4
  17.7 0.7 negate_convert_fusion
  18.4 0.2 copy.18.refs_5_
  19.4 9.1 %stage0.1 = (f32[2,2,256,2048]{3,2,1,0:T(8,128)}, bf16[2,2,256,1024]{3,2,1,0:T(8,128)(2,1)}, f32[2,2,2,512,128]{4,3,2,1,0:T(8,128)}, f32[2,256,256]{2,1,0:T(8,128)S(1)}) custom-call(s32[16]{0:T(128)S(1)} %copy-done.3, s32[16]{0:T(128)S(1)} %copy-done.4, s32[1]{0:T(128)S(6)} %copy.24.refs_2_, bf16[512,512]{1,0:T(8,128)(2,1)S(1)} %copy-done.1, ...), custom_call_target="tpu_custom_call" | custom-call | flops 3000000000 | bytes 8000000 | tf_op jit(solution)/shard_map/stage0/pallas_call | solution.py:373
  28.5 15.7 %stage1.1 = (f32[2,2,256,2048]{3,2,1,0:T(8,128)}, bf16[2,2,256,1024]{3,2,1,0:T(8,128)(2,1)}, f32[2,2,2,512,128]{4,3,2,1,0:T(8,128)}, f32[2,256,256]{2,1,0:T(8,128)S(1)}) custom-call(s32[16]{0:T(128)S(1)} %copy-done.3, s32[16]{0:T(128)S(1)} %copy-done.4, s32[1]{0:T(128)S(6)} %copy.24.refs_2_, ...), custom_call_target="tpu_custom_call", output_to_operand_aliasing={{0}: (14, {}), {1}: (15, {})} | custom-call | flops 3000000000 | bytes 8000000 | tf_op jit(solution)/shard_map/stage1/pallas_call | solution.py:373
  44.2 1.3 collective-permute-start.3
  45.5 9.8 %stage2.1 = (f32[2,2,256,2048]{3,2,1,0:T(8,128)}, bf16[2,2,256,1024]{3,2,1,0:T(8,128)(2,1)}, f32[2,256,256]{2,1,0:T(8,128)S(1)}) custom-call(s32[16]{0:T(128)S(1)} %copy-done.3, s32[16]{0:T(128)S(1)} %copy-done.4, s32[1]{0:T(128)S(6)} %copy.24.refs_2_, bf16[512,512]{1,0:T(8,128)(2,1)S(1)} %copy-done.1, ...), custom_call_target="tpu_custom_call", output_to_operand_aliasing={{0}: (14, {})} | custom-call | flops 3000000000 | bytes 8000000 | tf_op jit(solution)/shard_map/stage2/pallas_call | solution.py:373
  55.3 1.3 collective-permute-start.4
  56.7 2.4 %collective-permute-done.3.came_ref = bf16[2,2,256,1024]{3,2,1,0:T(8,128)(2,1)} collective-permute-done((bf16[2,2,256,1024]{3,2,1,0:T(8,128)(2,1)}, bf16[2,2,256,1024]{3,2,1,0:T(8,128)(2,1)}, u32[]{:S(2)}, u32[]{:S(2)}) %collective-permute-start.3) | collective-permute-done | bytes 2097184 | tf_op jit(solution)/shard_map/ppermute | solution.py:20
  59.1 4.9 %add0.1.held_ref = f32[2,2,256,2048]{3,2,1,0:T(8,128)} custom-call(f32[2,2,256,2048]{3,2,1,0:T(8,128)} %get-tuple-element.26.held_ref, bf16[2,2,256,1024]{3,2,1,0:T(8,128)(2,1)} %collective-permute-done.3.came_ref), custom_call_target="tpu_custom_call", output_to_operand_aliasing={{}: (0, {})} | custom-call | tf_op jit(solution)/shard_map/add0/pallas_call | solution.py:416
  64.0 30.6 %collective-permute-start.5 = (bf16[256,256]{1,0:T(8,128)(2,1)S(1)}, bf16[256,256]{1,0:T(8,128)(2,1)S(1)}, u32[]{:S(2)}, u32[]{:S(2)}) collective-permute-start(bf16[256,256]{1,0:T(8,128)(2,1)S(1)} %fusion.5), channel_id=1, source_target_pairs={{0,1},{1,0},{2,3},{3,2},{4,5},{5,4},{6,7},{7,6},{8,9},{9,8},{10,11... | collective-permute-start | bytes 393224 | tf_op jit(solution)/shard_map/ppermute | solution.py:434
  94.6 1.0 collective-permute-done.5
  95.6 0.6 collective-permute-start.6
  96.2 21.4 %collective-permute-done.6 = bf16[256,256]{1,0:T(8,128)(2,1)S(1)} collective-permute-done((bf16[256,256]{1,0:T(8,128)(2,1)S(1)}, bf16[256,256]{1,0:T(8,128)(2,1)S(1)}, u32[]{:S(2)}, u32[]{:S(2)}) %collective-permute-start.6) | collective-permute-done | bytes 131104 | tf_op jit(solution)/shard_map/ppermute | solution.py:434
  117.6 0.7 collective-permute-start.7
  118.4 4.7 %collective-permute-done.7 = bf16[256,256]{1,0:T(8,128)(2,1)S(1)} collective-permute-done((bf16[256,256]{1,0:T(8,128)(2,1)S(1)}, bf16[256,256]{1,0:T(8,128)(2,1)S(1)}, u32[]{:S(2)}, u32[]{:S(2)}) %collective-permute-start.7) | collective-permute-done | bytes 131104 | tf_op jit(solution)/shard_map/ppermute | solution.py:434
  123.1 0.1 collective-permute-start.8
  123.2 3.8 %collective-permute-done.8 = bf16[256,256]{1,0:T(8,128)(2,1)S(1)} collective-permute-done((bf16[256,256]{1,0:T(8,128)(2,1)S(1)}, bf16[256,256]{1,0:T(8,128)(2,1)S(1)}, u32[]{:S(2)}, u32[]{:S(2)}) %collective-permute-start.8) | collective-permute-done | bytes 131104 | tf_op jit(solution)/shard_map/ppermute | solution.py:434
  127.1 0.1 collective-permute-start.9
  127.2 3.9 %add8.1 = f32[2,2,256,2048]{3,2,1,0:T(8,128)} custom-call(f32[2,2,256,2048]{3,2,1,0:T(8,128)} %add0.1.held_ref, bf16[2,2,256,1024]{3,2,1,0:T(8,128)(2,1)S(1)} %collective-permute-done.4.came_ref), custom_call_target="tpu_custom_call", output_to_operand_aliasing={{}: (0, {})} | custom-call | tf_op jit(solution)/shard_map/add8/pallas_call | solution.py:416
  131.2 0.8 pad_maximum_fusion
  (26 shorter events, 0.4 us)
Async XLA Ops:
  4.2 11.3 %copy-start.7 = (f32[256]{0:T(256)S(1)}, f32[256]{0:T(256)}, u32[]{:S(2)}) copy-start(f32[256]{0:T(256)} %param.11) | copy-start | bytes 3076
  4.2 11.4 %copy-start.5 = (f32[256,256]{1,0:T(8,128)S(1)}, f32[256,256]{1,0:T(8,128)}, u32[]{:S(2)}) copy-start(f32[256,256]{1,0:T(8,128)} %constant.14.clone) | copy-start | bytes 786436
  4.2 11.4 %copy-start.6 = (f32[256,256]{1,0:T(8,128)S(1)}, f32[256,256]{1,0:T(8,128)}, u32[]{:S(2)}) copy-start(f32[256,256]{1,0:T(8,128)} %constant.15.clone) | copy-start | bytes 786436
  4.2 15.2 %collective-permute-start.1 = (bf16[2,2,256,640]{3,2,1,0:T(8,128)(2,1)}, bf16[2,2,256,640]{3,2,1,0:T(8,128)(2,1)}, u32[]{:S(2)}, u32[]{:S(2)}) collective-permute-start(bf16[2,2,256,640]{3,2,1,0:T(8,128)(2,1)} %get-tuple-element.32), channel_id=1, source_target_pairs={{1,0},{2,1},{3,2},{4,3},{5,4},{6,5},{7,6},{8,7},{9,8},{10,9},{11,1... | collective-permute-start | bytes 3932168 | tf_op jit(solution)/shard_map/ppermute | solution.py:20
  8.0 20.5 %collective-permute-start = (bf16[2,2,256,640]{3,2,1,0:T(8,128)(2,1)}, bf16[2,2,256,640]{3,2,1,0:T(8,128)(2,1)}, u32[]{:S(2)}, u32[]{:S(2)}) collective-permute-start(bf16[2,2,256,640]{3,2,1,0:T(8,128)(2,1)} %get-tuple-element.33), channel_id=1, source_target_pairs={{1,0},{2,1},{3,2},{4,3},{5,4},{6,5},{7,6},{8,7},{9,8},{10,9},{11,1... | collective-permute-start | bytes 3932168 | tf_op jit(solution)/shard_map/ppermute | solution.py:20
  13.1 31.1 %collective-permute-start.2 = (bf16[2,2,256,768]{3,2,1,0:T(8,128)(2,1)}, bf16[2,2,256,768]{3,2,1,0:T(8,128)(2,1)}, u32[]{:S(2)}, u32[]{:S(2)}) collective-permute-start(bf16[2,2,256,768]{3,2,1,0:T(8,128)(2,1)} %slice.19), channel_id=1, source_target_pairs={{1,0},{2,1},{3,2},{4,3},{5,4},{6,5},{7,6},{8,7},{9,8},{10,9},{11,1... | collective-permute-start | bytes 4718600 | tf_op jit(solution)/shard_map/ppermute | solution.py:20
  17.6 1.7 %copy-start = (f32[2,256,256]{2,1,0:T(8,128)S(1)}, f32[2,256,256]{2,1,0:T(8,128)}, u32[]{:S(2)}) copy-start(f32[2,256,256]{2,1,0:T(8,128)} %refs_7_.5) | copy-start | bytes 1572868
  17.6 1.7 %copy-start.1 = (bf16[512,512]{1,0:T(8,128)(2,1)S(1)}, bf16[512,512]{1,0:T(8,128)(2,1)}, u32[]{:S(2)}) copy-start(bf16[512,512]{1,0:T(8,128)(2,1)} %constant.26.refs_3_) | copy-start | bytes 1572868
  17.6 1.7 %copy-start.2 = (bf16[512,512]{1,0:T(8,128)(2,1)S(1)}, bf16[512,512]{1,0:T(8,128)(2,1)}, u32[]{:S(2)}) copy-start(bf16[512,512]{1,0:T(8,128)(2,1)} %constant.29.refs_4_) | copy-start | bytes 1572868
  17.7 1.7 %copy-start.3 = (s32[16]{0:T(128)S(1)}, s32[16]{0:T(128)}, u32[]{:S(2)}) copy-start(s32[16]{0:T(128)} %refs_0_.5) | copy-start | bytes 196
  17.7 1.7 %copy-start.4 = (s32[16]{0:T(128)S(1)}, s32[16]{0:T(128)}, u32[]{:S(2)}) copy-start(s32[16]{0:T(128)} %refs_1_.5) | copy-start | bytes 196
  44.2 14.9 %collective-permute-start.3 = (bf16[2,2,256,1024]{3,2,1,0:T(8,128)(2,1)}, bf16[2,2,256,1024]{3,2,1,0:T(8,128)(2,1)}, u32[]{:S(2)}, u32[]{:S(2)}) collective-permute-start(bf16[2,2,256,1024]{3,2,1,0:T(8,128)(2,1)} %get-tuple-element.27), channel_id=1, source_target_pairs={{0,1},{1,2},{2,3},{3,4},{4,5},{5,6},{6,7},{7,8},{8,9},{9,10},{10,1... | collective-permute-start | bytes 6291464 | tf_op jit(solution)/shard_map/ppermute | solution.py:20
  55.3 71.8 %collective-permute-start.4 = (bf16[2,2,256,1024]{3,2,1,0:T(8,128)(2,1)}, bf16[2,2,256,1024]{3,2,1,0:T(8,128)(2,1)S(1)}, u32[]{:S(2)}, u32[]{:S(2)}) collective-permute-start(bf16[2,2,256,1024]{3,2,1,0:T(8,128)(2,1)} %get-tuple-element.30), channel_id=1, source_target_pairs={{0,1},{1,2},{2,3},{3,4},{4,5},{5,6},{6,7},{7,8},{8,9},{9,10},{10,1... | collective-permute-start | bytes 6291464 | tf_op jit(solution)/shard_map/ppermute | solution.py:20
  64.0 31.5 %collective-permute-start.5 = (bf16[256,256]{1,0:T(8,128)(2,1)S(1)}, bf16[256,256]{1,0:T(8,128)(2,1)S(1)}, u32[]{:S(2)}, u32[]{:S(2)}) collective-permute-start(bf16[256,256]{1,0:T(8,128)(2,1)S(1)} %fusion.5), channel_id=1, source_target_pairs={{0,1},{1,0},{2,3},{3,2},{4,5},{5,4},{6,7},{7,6},{8,9},{9,8},{10,11... | collective-permute-start | bytes 393224 | tf_op jit(solution)/shard_map/ppermute | solution.py:434
  95.6 22.0 %collective-permute-start.6 = (bf16[256,256]{1,0:T(8,128)(2,1)S(1)}, bf16[256,256]{1,0:T(8,128)(2,1)S(1)}, u32[]{:S(2)}, u32[]{:S(2)}) collective-permute-start(bf16[256,256]{1,0:T(8,128)(2,1)S(1)} %fusion.1), channel_id=1, source_target_pairs={{0,4},{1,5},{2,6},{3,7},{4,0},{5,1},{6,2},{7,3},{8,12},{9,13},{10,... | collective-permute-start | bytes 393224 | tf_op jit(solution)/shard_map/ppermute | solution.py:434
  117.6 5.5 %collective-permute-start.7 = (bf16[256,256]{1,0:T(8,128)(2,1)S(1)}, bf16[256,256]{1,0:T(8,128)(2,1)S(1)}, u32[]{:S(2)}, u32[]{:S(2)}) collective-permute-start(bf16[256,256]{1,0:T(8,128)(2,1)S(1)} %add_convert_fusion.1), channel_id=1, source_target_pairs={{0,8},{1,9},{2,10},{3,11},{4,12},{5,13},{6,14},{7,15},{8,0},{9,1},... | collective-permute-start | bytes 393224 | tf_op jit(solution)/shard_map/ppermute | solution.py:434
  123.1 3.9 %collective-permute-start.8 = (bf16[256,256]{1,0:T(8,128)(2,1)S(1)}, bf16[256,256]{1,0:T(8,128)(2,1)S(1)}, u32[]{:S(2)}, u32[]{:S(2)}) collective-permute-start(bf16[256,256]{1,0:T(8,128)(2,1)S(1)} %add_convert_fusion), channel_id=1, source_target_pairs={{0,2},{1,3},{2,0},{3,1},{4,6},{5,7},{6,4},{7,5},{8,10},{9,11},{10,... | collective-permute-start | bytes 393224 | tf_op jit(solution)/shard_map/ppermute | solution.py:434
  127.1 4.0 %collective-permute-start.9 = (f32[256,256]{1,0:T(8,128)S(1)}, f32[256,256]{1,0:T(8,128)S(1)}, u32[]{:S(2)}, u32[]{:S(2)}) collective-permute-start(f32[256,256]{1,0:T(8,128)S(1)} %convert_add_fusion.1), channel_id=1, source_target_pairs={{0,1},{1,0},{2,3},{3,2},{4,5},{5,4},{6,7},{7,6},{8,9},{9,8},{10,11... | collective-permute-start | bytes 786440 | tf_op jit(solution)/shard_map/ppermute | solution.py:434

commit v5 on v4

--- a/solution.py
+++ b/solution.py
@@ -434,13 +434,20 @@
     return lax.ppermute(value, axis, [(k, k ^ step) for k in range(lax.axis_size(axis))])
 
 
-def sum_over(value, axis):
+def sum_over(value, axis, meanwhile):
     count = lax.axis_size(axis)
     steps = [1 << k for k in range(1, count.bit_length() - 1)]
     odd = lax.rem(lax.axis_index(axis), 2) == 1
     kept, given = jnp.where(odd, value[1], value[0]), jnp.where(odd, value[0], value[1])
     kept = kept.astype(BF).astype(F32) + exchanged(given.astype(BF), axis, 1).astype(F32)
-    for step in steps[1:] + steps[:1]:
+    for n in range(1, len(steps), 2):
+        mine = kept.astype(BF)
+        kept = mine.astype(F32) + exchanged(mine, axis, steps[n]).astype(F32)
+        if n + 1 < len(steps):
+            far, across = (exchanged(mine, axis, step) for step in (steps[n + 1], steps[n] ^ steps[n + 1]))
+            kept = kept + (far.astype(F32) + across.astype(F32))
+    kept = meanwhile(kept)
+    for step in steps[:1]:
         mine = kept.astype(BF)
         kept = mine.astype(F32) + exchanged(mine, axis, step).astype(F32)
     other = exchanged(kept, axis, 1)
@@ -472,16 +479,21 @@
             at = group[1]
     interior, _, probe_sum = past
     came = [(passed_along(chunk, "row", 1), first) for chunk, first in sent]
-    interior = add_chunk(interior, *came[0])
-    interior, probe_sum = lax.optimization_barrier((interior, probe_sum))
-    probe_total = sum_over(probe_sum, "row")
-    interior = add_chunk(interior, *came[1])
+    held = []
+
+    def meanwhile(kept):
+        kept, first = lax.optimization_barrier((kept, add_chunk(interior, *came[0])))
+        held.append(first)
+        return kept
+
+    probe_total = sum_over(probe_sum, "row", meanwhile)
+    interior = add_chunk(held[0], *came[1])
     return interior, probe_total
 
 
 def solution(mesh):
     return jax.shard_map(
-        functools.partial(body, (5, 10, 16), (1, 2)),
+        functools.partial(body, (5, 11, 16), (1, 2)),
         mesh=mesh,
         in_specs=(
             P("group", None, "row", None),

time: 130 us -> 139 us (1.069)
  the two profiles are of different devices: /device:TPU:31 before, /device:TPU:21 now
where the time goes in v5:
time: 139 us; the launch traced here: 137 us
  Pallas kernels  58.5 us (42%)
  waiting for transfers between devices  47.6 us (34%)
  starting transfers between devices  16.2 us (12%)
  local copies, waits for them, and re-layouts  7.25 us (5%)
  other arithmetic  3.17 us (2%)
  matrix products  2.72 us (2%)
  between operations  1.6 us (1%)
    pallas_call x3, Pallas kernels, run_stage(): pl.pallas_call(functools.partial(stage_kernel, plan, stage), out_shape=ou...  49.4 us
    ppermute x6, waiting for transfers between devices, exchanged(): lax.ppermute(value, axis, [(k, k ^ step) for k in range(lax.axis_size(axi...  33.4 us
    ppermute x5, waiting for transfers between devices, passed_along(): lax.ppermute(value, axis, [(source, source + steps) for source in range(f...  14.3 us
    ppermute x5, starting transfers between devices, passed_along(): lax.ppermute(value, axis, [(source, source + steps) for source in range(f...  11 us
    pallas_call x2, Pallas kernels, add_chunk(): pl.pallas_call(functools.partial(add_kernel, first_tile, tiles), out_shap...  9.1 us
    slice x2, local copies, waits for them, and re-layouts, body(): piece = source[:, :, :, start * LANES:end * LANES]  6.15 us
    ppermute x6, starting transfers between devices, exchanged(): lax.ppermute(value, axis, [(k, k ^ step) for k in range(lax.axis_size(axi...  5.24 us
  transfers between devices with their start and end apart: 11, of which 6 were waited for; matrix products, arithmetic and copies ran while one was open for 6% of the time, Pallas kernels for 43%

profile of v5, /device:TPU:21, one launch (start us, length us, event | category | flops | bytes accessed | tf_op | source)
XLA Modules:
  0.0 137.1 jit_solution(14953507748027698298)
XLA Ops:
  0.6 3.5 %fusion.14 = (bf16[2,2,256,640]{3,2,1,0:T(8,128)(2,1)}, bf16[2,2,256,640]{3,2,1,0:T(8,128)(2,1)}) fusion(bf16[2,2,256,2048]{3,2,1,0:T(8,128)(2,1)} %refs_9_.5), kind=kLoop, calls=%fused_computation.29 | loop fusion | bytes 5242880 | tf_op jit(solution)/shard_map/slice | solution.py:462
  4.1 2.7 %collective-permute-start.1 = (bf16[2,2,256,640]{3,2,1,0:T(8,128)(2,1)}, bf16[2,2,256,640]{3,2,1,0:T(8,128)(2,1)}, u32[]{:S(2)}, u32[]{:S(2)}) collective-permute-start(bf16[2,2,256,640]{3,2,1,0:T(8,128)(2,1)} %get-tuple-element.33), channel_id=1, source_target_pairs={{1,0},{2,1},{3,2},{4,3},{5,4},{6,5},{7,6},{8,7},{9,8},{10,9},{11,1... | collective-permute-start | bytes 3932168 | tf_op jit(solution)/shard_map/ppermute | solution.py:20
  6.8 2.7 %slice.17 = bf16[2,2,256,768]{3,2,1,0:T(8,128)(2,1)} slice(bf16[2,2,256,2048]{3,2,1,0:T(8,128)(2,1)} %refs_9_.5), slice={[0:2], [0:2], [0:256], [640:1408]} | slice | bytes 3145728 | tf_op jit(solution)/shard_map/slice | solution.py:462
  9.5 1.9 %collective-permute-start = (bf16[2,2,256,768]{3,2,1,0:T(8,128)(2,1)}, bf16[2,2,256,768]{3,2,1,0:T(8,128)(2,1)}, u32[]{:S(2)}, u32[]{:S(2)}) collective-permute-start(bf16[2,2,256,768]{3,2,1,0:T(8,128)(2,1)} %slice.17), channel_id=1, source_target_pairs={{1,0},{2,1},{3,2},{4,3},{5,4},{6,5},{7,6},{8,7},{9,8},{10,9},{11,1... | collective-permute-start | bytes 4718600 | tf_op jit(solution)/shard_map/ppermute | solution.py:20
  11.4 2.5 %collective-permute-start.2 = (bf16[2,2,256,640]{3,2,1,0:T(8,128)(2,1)}, bf16[2,2,256,640]{3,2,1,0:T(8,128)(2,1)}, u32[]{:S(2)}, u32[]{:S(2)}) collective-permute-start(bf16[2,2,256,640]{3,2,1,0:T(8,128)(2,1)} %get-tuple-element.32), channel_id=1, source_target_pairs={{1,0},{2,1},{3,2},{4,3},{5,4},{6,5},{7,6},{8,7},{9,8},{10,9},{11,1... | collective-permute-start | bytes 3932168 | tf_op jit(solution)/shard_map/ppermute | solution.py:20
  14.0 0.7 fusion.3
  14.7 0.7 fusion
  15.4 0.7 fusion.2
  16.1 0.7 negate_convert_fusion
  16.9 0.2 copy.18.refs_5_
  17.8 6.6 %collective-permute-done.1.refs_10_.refs_11_ = bf16[2,2,256,640]{3,2,1,0:T(8,128)(2,1)} collective-permute-done((bf16[2,2,256,640]{3,2,1,0:T(8,128)(2,1)}, bf16[2,2,256,640]{3,2,1,0:T(8,128)(2,1)}, u32[]{:S(2)}, u32[]{:S(2)}) %collective-permute-start.1) | collective-permute-done | bytes 1310752 | tf_op jit(solution)/shard_map/ppermute | solution.py:20
  24.4 9.2 %stage0.1 = (f32[2,2,256,2048]{3,2,1,0:T(8,128)}, bf16[2,2,256,1152]{3,2,1,0:T(8,128)(2,1)}, f32[2,2,2,512,128]{4,3,2,1,0:T(8,128)}, f32[2,256,256]{2,1,0:T(8,128)S(1)}) custom-call(s32[16]{0:T(128)S(1)} %copy-done.6, s32[16]{0:T(128)S(1)} %copy-done.7, s32[1]{0:T(128)S(6)} %copy.24.refs_2_, bf16[512,512]{1,0:T(8,128)(2,1)S(1)} %copy-done.1, ...), custom_call_target="tpu_custom_call" | custom-call | flops 3000000000 | bytes 8000000 | tf_op jit(solution)/shard_map/stage0/pallas_call | solution.py:373
  33.6 7.6 %collective-permute-done.refs_10_.refs_11_ = bf16[2,2,256,768]{3,2,1,0:T(8,128)(2,1)} collective-permute-done((bf16[2,2,256,768]{3,2,1,0:T(8,128)(2,1)}, bf16[2,2,256,768]{3,2,1,0:T(8,128)(2,1)}, u32[]{:S(2)}, u32[]{:S(2)}) %collective-permute-start) | collective-permute-done | bytes 1572896 | tf_op jit(solution)/shard_map/ppermute | solution.py:20
  41.2 19.6 %stage1.1 = (f32[2,2,256,2048]{3,2,1,0:T(8,128)}, bf16[2,2,256,1152]{3,2,1,0:T(8,128)(2,1)}, f32[2,2,2,512,128]{4,3,2,1,0:T(8,128)}, f32[2,256,256]{2,1,0:T(8,128)S(1)}) custom-call(s32[16]{0:T(128)S(1)} %copy-done.6, s32[16]{0:T(128)S(1)} %copy-done.7, s32[1]{0:T(128)S(6)} %copy.24.refs_2_, ...), custom_call_target="tpu_custom_call", output_to_operand_aliasing={{0}: (14, {}), {1}: (15, {})} | custom-call | flops 3000000000 | bytes 8000000 | tf_op jit(solution)/shard_map/stage1/pallas_call | solution.py:373
  60.8 1.9 %collective-permute-start.7 = (bf16[2,2,256,1152]{3,2,1,0:T(8,128)(2,1)}, bf16[2,2,256,1152]{3,2,1,0:T(8,128)(2,1)S(1)}, u32[]{:S(2)}, u32[]{:S(2)}) collective-permute-start(bf16[2,2,256,1152]{3,2,1,0:T(8,128)(2,1)} %get-tuple-element.28), channel_id=1, source_target_pairs={{0,1},{1,2},{2,3},{3,4},{4,5},{5,6},{6,7},{7,8},{8,9},{9,10},{10,1... | collective-permute-start | bytes 7077896 | tf_op jit(solution)/shard_map/ppermute | solution.py:20
  62.8 20.6 %stage2.1 = (f32[2,2,256,2048]{3,2,1,0:T(8,128)}, bf16[2,2,256,896]{3,2,1,0:T(8,128)(2,1)}, f32[2,256,256]{2,1,0:T(8,128)S(1)}) custom-call(s32[16]{0:T(128)S(1)} %copy-done.6, s32[16]{0:T(128)S(1)} %copy-done.7, s32[1]{0:T(128)S(6)} %copy.24.refs_2_, bf16[512,512]{1,0:T(8,128)(2,1)S(1)} %copy-done.2, ...), custom_call_target="tpu_custom_call", output_to_operand_aliasing={{0}: (14, {})} | custom-call | flops 3000000000 | bytes 8000000 | tf_op jit(solution)/shard_map/stage2/pallas_call | solution.py:373
  83.4 0.8 copy-done.5
  84.2 1.9 %collective-permute-start.8 = (bf16[2,2,256,896]{3,2,1,0:T(8,128)(2,1)}, bf16[2,2,256,896]{3,2,1,0:T(8,128)(2,1)}, u32[]{:S(2)}, u32[]{:S(2)}) collective-permute-start(bf16[2,2,256,896]{3,2,1,0:T(8,128)(2,1)} %get-tuple-element.30), channel_id=1, source_target_pairs={{0,1},{1,2},{2,3},{3,4},{4,5},{5,6},{6,7},{7,8},{8,9},{9,10},{10,1... | collective-permute-start | bytes 5505032 | tf_op jit(solution)/shard_map/ppermute | solution.py:20
  86.1 1.1 fusion.5
  87.2 0.6 collective-permute-start.3
  87.8 2.3 %collective-permute-done.3 = bf16[256,256]{1,0:T(8,128)(2,1)S(1)} collective-permute-done((bf16[256,256]{1,0:T(8,128)(2,1)S(1)}, bf16[256,256]{1,0:T(8,128)(2,1)S(1)}, u32[]{:S(2)}, u32[]{:S(2)}) %collective-permute-start.3) | collective-permute-done | bytes 131104 | tf_op jit(solution)/shard_map/ppermute | solution.py:434
  90.1 1.1 fusion.1
  91.1 0.1 collective-permute-start.4
  91.2 4.5 %collective-permute-start.5 = (bf16[256,256]{1,0:T(8,128)(2,1)S(1)}, bf16[256,256]{1,0:T(8,128)(2,1)S(1)}, u32[]{:S(2)}, u32[]{:S(2)}) collective-permute-start(bf16[256,256]{1,0:T(8,128)(2,1)S(1)} %fusion.1), channel_id=1, source_target_pairs={{0,8},{1,9},{2,10},{3,11},{4,12},{5,13},{6,14},{7,15},{8,0},{9,1},... | collective-permute-start | bytes 393224 | tf_op jit(solution)/shard_map/ppermute | solution.py:434
  95.7 19.7 %collective-permute-done.4 = bf16[256,256]{1,0:T(8,128)(2,1)S(1)} collective-permute-done((bf16[256,256]{1,0:T(8,128)(2,1)S(1)}, bf16[256,256]{1,0:T(8,128)(2,1)S(1)}, u32[]{:S(2)}, u32[]{:S(2)}) %collective-permute-start.4) | collective-permute-done | bytes 131104 | tf_op jit(solution)/shard_map/ppermute | solution.py:434
  115.4 7.5 %collective-permute-done.6 = bf16[256,256]{1,0:T(8,128)(2,1)S(1)} collective-permute-done((bf16[256,256]{1,0:T(8,128)(2,1)S(1)}, bf16[256,256]{1,0:T(8,128)(2,1)S(1)}, u32[]{:S(2)}, u32[]{:S(2)}) %collective-permute-start.6) | collective-permute-done | bytes 131104 | tf_op jit(solution)/shard_map/ppermute | solution.py:434
  123.0 4.5 %add0.1.held_ref = f32[2,2,256,2048]{3,2,1,0:T(8,128)} custom-call(f32[2,2,256,2048]{3,2,1,0:T(8,128)} %get-tuple-element.27.held_ref, bf16[2,2,256,1152]{3,2,1,0:T(8,128)(2,1)S(1)} %collective-permute-done.7.came_ref), custom_call_target="tpu_custom_call", output_to_operand_aliasing={{}: (0, {})} | custom-call | tf_op jit(solution)/shard_map/add0/pallas_call | solution.py:416
  127.5 0.1 collective-permute-start.9
  127.6 3.8 %collective-permute-done.9 = bf16[256,256]{1,0:T(8,128)(2,1)S(1)} collective-permute-done((bf16[256,256]{1,0:T(8,128)(2,1)S(1)}, bf16[256,256]{1,0:T(8,128)(2,1)S(1)}, u32[]{:S(2)}, u32[]{:S(2)}) %collective-permute-start.9) | collective-permute-done | bytes 131104 | tf_op jit(solution)/shard_map/ppermute | solution.py:434
  131.5 0.1 collective-permute-start.10
  131.6 4.6 %add9.1 = f32[2,2,256,2048]{3,2,1,0:T(8,128)} custom-call(f32[2,2,256,2048]{3,2,1,0:T(8,128)} %add0.1.held_ref, bf16[2,2,256,896]{3,2,1,0:T(8,128)(2,1)} %collective-permute-done.8.came_ref), custom_call_target="tpu_custom_call", output_to_operand_aliasing={{}: (0, {})} | custom-call | tf_op jit(solution)/shard_map/add9/pallas_call | solution.py:416
  136.2 0.8 pad_maximum_fusion
  (33 shorter events, 0.3 us)
Async XLA Ops:
  4.1 9.8 %copy-start.10 = (f32[256]{0:T(256)S(1)}, f32[256]{0:T(256)}, u32[]{:S(2)}) copy-start(f32[256]{0:T(256)} %param.11) | copy-start | bytes 3076
  4.1 9.9 %copy-start.8 = (f32[256,256]{1,0:T(8,128)S(1)}, f32[256,256]{1,0:T(8,128)}, u32[]{:S(2)}) copy-start(f32[256,256]{1,0:T(8,128)} %constant.14.clone) | copy-start | bytes 786436
  4.1 9.9 %copy-start.9 = (f32[256,256]{1,0:T(8,128)S(1)}, f32[256,256]{1,0:T(8,128)}, u32[]{:S(2)}) copy-start(f32[256,256]{1,0:T(8,128)} %constant.15.clone) | copy-start | bytes 786436
  4.1 20.3 %collective-permute-start.1 = (bf16[2,2,256,640]{3,2,1,0:T(8,128)(2,1)}, bf16[2,2,256,640]{3,2,1,0:T(8,128)(2,1)}, u32[]{:S(2)}, u32[]{:S(2)}) collective-permute-start(bf16[2,2,256,640]{3,2,1,0:T(8,128)(2,1)} %get-tuple-element.33), channel_id=1, source_target_pairs={{1,0},{2,1},{3,2},{4,3},{5,4},{6,5},{7,6},{8,7},{9,8},{10,9},{11,1... | collective-permute-start | bytes 3932168 | tf_op jit(solution)/shard_map/ppermute | solution.py:20
  9.5 31.7 %collective-permute-start = (bf16[2,2,256,768]{3,2,1,0:T(8,128)(2,1)}, bf16[2,2,256,768]{3,2,1,0:T(8,128)(2,1)}, u32[]{:S(2)}, u32[]{:S(2)}) collective-permute-start(bf16[2,2,256,768]{3,2,1,0:T(8,128)(2,1)} %slice.17), channel_id=1, source_target_pairs={{1,0},{2,1},{3,2},{4,3},{5,4},{6,5},{7,6},{8,7},{9,8},{10,9},{11,1... | collective-permute-start | bytes 4718600 | tf_op jit(solution)/shard_map/ppermute | solution.py:20
  11.4 49.4 %collective-permute-start.2 = (bf16[2,2,256,640]{3,2,1,0:T(8,128)(2,1)}, bf16[2,2,256,640]{3,2,1,0:T(8,128)(2,1)}, u32[]{:S(2)}, u32[]{:S(2)}) collective-permute-start(bf16[2,2,256,640]{3,2,1,0:T(8,128)(2,1)} %get-tuple-element.32), channel_id=1, source_target_pairs={{1,0},{2,1},{3,2},{4,3},{5,4},{6,5},{7,6},{8,7},{9,8},{10,9},{11,1... | collective-permute-start | bytes 3932168 | tf_op jit(solution)/shard_map/ppermute | solution.py:20
  16.1 8.3 %copy-start = (f32[2,256,256]{2,1,0:T(8,128)S(1)}, f32[2,256,256]{2,1,0:T(8,128)}, u32[]{:S(2)}) copy-start(f32[2,256,256]{2,1,0:T(8,128)} %refs_7_.5) | copy-start | bytes 1572868
  16.1 8.3 %copy-start.1 = (bf16[512,512]{1,0:T(8,128)(2,1)S(1)}, bf16[512,512]{1,0:T(8,128)(2,1)}, u32[]{:S(2)}) copy-start(bf16[512,512]{1,0:T(8,128)(2,1)} %constant.26.refs_3_) | copy-start | bytes 1572868
  16.1 8.3 %copy-start.3 = (bf16[512,512]{1,0:T(8,128)(2,1)S(1)}, bf16[512,512]{1,0:T(8,128)(2,1)}, u32[]{:S(2)}) copy-start(bf16[512,512]{1,0:T(8,128)(2,1)} %constant.29.refs_4_) | copy-start | bytes 1572868
  16.1 8.3 %copy-start.6 = (s32[16]{0:T(128)S(1)}, s32[16]{0:T(128)}, u32[]{:S(2)}) copy-start(s32[16]{0:T(128)} %refs_0_.5) | copy-start | bytes 196
  16.1 8.3 %copy-start.7 = (s32[16]{0:T(128)S(1)}, s32[16]{0:T(128)}, u32[]{:S(2)}) copy-start(s32[16]{0:T(128)} %refs_1_.5) | copy-start | bytes 196
  41.2 21.5 %copy-start.2 = (bf16[512,512]{1,0:T(8,128)(2,1)S(1)}, bf16[512,512]{1,0:T(8,128)(2,1)}, u32[]{:S(2)}) copy-start(bf16[512,512]{1,0:T(8,128)(2,1)} %constant.26.refs_3_) | copy-start | bytes 1572868
  41.2 21.5 %copy-start.4 = (bf16[512,512]{1,0:T(8,128)(2,1)S(1)}, bf16[512,512]{1,0:T(8,128)(2,1)}, u32[]{:S(2)}) copy-start(bf16[512,512]{1,0:T(8,128)(2,1)} %constant.29.refs_4_) | copy-start | bytes 1572868
  60.8 62.2 %collective-permute-start.7 = (bf16[2,2,256,1152]{3,2,1,0:T(8,128)(2,1)}, bf16[2,2,256,1152]{3,2,1,0:T(8,128)(2,1)S(1)}, u32[]{:S(2)}, u32[]{:S(2)}) collective-permute-start(bf16[2,2,256,1152]{3,2,1,0:T(8,128)(2,1)} %get-tuple-element.28), channel_id=1, source_target_pairs={{0,1},{1,2},{2,3},{3,4},{4,5},{5,6},{6,7},{7,8},{8,9},{9,10},{10,1... | collective-permute-start | bytes 7077896 | tf_op jit(solution)/shard_map/ppermute | solution.py:20
  83.4 0.8 copy-start.5
  84.2 47.3 %collective-permute-start.8 = (bf16[2,2,256,896]{3,2,1,0:T(8,128)(2,1)}, bf16[2,2,256,896]{3,2,1,0:T(8,128)(2,1)}, u32[]{:S(2)}, u32[]{:S(2)}) collective-permute-start(bf16[2,2,256,896]{3,2,1,0:T(8,128)(2,1)} %get-tuple-element.30), channel_id=1, source_target_pairs={{0,1},{1,2},{2,3},{3,4},{4,5},{5,6},{6,7},{7,8},{8,9},{9,10},{10,1... | collective-permute-start | bytes 5505032 | tf_op jit(solution)/shard_map/ppermute | solution.py:20
  87.2 2.9 %collective-permute-start.3 = (bf16[256,256]{1,0:T(8,128)(2,1)S(1)}, bf16[256,256]{1,0:T(8,128)(2,1)S(1)}, u32[]{:S(2)}, u32[]{:S(2)}) collective-permute-start(bf16[256,256]{1,0:T(8,128)(2,1)S(1)} %fusion.5), channel_id=1, source_target_pairs={{0,1},{1,0},{2,3},{3,2},{4,5},{5,4},{6,7},{7,6},{8,9},{9,8},{10,11... | collective-permute-start | bytes 393224 | tf_op jit(solution)/shard_map/ppermute | solution.py:434
  91.1 24.3 %collective-permute-start.4 = (bf16[256,256]{1,0:T(8,128)(2,1)S(1)}, bf16[256,256]{1,0:T(8,128)(2,1)S(1)}, u32[]{:S(2)}, u32[]{:S(2)}) collective-permute-start(bf16[256,256]{1,0:T(8,128)(2,1)S(1)} %fusion.1), channel_id=1, source_target_pairs={{0,4},{1,5},{2,6},{3,7},{4,0},{5,1},{6,2},{7,3},{8,12},{9,13},{10,... | collective-permute-start | bytes 393224 | tf_op jit(solution)/shard_map/ppermute | solution.py:434
  91.2 24.2 %collective-permute-start.5 = (bf16[256,256]{1,0:T(8,128)(2,1)S(1)}, bf16[256,256]{1,0:T(8,128)(2,1)S(1)}, u32[]{:S(2)}, u32[]{:S(2)}) collective-permute-start(bf16[256,256]{1,0:T(8,128)(2,1)S(1)} %fusion.1), channel_id=1, source_target_pairs={{0,8},{1,9},{2,10},{3,11},{4,12},{5,13},{6,14},{7,15},{8,0},{9,1},... | collective-permute-start | bytes 393224 | tf_op jit(solution)/shard_map/ppermute | solution.py:434
  95.7 27.3 %collective-permute-start.6 = (bf16[256,256]{1,0:T(8,128)(2,1)S(1)}, bf16[256,256]{1,0:T(8,128)(2,1)S(1)}, u32[]{:S(2)}, u32[]{:S(2)}) collective-permute-start(bf16[256,256]{1,0:T(8,128)(2,1)S(1)} %fusion.1), channel_id=1, source_target_pairs={{0,12},{1,13},{2,14},{3,15},{4,8},{5,9},{6,10},{7,11},{8,4},{9,5},... | collective-permute-start | bytes 393224 | tf_op jit(solution)/shard_map/ppermute | solution.py:434
  127.5 3.9 %collective-permute-start.9 = (bf16[256,256]{1,0:T(8,128)(2,1)S(1)}, bf16[256,256]{1,0:T(8,128)(2,1)S(1)}, u32[]{:S(2)}, u32[]{:S(2)}) collective-permute-start(bf16[256,256]{1,0:T(8,128)(2,1)S(1)} %add_add_fusion), channel_id=1, source_target_pairs={{0,2},{1,3},{2,0},{3,1},{4,6},{5,7},{6,4},{7,5},{8,10},{9,11},{10,... | collective-permute-start | bytes 393224 | tf_op jit(solution)/shard_map/ppermute | solution.py:434
  131.5 4.7 %collective-permute-start.10 = (f32[256,256]{1,0:T(8,128)S(1)}, f32[256,256]{1,0:T(8,128)S(1)}, u32[]{:S(2)}, u32[]{:S(2)}) collective-permute-start(f32[256,256]{1,0:T(8,128)S(1)} %convert_add_fusion.1), channel_id=1, source_target_pairs={{0,1},{1,0},{2,3},{3,2},{4,5},{5,4},{6,7},{7,6},{8,9},{9,8},{10,11... | collective-permute-start | bytes 786440 | tf_op jit(solution)/shard_map/ppermute | solution.py:434

commit v6 on v4

--- a/solution.py
+++ b/solution.py
@@ -440,7 +440,13 @@
     odd = lax.rem(lax.axis_index(axis), 2) == 1
     kept, given = jnp.where(odd, value[1], value[0]), jnp.where(odd, value[0], value[1])
     kept = kept.astype(BF).astype(F32) + exchanged(given.astype(BF), axis, 1).astype(F32)
-    for step in steps[1:] + steps[:1]:
+    for n in range(1, len(steps), 2):
+        mine = kept.astype(BF)
+        kept = mine.astype(F32) + exchanged(mine, axis, steps[n]).astype(F32)
+        if n + 1 < len(steps):
+            far, across = (exchanged(mine, axis, step) for step in (steps[n + 1], steps[n] ^ steps[n + 1]))
+            kept = kept + (far.astype(F32) + across.astype(F32))
+    for step in steps[:1]:
         mine = kept.astype(BF)
         kept = mine.astype(F32) + exchanged(mine, axis, step).astype(F32)
     other = exchanged(kept, axis, 1)

time: 130 us -> 135 us (1.038)
  the two profiles are of different devices: /device:TPU:31 before, /device:TPU:21 now
where the time goes in v6:
time: 135 us; the launch traced here: 132 us
  Pallas kernels  62.7 us (46%)
  waiting for transfers between devices  41.3 us (31%)
  starting transfers between devices  16.5 us (12%)
  local copies, waits for them, and re-layouts  6.61 us (5%)
  matrix products  2.72 us (2%)
  between operations  1.59 us (1%)
    pallas_call x3, Pallas kernels, run_stage(): pl.pallas_call(functools.partial(stage_kernel, plan, stage), out_shape=ou...  53.8 us
    ppermute x6, waiting for transfers between devices, exchanged(): lax.ppermute(value, axis, [(k, k ^ step) for k in range(lax.axis_size(axi...  27.2 us
    ppermute x5, waiting for transfers between devices, passed_along(): lax.ppermute(value, axis, [(source, source + steps) for source in range(f...  14.1 us
    ppermute x5, starting transfers between devices, passed_along(): lax.ppermute(value, axis, [(source, source + steps) for source in range(f...  13.1 us
    pallas_call x2, Pallas kernels, add_chunk(): pl.pallas_call(functools.partial(add_kernel, first_tile, tiles), out_shap...  8.81 us
    slice x2, local copies, waits for them, and re-layouts, body(): piece = source[:, :, :, start * LANES:end * LANES]  6.31 us
    ppermute x6, starting transfers between devices, exchanged(): lax.ppermute(value, axis, [(k, k ^ step) for k in range(lax.axis_size(axi...  3.4 us
  transfers between devices with their start and end apart: 11, of which 6 were waited for; matrix products, arithmetic and copies ran while one was open for 5% of the time, Pallas kernels for 47%

profile of v6, /device:TPU:21, one launch (start us, length us, event | category | flops | bytes accessed | tf_op | source)
XLA Modules:
  0.0 132.5 jit_solution(1417899833530789201)
XLA Ops:
  0.6 3.5 %fusion.14 = (bf16[2,2,256,640]{3,2,1,0:T(8,128)(2,1)}, bf16[2,2,256,640]{3,2,1,0:T(8,128)(2,1)}) fusion(bf16[2,2,256,2048]{3,2,1,0:T(8,128)(2,1)} %refs_9_.5), kind=kLoop, calls=%fused_computation.29 | loop fusion | bytes 5242880 | tf_op jit(solution)/shard_map/slice | solution.py:461
  4.2 2.7 %collective-permute-start.1 = (bf16[2,2,256,640]{3,2,1,0:T(8,128)(2,1)}, bf16[2,2,256,640]{3,2,1,0:T(8,128)(2,1)}, u32[]{:S(2)}, u32[]{:S(2)}) collective-permute-start(bf16[2,2,256,640]{3,2,1,0:T(8,128)(2,1)} %get-tuple-element.32), channel_id=1, source_target_pairs={{1,0},{2,1},{3,2},{4,3},{5,4},{6,5},{7,6},{8,7},{9,8},{10,9},{11,1... | collective-permute-start | bytes 3932168 | tf_op jit(solution)/shard_map/ppermute | solution.py:20
  6.9 1.9 %collective-permute-start = (bf16[2,2,256,640]{3,2,1,0:T(8,128)(2,1)}, bf16[2,2,256,640]{3,2,1,0:T(8,128)(2,1)}, u32[]{:S(2)}, u32[]{:S(2)}) collective-permute-start(bf16[2,2,256,640]{3,2,1,0:T(8,128)(2,1)} %get-tuple-element.33), channel_id=1, source_target_pairs={{1,0},{2,1},{3,2},{4,3},{5,4},{6,5},{7,6},{8,7},{9,8},{10,9},{11,1... | collective-permute-start | bytes 3932168 | tf_op jit(solution)/shard_map/ppermute | solution.py:20
  8.8 2.8 %slice.19 = bf16[2,2,256,768]{3,2,1,0:T(8,128)(2,1)} slice(bf16[2,2,256,2048]{3,2,1,0:T(8,128)(2,1)} %refs_9_.5), slice={[0:2], [0:2], [0:256], [1280:2048]} | slice | bytes 3145728 | tf_op jit(solution)/shard_map/slice | solution.py:461
  11.6 2.5 %collective-permute-start.2 = (bf16[2,2,256,768]{3,2,1,0:T(8,128)(2,1)}, bf16[2,2,256,768]{3,2,1,0:T(8,128)(2,1)}, u32[]{:S(2)}, u32[]{:S(2)}) collective-permute-start(bf16[2,2,256,768]{3,2,1,0:T(8,128)(2,1)} %slice.19), channel_id=1, source_target_pairs={{1,0},{2,1},{3,2},{4,3},{5,4},{6,5},{7,6},{8,7},{9,8},{10,9},{11,1... | collective-permute-start | bytes 4718600 | tf_op jit(solution)/shard_map/ppermute | solution.py:20
  14.2 0.7 fusion.2
  14.9 0.7 fusion.3
  15.6 0.7 fusion
  16.2 0.0 copy-start.1
  16.3 0.7 negate_convert_fusion
  17.0 0.2 copy.18.refs_5_
  17.9 6.5 %collective-permute-done.1.refs_10_.refs_11_ = bf16[2,2,256,640]{3,2,1,0:T(8,128)(2,1)} collective-permute-done((bf16[2,2,256,640]{3,2,1,0:T(8,128)(2,1)}, bf16[2,2,256,640]{3,2,1,0:T(8,128)(2,1)}, u32[]{:S(2)}, u32[]{:S(2)}) %collective-permute-start.1) | collective-permute-done | bytes 1310752 | tf_op jit(solution)/shard_map/ppermute | solution.py:20
  24.5 13.7 %stage0.1 = (f32[2,2,256,2048]{3,2,1,0:T(8,128)}, bf16[2,2,256,1024]{3,2,1,0:T(8,128)(2,1)}, f32[2,2,2,512,128]{4,3,2,1,0:T(8,128)}, f32[2,256,256]{2,1,0:T(8,128)S(1)}) custom-call(s32[16]{0:T(128)S(1)} %copy-done.3, s32[16]{0:T(128)S(1)} %copy-done.4, s32[1]{0:T(128)S(6)} %copy.24.refs_2_, bf16[512,512]{1,0:T(8,128)(2,1)S(1)} %copy-done.1, ...), custom_call_target="tpu_custom_call" | custom-call | flops 3000000000 | bytes 8000000 | tf_op jit(solution)/shard_map/stage0/pallas_call | solution.py:373
  38.2 0.3 collective-permute-done.refs_10_.refs_11_
  38.5 9.6 %stage1.1 = (f32[2,2,256,2048]{3,2,1,0:T(8,128)}, bf16[2,2,256,1024]{3,2,1,0:T(8,128)(2,1)}, f32[2,2,2,512,128]{4,3,2,1,0:T(8,128)}, f32[2,256,256]{2,1,0:T(8,128)S(1)}) custom-call(s32[16]{0:T(128)S(1)} %copy-done.3, s32[16]{0:T(128)S(1)} %copy-done.4, s32[1]{0:T(128)S(6)} %copy.24.refs_2_, ...), custom_call_target="tpu_custom_call", output_to_operand_aliasing={{0}: (14, {}), {1}: (15, {})} | custom-call | flops 3000000000 | bytes 8000000 | tf_op jit(solution)/shard_map/stage1/pallas_call | solution.py:373
  48.1 7.3 %collective-permute-done.2.refs_10_ = bf16[2,2,256,768]{3,2,1,0:T(8,128)(2,1)} collective-permute-done((bf16[2,2,256,768]{3,2,1,0:T(8,128)(2,1)}, bf16[2,2,256,768]{3,2,1,0:T(8,128)(2,1)}, u32[]{:S(2)}, u32[]{:S(2)}) %collective-permute-start.2) | collective-permute-done | bytes 1572896 | tf_op jit(solution)/shard_map/ppermute | solution.py:20
  55.3 4.1 %collective-permute-start.3 = (bf16[2,2,256,1024]{3,2,1,0:T(8,128)(2,1)}, bf16[2,2,256,1024]{3,2,1,0:T(8,128)(2,1)}, u32[]{:S(2)}, u32[]{:S(2)}) collective-permute-start(bf16[2,2,256,1024]{3,2,1,0:T(8,128)(2,1)} %get-tuple-element.27), channel_id=1, source_target_pairs={{0,1},{1,2},{2,3},{3,4},{4,5},{5,6},{6,7},{7,8},{8,9},{9,10},{10,1... | collective-permute-start | bytes 6291464 | tf_op jit(solution)/shard_map/ppermute | solution.py:20
  59.4 30.6 %stage2.1 = (f32[2,2,256,2048]{3,2,1,0:T(8,128)}, bf16[2,2,256,1024]{3,2,1,0:T(8,128)(2,1)}, f32[2,256,256]{2,1,0:T(8,128)S(1)}) custom-call(s32[16]{0:T(128)S(1)} %copy-done.3, s32[16]{0:T(128)S(1)} %copy-done.4, s32[1]{0:T(128)S(6)} %copy.24.refs_2_, bf16[512,512]{1,0:T(8,128)(2,1)S(1)} %copy-done.1, ...), custom_call_target="tpu_custom_call", output_to_operand_aliasing={{0}: (14, {})} | custom-call | flops 3000000000 | bytes 8000000 | tf_op jit(solution)/shard_map/stage2/pallas_call | solution.py:373
  90.0 1.9 %collective-permute-start.4 = (bf16[2,2,256,1024]{3,2,1,0:T(8,128)(2,1)}, bf16[2,2,256,1024]{3,2,1,0:T(8,128)(2,1)S(1)}, u32[]{:S(2)}, u32[]{:S(2)}) collective-permute-start(bf16[2,2,256,1024]{3,2,1,0:T(8,128)(2,1)} %get-tuple-element.30), channel_id=1, source_target_pairs={{0,1},{1,2},{2,3},{3,4},{4,5},{5,6},{6,7},{7,8},{8,9},{9,10},{10,1... | collective-permute-start | bytes 6291464 | tf_op jit(solution)/shard_map/ppermute | solution.py:20
  92.0 4.9 %add0.1.held_ref = f32[2,2,256,2048]{3,2,1,0:T(8,128)} custom-call(f32[2,2,256,2048]{3,2,1,0:T(8,128)} %get-tuple-element.26.held_ref, bf16[2,2,256,1024]{3,2,1,0:T(8,128)(2,1)} %collective-permute-done.3.came_ref), custom_call_target="tpu_custom_call", output_to_operand_aliasing={{}: (0, {})} | custom-call | tf_op jit(solution)/shard_map/add0/pallas_call | solution.py:416
  96.9 0.6 collective-permute-start.5
  97.4 1.0 collective-permute-done.5
  98.5 0.1 collective-permute-start.6
  98.6 0.1 collective-permute-start.7
  98.6 2.6 %collective-permute-start.8 = (bf16[256,256]{1,0:T(8,128)(2,1)S(1)}, bf16[256,256]{1,0:T(8,128)(2,1)S(1)}, u32[]{:S(2)}, u32[]{:S(2)}) collective-permute-start(bf16[256,256]{1,0:T(8,128)(2,1)S(1)} %fusion.1), channel_id=1, source_target_pairs={{0,12},{1,13},{2,14},{3,15},{4,8},{5,9},{6,10},{7,11},{8,4},{9,5},... | collective-permute-start | bytes 393224 | tf_op jit(solution)/shard_map/ppermute | solution.py:434
  101.2 22.4 %collective-permute-done.6 = bf16[256,256]{1,0:T(8,128)(2,1)S(1)} collective-permute-done((bf16[256,256]{1,0:T(8,128)(2,1)S(1)}, bf16[256,256]{1,0:T(8,128)(2,1)S(1)}, u32[]{:S(2)}, u32[]{:S(2)}) %collective-permute-start.6) | collective-permute-done | bytes 131104 | tf_op jit(solution)/shard_map/ppermute | solution.py:434
  123.6 0.1 add_convert_fusion
  123.6 0.1 collective-permute-start.9
  123.7 3.8 %collective-permute-done.9 = bf16[256,256]{1,0:T(8,128)(2,1)S(1)} collective-permute-done((bf16[256,256]{1,0:T(8,128)(2,1)S(1)}, bf16[256,256]{1,0:T(8,128)(2,1)S(1)}, u32[]{:S(2)}, u32[]{:S(2)}) %collective-permute-start.9) | collective-permute-done | bytes 131104 | tf_op jit(solution)/shard_map/ppermute | solution.py:434
  127.6 0.1 collective-permute-start.10
  127.7 3.9 %add8.1 = f32[2,2,256,2048]{3,2,1,0:T(8,128)} custom-call(f32[2,2,256,2048]{3,2,1,0:T(8,128)} %add0.1.held_ref, bf16[2,2,256,1024]{3,2,1,0:T(8,128)(2,1)S(1)} %collective-permute-done.4.came_ref), custom_call_target="tpu_custom_call", output_to_operand_aliasing={{}: (0, {})} | custom-call | tf_op jit(solution)/shard_map/add8/pallas_call | solution.py:416
  131.7 0.8 pad_maximum_fusion
  (27 shorter events, 0.3 us)
Async XLA Ops:
  4.2 9.9 %copy-start.7 = (f32[256]{0:T(256)S(1)}, f32[256]{0:T(256)}, u32[]{:S(2)}) copy-start(f32[256]{0:T(256)} %param.11) | copy-start | bytes 3076
  4.2 10.0 %copy-start.5 = (f32[256,256]{1,0:T(8,128)S(1)}, f32[256,256]{1,0:T(8,128)}, u32[]{:S(2)}) copy-start(f32[256,256]{1,0:T(8,128)} %constant.14.clone) | copy-start | bytes 786436
  4.2 10.0 %copy-start.6 = (f32[256,256]{1,0:T(8,128)S(1)}, f32[256,256]{1,0:T(8,128)}, u32[]{:S(2)}) copy-start(f32[256,256]{1,0:T(8,128)} %constant.15.clone) | copy-start | bytes 786436
  4.2 20.3 %collective-permute-start.1 = (bf16[2,2,256,640]{3,2,1,0:T(8,128)(2,1)}, bf16[2,2,256,640]{3,2,1,0:T(8,128)(2,1)}, u32[]{:S(2)}, u32[]{:S(2)}) collective-permute-start(bf16[2,2,256,640]{3,2,1,0:T(8,128)(2,1)} %get-tuple-element.32), channel_id=1, source_target_pairs={{1,0},{2,1},{3,2},{4,3},{5,4},{6,5},{7,6},{8,7},{9,8},{10,9},{11,1... | collective-permute-start | bytes 3932168 | tf_op jit(solution)/shard_map/ppermute | solution.py:20
  6.9 31.6 %collective-permute-start = (bf16[2,2,256,640]{3,2,1,0:T(8,128)(2,1)}, bf16[2,2,256,640]{3,2,1,0:T(8,128)(2,1)}, u32[]{:S(2)}, u32[]{:S(2)}) collective-permute-start(bf16[2,2,256,640]{3,2,1,0:T(8,128)(2,1)} %get-tuple-element.33), channel_id=1, source_target_pairs={{1,0},{2,1},{3,2},{4,3},{5,4},{6,5},{7,6},{8,7},{9,8},{10,9},{11,1... | collective-permute-start | bytes 3932168 | tf_op jit(solution)/shard_map/ppermute | solution.py:20
  11.6 43.7 %collective-permute-start.2 = (bf16[2,2,256,768]{3,2,1,0:T(8,128)(2,1)}, bf16[2,2,256,768]{3,2,1,0:T(8,128)(2,1)}, u32[]{:S(2)}, u32[]{:S(2)}) collective-permute-start(bf16[2,2,256,768]{3,2,1,0:T(8,128)(2,1)} %slice.19), channel_id=1, source_target_pairs={{1,0},{2,1},{3,2},{4,3},{5,4},{6,5},{7,6},{8,7},{9,8},{10,9},{11,1... | collective-permute-start | bytes 4718600 | tf_op jit(solution)/shard_map/ppermute | solution.py:20
  16.2 8.2 %copy-start = (f32[2,256,256]{2,1,0:T(8,128)S(1)}, f32[2,256,256]{2,1,0:T(8,128)}, u32[]{:S(2)}) copy-start(f32[2,256,256]{2,1,0:T(8,128)} %refs_7_.5) | copy-start | bytes 1572868
  16.2 8.2 %copy-start.1 = (bf16[512,512]{1,0:T(8,128)(2,1)S(1)}, bf16[512,512]{1,0:T(8,128)(2,1)}, u32[]{:S(2)}) copy-start(bf16[512,512]{1,0:T(8,128)(2,1)} %constant.26.refs_3_) | copy-start | bytes 1572868
  16.3 8.2 %copy-start.2 = (bf16[512,512]{1,0:T(8,128)(2,1)S(1)}, bf16[512,512]{1,0:T(8,128)(2,1)}, u32[]{:S(2)}) copy-start(bf16[512,512]{1,0:T(8,128)(2,1)} %constant.29.refs_4_) | copy-start | bytes 1572868
  16.3 8.2 %copy-start.3 = (s32[16]{0:T(128)S(1)}, s32[16]{0:T(128)}, u32[]{:S(2)}) copy-start(s32[16]{0:T(128)} %refs_0_.5) | copy-start | bytes 196
  16.3 8.2 %copy-start.4 = (s32[16]{0:T(128)S(1)}, s32[16]{0:T(128)}, u32[]{:S(2)}) copy-start(s32[16]{0:T(128)} %refs_1_.5) | copy-start | bytes 196
  55.3 36.6 %collective-permute-start.3 = (bf16[2,2,256,1024]{3,2,1,0:T(8,128)(2,1)}, bf16[2,2,256,1024]{3,2,1,0:T(8,128)(2,1)}, u32[]{:S(2)}, u32[]{:S(2)}) collective-permute-start(bf16[2,2,256,1024]{3,2,1,0:T(8,128)(2,1)} %get-tuple-element.27), channel_id=1, source_target_pairs={{0,1},{1,2},{2,3},{3,4},{4,5},{5,6},{6,7},{7,8},{8,9},{9,10},{10,1... | collective-permute-start | bytes 6291464 | tf_op jit(solution)/shard_map/ppermute | solution.py:20
  90.0 37.6 %collective-permute-start.4 = (bf16[2,2,256,1024]{3,2,1,0:T(8,128)(2,1)}, bf16[2,2,256,1024]{3,2,1,0:T(8,128)(2,1)S(1)}, u32[]{:S(2)}, u32[]{:S(2)}) collective-permute-start(bf16[2,2,256,1024]{3,2,1,0:T(8,128)(2,1)} %get-tuple-element.30), channel_id=1, source_target_pairs={{0,1},{1,2},{2,3},{3,4},{4,5},{5,6},{6,7},{7,8},{8,9},{9,10},{10,1... | collective-permute-start | bytes 6291464 | tf_op jit(solution)/shard_map/ppermute | solution.py:20
  96.9 1.6 %collective-permute-start.5 = (bf16[256,256]{1,0:T(8,128)(2,1)S(1)}, bf16[256,256]{1,0:T(8,128)(2,1)S(1)}, u32[]{:S(2)}, u32[]{:S(2)}) collective-permute-start(bf16[256,256]{1,0:T(8,128)(2,1)S(1)} %fusion.5), channel_id=1, source_target_pairs={{0,1},{1,0},{2,3},{3,2},{4,5},{5,4},{6,7},{7,6},{8,9},{9,8},{10,11... | collective-permute-start | bytes 393224 | tf_op jit(solution)/shard_map/ppermute | solution.py:434
  98.5 25.1 %collective-permute-start.6 = (bf16[256,256]{1,0:T(8,128)(2,1)S(1)}, bf16[256,256]{1,0:T(8,128)(2,1)S(1)}, u32[]{:S(2)}, u32[]{:S(2)}) collective-permute-start(bf16[256,256]{1,0:T(8,128)(2,1)S(1)} %fusion.1), channel_id=1, source_target_pairs={{0,4},{1,5},{2,6},{3,7},{4,0},{5,1},{6,2},{7,3},{8,12},{9,13},{10,... | collective-permute-start | bytes 393224 | tf_op jit(solution)/shard_map/ppermute | solution.py:434
  98.6 25.0 %collective-permute-start.7 = (bf16[256,256]{1,0:T(8,128)(2,1)S(1)}, bf16[256,256]{1,0:T(8,128)(2,1)S(1)}, u32[]{:S(2)}, u32[]{:S(2)}) collective-permute-start(bf16[256,256]{1,0:T(8,128)(2,1)S(1)} %fusion.1), channel_id=1, source_target_pairs={{0,8},{1,9},{2,10},{3,11},{4,12},{5,13},{6,14},{7,15},{8,0},{9,1},... | collective-permute-start | bytes 393224 | tf_op jit(solution)/shard_map/ppermute | solution.py:434
  98.6 24.9 %collective-permute-start.8 = (bf16[256,256]{1,0:T(8,128)(2,1)S(1)}, bf16[256,256]{1,0:T(8,128)(2,1)S(1)}, u32[]{:S(2)}, u32[]{:S(2)}) collective-permute-start(bf16[256,256]{1,0:T(8,128)(2,1)S(1)} %fusion.1), channel_id=1, source_target_pairs={{0,12},{1,13},{2,14},{3,15},{4,8},{5,9},{6,10},{7,11},{8,4},{9,5},... | collective-permute-start | bytes 393224 | tf_op jit(solution)/shard_map/ppermute | solution.py:434
  123.6 3.9 %collective-permute-start.9 = (bf16[256,256]{1,0:T(8,128)(2,1)S(1)}, bf16[256,256]{1,0:T(8,128)(2,1)S(1)}, u32[]{:S(2)}, u32[]{:S(2)}) collective-permute-start(bf16[256,256]{1,0:T(8,128)(2,1)S(1)} %add_convert_fusion), channel_id=1, source_target_pairs={{0,2},{1,3},{2,0},{3,1},{4,6},{5,7},{6,4},{7,5},{8,10},{9,11},{10,... | collective-permute-start | bytes 393224 | tf_op jit(solution)/shard_map/ppermute | solution.py:434
  127.6 4.0 %collective-permute-start.10 = (f32[256,256]{1,0:T(8,128)S(1)}, f32[256,256]{1,0:T(8,128)S(1)}, u32[]{:S(2)}, u32[]{:S(2)}) collective-permute-start(f32[256,256]{1,0:T(8,128)S(1)} %convert_add_fusion.1), channel_id=1, source_target_pairs={{0,1},{1,0},{2,3},{3,2},{4,5},{5,4},{6,7},{7,6},{8,9},{9,8},{10,11... | collective-permute-start | bytes 786440 | tf_op jit(solution)/shard_map/ppermute | solution.py:434
